TPU v7x, 32 devices: a whole 2x2x4 slice. The times are simulated.
32 devices in a mesh: view: 8 (over y, x, core), bulk: 4 (over z).
Axes of the slice: x: 2, y: 2, z: 4, core: 2. Of those that a mesh axis runs over, the one named last changes fastest.
Arguments:
- estimate: float32 [128, 32, 128], P('bulk'), may hold values from 0.5 to 2
- image: float32 [8, 128, 32, 128], P('view', 'bulk'), may hold values from 0.05 to 20, as said below
- psf: float32 [8, 3, 15], P('view'), may hold values from 0.05 to 1
- perm: int32 [8], P('view'), may hold values from 0 to 1
- shift: int32 [8], P('view'), may hold values from -8 to 7
- visible: int32 [8, 128], P('view', 'bulk'), may hold values 0 or 1
Outputs:
- updated: float32 [128, 32, 128], P('bulk')
Inputs may be any that keep to these rules, and one draw needn't show every extreme that they name: `image`: every entry is positive.
All inputs are finite; a program needn't handle non-finite values. No bound on the sum of `visible` on one device may be relied on, other than what follows from the above.
Results may differ from a plain program's by a relative error of at most 0.0003.
Values sent between devices are 32-bit elements; how exact they have to be, the bound alone decides.
No kernel may reach another device: no remote copies, remote signals or barrier semaphores. Data moves between devices by JAX's collectives and lax.ppermute only.
A program may use at most 128 MiB of HBM per device.

v0:
```python
import jax
import jax.numpy as jnp
from jax import lax
from jax.sharding import PartitionSpec as P


def extended(block, sides, width):
    for axis, dim in sides:
        count = lax.axis_size(axis)
        forward = [(i, i + 1) for i in range(count - 1)]
        backward = [(target, source) for source, target in forward]
        low = lax.ppermute(
            lax.slice_in_dim(block, block.shape[dim] - width, None, axis=dim), axis, forward
        )
        high = lax.ppermute(lax.slice_in_dim(block, 0, width, axis=dim), axis, backward)
        block = jnp.concatenate([low, block, high], axis=dim)
    return block


def blur_local(values, kernel, axis, cyclic):
    margin = kernel.shape[0] // 2
    widths = [(0, 0)] * values.ndim
    widths[axis] = (margin, margin)
    padded = jnp.pad(values, widths, mode="wrap" if cyclic else "constant")
    extent = values.shape[axis]
    summed = jnp.zeros(values.shape, jnp.float32)
    for offset in range(kernel.shape[0]):
        summed = summed + kernel[offset] * lax.slice_in_dim(
            padded, offset, offset + extent, axis=axis
        )
    return summed


def blur_bulk(values, kernel):
    margin = kernel.shape[0] // 2
    padded = extended(values, (("bulk", 0),), margin)
    extent = values.shape[0]
    summed = jnp.zeros(values.shape, jnp.float32)
    for offset in range(kernel.shape[0]):
        summed = summed + kernel[offset] * padded[offset : offset + extent]
    return summed


def forward(values, kernels):
    return blur_local(
        blur_local(blur_bulk(values, kernels[0]), kernels[1], 1, True), kernels[2], 2, False
    )


def adjoint(values, flipped):
    return blur_bulk(
        blur_local(blur_local(values, flipped[2], 2, False), flipped[1], 1, True), flipped[0]
    )


def shards(estimate, image, psf, perm, shift, visible):
    turned = perm[0]
    moved = shift[0]
    kernels = psf[0] / jnp.sum(psf[0], axis=1, keepdims=True)
    stack = image[0]
    weight = jnp.where(visible[0] == 1, 1.0, 0.0).astype(jnp.float32)[:, None, None]
    swapped = jnp.transpose(
        lax.all_to_all(estimate, "bulk", split_axis=2, concat_axis=0, tiled=True), (2, 1, 0)
    )
    viewed = jnp.roll(jnp.where(turned == 1, swapped, estimate), moved, axis=1)
    blurred = forward(viewed, kernels)
    correction = adjoint(stack / blurred, kernels[:, ::-1])
    unrolled = jnp.roll(correction, -moved, axis=1)
    returned = lax.all_to_all(
        jnp.transpose(unrolled, (2, 1, 0)), "bulk", split_axis=0, concat_axis=2, tiled=True
    )
    joined = jnp.where(turned == 1, returned, unrolled)
    log_terms = weight * jnp.log(joined)
    views_count = float(lax.axis_size("view"))
    log_total = lax.psum(log_terms, "view")
    return estimate * jnp.exp(log_total / views_count)


def solution(mesh):
    placed = (
        P("bulk", None, None),
        P("view", "bulk", None, None),
        P("view", None, None),
        P("view"),
        P("view"),
        P("view", "bulk"),
    )
    return jax.shard_map(
        shards, mesh=mesh, in_specs=placed, out_specs=P("bulk", None, None), check_vma=False
    )
```

profile of v0, /device:TPU:0, one launch (start us, length us, event | category | flops | bytes accessed | tf_op | source)
XLA Modules:
  0.0 213.7 jit_solution(10791936641872334056)
XLA Ops:
  6.5 2.9 %copy.102 = f32[32,32,128]{1,0,2:T(8,128)S(1)} copy(f32[32,32,128]{2,1,0:T(8,128)} %param.8) | data formatting | bytes 1048576 | tf_op args[0]
  11.1 6.3 %all-to-all-start = ((f32[4,1,32768]{2,1,0:T(1,128)}), f32[4,1,32768]{2,1,0:T(1,128)S(1)}, u32[]{:S(2)}, u32[]{:S(2)}) async-start(f32[4,1,32768]{2,1,0:T(1,128)} %reshape.194), calls=%async_computation | async-start | bytes 1048576 | tf_op jit(solution)/shard_map/all_to_all | solution.py:63
  19.6 12.2 %all-to-all-done = f32[4,1,32768]{2,1,0:T(1,128)S(1)} async-done(((f32[4,1,32768]{2,1,0:T(1,128)}), f32[4,1,32768]{2,1,0:T(1,128)S(1)}, u32[]{:S(2)}, u32[]{:S(2)}) %all-to-all-start) | async-done | bytes 524320 | tf_op jit(solution)/shard_map/all_to_all | solution.py:63
  32.3 2.0 reduce.1
  35.1 1.9 copy.103
  37.0 2.5 %all_to_all.29 = f32[128,32,32]{0,1,2:T(8,128)S(1)} reshape(f32[4,32,32,32]{1,0,2,3:T(4,128)} %bitcast.74) | data formatting | bytes 1048576 | tf_op jit(solution)/shard_map/all_to_all | solution.py:63
  44.1 3.8 %collective-permute-done.1 = f32[7,32,128]{2,1,0:T(8,128)S(1)} collective-permute-done((f32[7,32,128]{2,1,0:T(8,128)S(1)}, f32[7,32,128]{2,1,0:T(8,128)S(1)}, u32[]{:S(2)}, u32[]{:S(2)}) %collective-permute-start.1) | collective-permute-done | bytes 114720 | tf_op jit(solution)/shard_map/ppermute | solution.py:15
  47.9 9.7 %fusion.41 = f32[32,32,128]{2,1,0:T(8,128)S(1)} fusion(f32[32,32,128]{2,1,0:T(8,128)S(1)} %fusion.153, f32[7,32,128]{2,1,0:T(8,128)S(1)} %collective-permute-done.1, f32[7,32,128]{2,1,0:T(8,128)S(1)} %collective-permute-done, f32[]{:T(128)} %bitcast.25, f32[]{:T(128)} %bitcast.24, f32[]{:T(128)} %bitcast.23, f32[]{:T(128)} %bitcast.22, f32[]{:T(128)} %bitcast.21, ...), kind=kLoop, calls=%fused_computation.169 | loop fusion | flops 5636096 | bytes 1278012 | tf_op jit(solution)/shard_map/add | solution.py:40
  57.6 10.6 %fusion.117 = f32[32,32,128]{2,1,0:T(8,128)S(1)} fusion(f32[32,32,128]{2,1,0:T(8,128)S(1)} %fusion.41, f32[32,7,128]{2,1,0:T(8,128)S(1)} %get-tuple-element.11, f32[32,7,128]{2,1,0:T(8,128)S(1)} %get-tuple-element.10, f32[]{:T(128)} %bitcast.38, f32[]{:T(128)} %bitcast.37, f32[]{:T(128)} %bitcast.36, f32[]{:T(128)} %bitcast.35, f32[]{:T(128)} %bitcast.34, ...), kind=kLoop, calls=%fused_computation.245 | loop fusion | flops 5636096 | bytes 1278012 | tf_op jit(solution)/shard_map/add | solution.py:28
  68.2 11.4 %fusion.169 = f32[32,32,128]{2,1,0:T(8,128)S(1)} fusion(f32[32,32,128]{2,1,0:T(8,128)S(1)} %fusion.117, f32[1,32,32,128]{3,2,1,0:T(8,128)S(1)} %copy-done.1, f32[]{:T(128)} %bitcast.51, f32[]{:T(128)} %bitcast.50, f32[]{:T(128)} %bitcast.49, f32[]{:T(128)} %bitcast.48, f32[]{:T(128)} %bitcast.47, f32[]{:T(128)} %bitcast.46, f32[]{:T(128)} %bitcast.45, ...), kind=kLoop, calls=%fused_computation.297 | loop fusion | flops 3932160 | bytes 1572924 | tf_op jit(solution)/shard_map/div | solution.py:67
  79.7 11.4 %fusion.197 = f32[32,32,128]{2,1,0:T(8,128)S(1)} fusion(f32[32,32,128]{2,1,0:T(8,128)S(1)} %fusion.169, f32[]{:T(128)} %bitcast.51, f32[]{:T(128)} %bitcast.50, f32[]{:T(128)} %bitcast.49, f32[]{:T(128)} %bitcast.48, f32[]{:T(128)} %bitcast.47, f32[]{:T(128)} %bitcast.46, f32[]{:T(128)} %bitcast.45, f32[]{:T(128)} %bitcast.44, f32[]{:T(128)} %bitcast.43, ...), kind=kLoop, calls=%fused_computation.325 | loop fusion | flops 3801088 | bytes 1048636 | tf_op jit(solution)/shard_map/add | solution.py:28
  91.1 10.6 %fusion.79 = f32[32,32,128]{2,1,0:T(8,128)S(1)} fusion(f32[32,32,128]{2,1,0:T(8,128)S(1)} %fusion.197, f32[32,7,128]{2,1,0:T(8,128)S(1)} %get-tuple-element.9, f32[32,7,128]{2,1,0:T(8,128)S(1)} %get-tuple-element.8, f32[]{:T(128)} %bitcast.38, f32[]{:T(128)} %bitcast.37, f32[]{:T(128)} %bitcast.36, f32[]{:T(128)} %bitcast.35, f32[]{:T(128)} %bitcast.34, ...), kind=kLoop, calls=%fused_computation.207 | loop fusion | flops 5636096 | bytes 1278012 | tf_op jit(solution)/shard_map/add | solution.py:28
  101.7 3.1 %collective-permute-start.2 = (f32[7,32,128]{2,1,0:T(8,128)S(1)}, f32[7,32,128]{2,1,0:T(8,128)S(1)}, u32[]{:S(2)}, u32[]{:S(2)}) collective-permute-start(f32[7,32,128]{2,1,0:T(8,128)S(1)} %get-tuple-element.6), channel_id=1, source_target_pairs={{0,1},{1,2},{2,3},{4,5},{5,6},{6,7},{8,9},{9,10},{10,11},{12,13},{... | collective-permute-start | bytes 344072 | tf_op jit(solution)/shard_map/ppermute | solution.py:12
  107.2 4.3 %collective-permute-done.3 = f32[7,32,128]{2,1,0:T(8,128)S(1)} collective-permute-done((f32[7,32,128]{2,1,0:T(8,128)S(1)}, f32[7,32,128]{2,1,0:T(8,128)S(1)}, u32[]{:S(2)}, u32[]{:S(2)}) %collective-permute-start.3) | collective-permute-done | bytes 114720 | tf_op jit(solution)/shard_map/ppermute | solution.py:15
  111.5 9.7 %fusion.3 = f32[32,32,128]{2,1,0:T(8,128)S(1)} fusion(f32[32,32,128]{2,1,0:T(8,128)S(1)} %fusion.79, f32[7,32,128]{2,1,0:T(8,128)S(1)} %collective-permute-done.3, f32[7,32,128]{2,1,0:T(8,128)S(1)} %collective-permute-done.2, f32[]{:T(128)} %bitcast.25, f32[]{:T(128)} %bitcast.24, f32[]{:T(128)} %bitcast.23, f32[]{:T(128)} %bitcast.22, f32[]{:T(128)} %bitcast.21, ...), kind=kLoop, calls=%fused_computation.131 | loop fusion | flops 5636096 | bytes 1278012 | tf_op jit(solution)/shard_map/add | solution.py:40
  122.2 2.9 %copy.104 = f32[128,32,32]{1,2,0:T(8,128)S(1)} copy(f32[128,32,32]{0,1,2:T(8,128)} %fusion.219) | data formatting | bytes 1048576 | tf_op jit(solution)/shard_map/transpose | solution.py:70
  126.7 3.5 %all-to-all-start.1 = ((f32[4,1,32768]{2,1,0:T(1,128)}), f32[4,1,32768]{2,1,0:T(1,128)S(1)}, u32[]{:S(2)}, u32[]{:S(2)}) async-start(f32[4,1,32768]{2,1,0:T(1,128)} %reshape.196), calls=%async_computation.1 | async-start | bytes 1048576 | tf_op jit(solution)/shard_map/all_to_all | solution.py:69
  130.5 10.5 %all-to-all-done.1 = f32[4,1,32768]{2,1,0:T(1,128)S(1)} async-done(((f32[4,1,32768]{2,1,0:T(1,128)}), f32[4,1,32768]{2,1,0:T(1,128)S(1)}, u32[]{:S(2)}, u32[]{:S(2)}) %all-to-all-start.1) | async-done | bytes 524320 | tf_op jit(solution)/shard_map/all_to_all | solution.py:69
  140.9 2.8 %reduce.2 = f32[4,32768]{1,0:T(4,128)} reduce(f32[4,1,32768]{2,1,0:T(1,128)S(1)} %all-to-all-done.1, f32[]{:T(128)} %broadcast.25), dimensions={1}, to_apply=%all_to_all.30.reduce_sub_computation | reduce | bytes 1048580 | tf_op jit(solution)/shard_map/all_to_all | solution.py:69
  143.8 1.8 reshape.197
  145.5 1.9 copy.105
  147.4 2.4 %all_to_all.33 = f32[32,32,128]{2,1,0:T(8,128)S(1)} reshape(f32[32,32,4,32]{3,2,1,0:T(4,128)} %bitcast.76) | data formatting | bytes 1048576 | tf_op jit(solution)/shard_map/all_to_all | solution.py:69
  150.9 54.0 %all-reduce.4.cloned.1.call-done = f32[32,32,128]{2,1,0:T(8,128)} async-done(((f32[32,32,128]{2,1,0:T(8,128)}), f32[32,32,128]{2,1,0:T(8,128)}) %all-reduce.4.cloned.1.call-update) | async-done | bytes 524304 | tf_op jit(solution)/shard_map/psum | solution.py:75
  204.9 1.9 exponential_multiply_fusion
  (33 shorter events, 14.6 us)
Async XLA Ops:
  9.4 9.3 %copy-start.2 = (f32[1,3,15]{2,0,1:T(1,128)S(1)}, f32[1,3,15]{2,0,1:T(1,128)}, u32[]{:S(2)}) copy-start(f32[1,3,15]{2,0,1:T(1,128)} %param.10) | copy-start | bytes 544
  11.1 20.8 %all-to-all-start = ((f32[4,1,32768]{2,1,0:T(1,128)}), f32[4,1,32768]{2,1,0:T(1,128)S(1)}, u32[]{:S(2)}, u32[]{:S(2)}) async-start(f32[4,1,32768]{2,1,0:T(1,128)} %reshape.194), calls=%async_computation | async-start | bytes 1048576 | tf_op jit(solution)/shard_map/all_to_all | solution.py:63
  37.0 2.5 %copy-start = (f32[32,32,128]{2,1,0:T(8,128)S(1)}, f32[32,32,128]{2,1,0:T(8,128)}, u32[]{:S(2)}) copy-start(f32[32,32,128]{2,1,0:T(8,128)} %param.8) | copy-start | bytes 1572868
  39.7 28.5 %copy-start.1 = (f32[1,32,32,128]{3,2,1,0:T(8,128)S(1)}, f32[1,32,32,128]{3,2,1,0:T(8,128)}, u32[]{:S(2)}) copy-start(f32[1,32,32,128]{3,2,1,0:T(8,128)} %param.9) | copy-start | bytes 1572868
  39.8 4.3 %collective-permute-start = (f32[7,32,128]{2,1,0:T(8,128)S(1)}, f32[7,32,128]{2,1,0:T(8,128)S(1)}, u32[]{:S(2)}, u32[]{:S(2)}) collective-permute-start(f32[7,32,128]{2,1,0:T(8,128)S(1)} %get-tuple-element.12), channel_id=1, source_target_pairs={{0,1},{1,2},{2,3},{4,5},{5,6},{6,7},{8,9},{9,10},{10,11},{12,13},{... | collective-permute-start | bytes 344072 | tf_op jit(solution)/shard_map/ppermute | solution.py:12
  41.2 6.7 %collective-permute-start.1 = (f32[7,32,128]{2,1,0:T(8,128)S(1)}, f32[7,32,128]{2,1,0:T(8,128)S(1)}, u32[]{:S(2)}, u32[]{:S(2)}) collective-permute-start(f32[7,32,128]{2,1,0:T(8,128)S(1)} %get-tuple-element.13), channel_id=1, source_target_pairs={{1,0},{2,1},{3,2},{5,4},{6,5},{7,6},{9,8},{10,9},{11,10},{13,12},{... | collective-permute-start | bytes 344072 | tf_op jit(solution)/shard_map/ppermute | solution.py:15
  101.7 5.4 %collective-permute-start.2 = (f32[7,32,128]{2,1,0:T(8,128)S(1)}, f32[7,32,128]{2,1,0:T(8,128)S(1)}, u32[]{:S(2)}, u32[]{:S(2)}) collective-permute-start(f32[7,32,128]{2,1,0:T(8,128)S(1)} %get-tuple-element.6), channel_id=1, source_target_pairs={{0,1},{1,2},{2,3},{4,5},{5,6},{6,7},{8,9},{9,10},{10,11},{12,13},{... | collective-permute-start | bytes 344072 | tf_op jit(solution)/shard_map/ppermute | solution.py:12
  104.8 6.7 %collective-permute-start.3 = (f32[7,32,128]{2,1,0:T(8,128)S(1)}, f32[7,32,128]{2,1,0:T(8,128)S(1)}, u32[]{:S(2)}, u32[]{:S(2)}) collective-permute-start(f32[7,32,128]{2,1,0:T(8,128)S(1)} %get-tuple-element.7), channel_id=1, source_target_pairs={{1,0},{2,1},{3,2},{5,4},{6,5},{7,6},{9,8},{10,9},{11,10},{13,12},{... | collective-permute-start | bytes 344072 | tf_op jit(solution)/shard_map/ppermute | solution.py:15
  125.1 5.4 %copy-start.3 = (s32[1,32]{1,0:T(1,128)S(1)}, s32[1,32]{1,0:T(1,128)}, u32[]{:S(2)}) copy-start(s32[1,32]{1,0:T(1,128)} %param.13) | copy-start | bytes 388
  126.7 14.2 %all-to-all-start.1 = ((f32[4,1,32768]{2,1,0:T(1,128)}), f32[4,1,32768]{2,1,0:T(1,128)S(1)}, u32[]{:S(2)}, u32[]{:S(2)}) async-start(f32[4,1,32768]{2,1,0:T(1,128)} %reshape.196), calls=%async_computation.1 | async-start | bytes 1048576 | tf_op jit(solution)/shard_map/all_to_all | solution.py:69
  130.2 74.7 %all-reduce.4.cloned.1.call-start = ((), (), s32[]{:S(2)}) async-start(), calls=%async_computation.2 | async-start | bytes 1048576 | tf_op jit(solution)/shard_map/psum | solution.py:75
Sparse Core Ops, SparseCore 0:
  151.0 53.8 all-reduce.3
where the time goes:
time: 215 us; the launch traced here: 214 us
  waiting for transfers between devices  85.9 us (40%)
  other arithmetic  72.6 us (34%)
  local copies, waits for them, and re-layouts  22.8 us (11%)
  starting transfers between devices  17.3 us (8%)
  between operations  15 us (7%)
    psum x1, waiting for transfers between devices, shards(): log_total = lax.psum(log_terms, 'view')  54 us
    add x3, other arithmetic, blur_local(): summed + kernel[offset] * lax.slice_in_dim(padded, offset, offset + exten...  32.6 us
    add x2, other arithmetic, blur_bulk(): summed = summed + kernel[offset] * padded[offset:offset + extent]  19.4 us
    all_to_all x1, waiting for transfers between devices, shards(): lax.all_to_all(estimate, 'bulk', split_axis=2, concat_axis=0, tiled=True)  12.2 us
    div x1, other arithmetic, shards(): correction = adjoint(stack / blurred, kernels[:, ::-1])  11.4 us
    all_to_all x1, waiting for transfers between devices, shards(): lax.all_to_all(jnp.transpose(unrolled, (2, 1, 0)), 'bulk', split_axis=0,...  10.5 us
    unnamed x13, local copies, waits for them, and re-layouts  8.64 us
    ppermute x2, waiting for transfers between devices, extended(): lax.ppermute(lax.slice_in_dim(block, 0, width, axis=dim), axis, backward)  8.14 us
  transfers between devices with their start and end apart: 7, of which 6 were waited for; matrix products, arithmetic and copies ran while one was open for 1% of the time, Pallas kernels for 0%

commit v1 on v0

v1 whole, which is shorter than its diff:
```python
import functools

import jax
import jax.numpy as jnp
from jax import lax
from jax.experimental import pallas as pl
from jax.experimental.pallas import tpu as pltpu
from jax.sharding import PartitionSpec as P

LANES = 128
ROWS = 8
WIDE = 256
VMEM = pl.BlockSpec(memory_space=pltpu.VMEM)
SMEM = pl.BlockSpec(memory_space=pltpu.SMEM)
PARAMS = pltpu.CompilerParams(vmem_limit_bytes=40 * 1024 * 1024)


def struct(shape, dtype=jnp.float32):
    return jax.ShapeDtypeStruct(shape, dtype)


def halves(values):
    high = values.astype(jnp.bfloat16)
    low = (values - high.astype(jnp.float32)).astype(jnp.bfloat16)
    return high, low


def dot(left, right):
    return jnp.dot(left, right, preferred_element_type=jnp.float32)


def blur_rows(left_high, left_low, values):
    width = values.shape[1]
    high, low = halves(values)
    both = dot(left_high, jnp.concatenate([high, low], axis=1))
    return both[:, :width] + both[:, width:] + dot(left_low, high)


def blur_lanes(right, values):
    width = values.shape[1]
    out = dot(jnp.concatenate(halves(values), axis=1), right)
    return out[:, :width] + out[:, width:]


def lanes_matrix(taps_ref, row, extent, adjoint):
    taps = taps_ref.shape[1]
    source = lax.broadcasted_iota(jnp.int32, (extent, extent), 0)
    target = lax.broadcasted_iota(jnp.int32, (extent, extent), 1)
    offset = (target - source if adjoint else source - target) + taps // 2
    matrix = jnp.zeros((extent, extent), jnp.float32)
    for t in range(taps):
        matrix = jnp.where(offset == t, taps_ref[row, t], matrix)
    high, low = halves(matrix)
    pair = jnp.concatenate([high, low], axis=1)
    return jnp.concatenate([pair, pair], axis=0)


def rows_matrix(taps_ref, row, period, moved, adjoint):
    taps = taps_ref.shape[1]
    target = lax.broadcasted_iota(jnp.int32, (WIDE, WIDE), 0)
    source = lax.broadcasted_iota(jnp.int32, (WIDE, WIDE), 1)
    same = (target // period) == (source // period)
    ahead = target - source if adjoint else source - target
    offset = jnp.bitwise_and(ahead + taps // 2 + moved, period - 1)
    offset = jnp.where(same, offset, taps)
    matrix = jnp.zeros((WIDE, WIDE), jnp.float32)
    for t in range(taps):
        matrix = jnp.where(offset == t, taps_ref[row, t], matrix)
    return halves(matrix)


def pack_kernel(zb, ny, nx, count, perm_ref, image_ref, *refs):
    sends, (turned_ref, tile_ref) = refs[:count], refs[count:]
    reach = 7
    b = lax.axis_index("bulk")
    groups = ny // ROWS

    @pl.when(perm_ref[0] == 1)
    def _():
        edge = jnp.zeros((reach * ROWS, LANES), jnp.float32)
        turned_ref[: reach * ROWS] = edge
        turned_ref[(reach + nx) * ROWS :] = edge
        for tile in range(nx // LANES):
            if nx > LANES:
                tile_ref[...] = image_ref[:, tile * LANES : (tile + 1) * LANES]
                source = tile_ref
            else:
                source = image_ref
            for low in range(ROWS):
                pieces = [
                    source[pl.ds(ROWS * group + low, zb, stride=ny), :]
                    for group in range(groups)
                ]
                block = jnp.concatenate(pieces, axis=0).T
                turned_ref[
                    pl.ds((tile * LANES + reach) * ROWS + low, LANES, stride=ROWS), :
                ] = block
        extent = (zb + 2 * reach) * ROWS
        for d in range(count):
            start = lax.rem(b + d, count) * (zb * ROWS)
            sends[d][:extent] = turned_ref[pl.ds(pl.multiple_of(start, ROWS), extent), :]

    @pl.when(perm_ref[0] != 1)
    def _():
        extent = reach * ny
        for tile in range(nx // LANES):
            lanes = slice(tile * LANES, (tile + 1) * LANES)
            place = slice(tile * extent, (tile + 1) * extent)
            sends[1][place] = image_ref[(zb - reach) * ny :, lanes]
            sends[count - 1][place] = image_ref[:extent, lanes]


def forward_kernel(zb, ny, nx, planes, scalar_ref, taps_ref, estimate_ref, low_ref, high_ref,
                   other_ref, inverse_ref, rows_high_ref, rows_low_ref, lanes_ref, wide_ref):
    taps = taps_ref.shape[1]
    reach = taps // 2
    moved, core = scalar_ref[0], scalar_ref[1]
    wide_ref[pl.ds(reach * core, reach)] = low_ref[...]
    wide_ref[pl.ds(reach * (1 - core), reach)] = other_ref[0]
    wide_ref[2 * reach : 2 * reach + zb] = estimate_ref[...]
    wide_ref[pl.ds(2 * reach + zb + reach * core, reach)] = high_ref[...]
    wide_ref[pl.ds(2 * reach + zb + reach * (1 - core), reach)] = other_ref[1]
    rest = planes - zb - 2 * reach
    wide_ref[4 * reach + zb :] = jnp.zeros((rest, ny, nx), jnp.float32)

    rows_high, rows_low = rows_matrix(taps_ref, 1, ny, moved, False)
    lanes = lanes_matrix(taps_ref, 2, nx, False)
    group = WIDE // ny

    def step(index, carry):
        base = index * group
        blurred = []
        for plane in range(group):
            total = taps_ref[0, 0] * wide_ref[base + plane]
            for t in range(1, taps):
                total = total + taps_ref[0, t] * wide_ref[base + plane + t]
            blurred.append(total)
        values = jnp.concatenate(blurred, axis=0)
        values = blur_lanes(lanes, blur_rows(rows_high, rows_low, values))
        inverse_ref[pl.ds(base, group)] = (1.0 / values).reshape(group, ny, nx)
        return carry

    lax.fori_loop(0, planes // group, step, 0)
    high, low = rows_matrix(taps_ref, 1, ny, moved, True)
    rows_high_ref[...] = high
    rows_low_ref[...] = low
    lanes_ref[...] = lanes_matrix(taps_ref, 2, nx, True)


def adjoint_kernel(zb, ny, nx, count, scalar_ref, taps_ref, visible_ref, image_ref, inverse_ref,
                   rows_high_ref, rows_low_ref, lanes_ref, *refs):
    blocks, (send_ref, keep_ref, ratio_ref, placed_ref) = refs[:count], refs[count:]
    taps = taps_ref.shape[1]
    reach = taps // 2
    core, turned = scalar_ref[1], scalar_ref[2]
    b = lax.axis_index("bulk")
    groups = ny // ROWS
    planes = zb + 2 * reach

    @pl.when(turned == 1)
    def _():
        for d in range(count):
            placed_ref[lax.rem(b + count - d, count)] = blocks[d][: planes * ROWS]
        chunk = 8
        for tile in range(nx // LANES):
            lanes = slice(tile * LANES, (tile + 1) * LANES)
            for first in range(0, planes, chunk):
                size = min(chunk, planes - first)
                spot = lax.broadcasted_iota(jnp.int32, (size * ROWS, LANES), 1) // zb
                parts = [
                    placed_ref[groups * tile + c, first * ROWS : (first + size) * ROWS]
                    for c in range(groups)
                ]
                for g in range(groups):
                    value = None
                    for c in range(groups):
                        shift = (zb * (c - g)) % LANES
                        moved = pltpu.roll(parts[c], shift, 1) if shift else parts[c]
                        value = moved if value is None else jnp.where(spot == c, moved, value)
                    ratio_ref[first : first + size, g * ROWS : (g + 1) * ROWS, lanes] = (
                        value.reshape(size, ROWS, LANES)
                        * inverse_ref[first : first + size, g * ROWS : (g + 1) * ROWS, lanes]
                    )

    @pl.when(turned != 1)
    def _():
        extent = reach * ny
        ratio_ref[reach : reach + zb] = (
            image_ref[...].reshape(zb, ny, nx) * inverse_ref[reach : reach + zb]
        )
        for tile in range(nx // LANES):
            lanes = slice(tile * LANES, (tile + 1) * LANES)
            place = slice(tile * extent, (tile + 1) * extent)
            before = blocks[1][place].reshape(reach, ny, LANES)
            after = blocks[count - 1][place].reshape(reach, ny, LANES)
            before = jnp.where(b > 0, before * inverse_ref[:reach, :, lanes], 0.0)
            after = jnp.where(
                b < count - 1, after * inverse_ref[reach + zb : planes, :, lanes], 0.0
            )
            ratio_ref[:reach, :, lanes] = before
            ratio_ref[reach + zb :, :, lanes] = after

    rows_high, rows_low, lanes_pair = rows_high_ref[...], rows_low_ref[...], lanes_ref[...]
    group = WIDE // ny
    half = zb // 2
    for out_ref, side in ((send_ref, 1 - core), (keep_ref, core)):
        for first in range(0, half, group):
            base = side * half + first
            blurred = []
            for plane in range(group):
                total = taps_ref[0, taps - 1] * ratio_ref[base + plane]
                for t in range(1, taps):
                    total = total + taps_ref[0, taps - 1 - t] * ratio_ref[base + plane + t]
                blurred.append(total)
            values = jnp.concatenate(blurred, axis=0)
            values = blur_lanes(lanes_pair, blur_rows(rows_high, rows_low, values))
            logs = jnp.log(values).reshape(group, ny, nx)
            for plane in range(group):
                weight = jnp.where(visible_ref[base + plane] == 1, 1.0, 0.0)
                out_ref[first + plane] = weight * logs[plane]


def shards(estimate, image, psf, perm, shift, visible):
    zb, ny, nx = estimate.shape
    views, count = lax.axis_size("view"), lax.axis_size("bulk")
    view = lax.axis_index("view")
    core, chip = view % 2, view // 2
    taps = psf.shape[2]
    reach = taps // 2
    kernels = psf[0] / jnp.sum(psf[0], axis=1, keepdims=True)
    joined_taps = jnp.where(perm[0] == 1, kernels[::-1], kernels)
    scalars = jnp.stack([shift[0], core.astype(jnp.int32), perm[0]])
    stack = image[0].reshape(zb * ny, nx)

    extent = max((zb + 2 * reach) * ROWS, reach * ny * (nx // LANES))
    packed = pl.pallas_call(
        functools.partial(pack_kernel, zb, ny, nx, count),
        out_shape=[struct((extent, LANES))] * count,
        in_specs=[SMEM, VMEM],
        out_specs=[VMEM] * count,
        scratch_shapes=[
            pltpu.VMEM(((nx + 2 * reach) * ROWS, LANES), jnp.float32),
            pltpu.VMEM((zb * ny, LANES), jnp.float32),
        ],
        compiler_params=PARAMS,
    )(perm, stack)
    blocks = [packed[0]] + [
        lax.ppermute(packed[d], "bulk", [(i, (i + d) % count) for i in range(count)])
        for d in range(1, count)
    ]

    swap = [(i, i ^ 1) for i in range(views)]
    forward = [(i, i + 1) for i in range(count - 1)]
    backward = [(i + 1, i) for i in range(count - 1)]
    low = lax.ppermute(
        lax.dynamic_slice_in_dim(estimate, zb - 2 * reach + reach * core, reach, 0),
        "bulk", forward,
    )
    high = lax.ppermute(
        lax.dynamic_slice_in_dim(estimate, reach * core, reach, 0), "bulk", backward
    )
    other = lax.ppermute(jnp.stack([low, high]), "view", swap)

    group = WIDE // ny
    planes = -(-(zb + 2 * reach) // group) * group
    inverse, rows_high, rows_low, lanes_pair = pl.pallas_call(
        functools.partial(forward_kernel, zb, ny, nx, planes),
        out_shape=[
            struct((planes, ny, nx)),
            struct((WIDE, WIDE), jnp.bfloat16),
            struct((WIDE, WIDE), jnp.bfloat16),
            struct((2 * nx, 2 * nx), jnp.bfloat16),
        ],
        in_specs=[SMEM, SMEM] + [VMEM] * 4,
        out_specs=[VMEM] * 4,
        scratch_shapes=[pltpu.VMEM((planes + 2 * reach, ny, nx), jnp.float32)],
        compiler_params=PARAMS,
    )(scalars, joined_taps, estimate, low, high, other)

    half = zb // 2
    send, keep = pl.pallas_call(
        functools.partial(adjoint_kernel, zb, ny, nx, count),
        out_shape=[struct((half, ny, nx))] * 2,
        in_specs=[SMEM] * 3 + [VMEM] * (5 + count),
        out_specs=[VMEM] * 2,
        scratch_shapes=[
            pltpu.VMEM((zb + 2 * reach, ny, nx), jnp.float32),
            pltpu.VMEM((count, (zb + 2 * reach) * ROWS, LANES), jnp.float32),
        ],
        compiler_params=PARAMS,
    )(scalars, joined_taps, visible[0], stack, inverse, rows_high, rows_low, lanes_pair, *blocks)

    chips = views // 2
    piece = half // chips
    summed = keep + lax.ppermute(send, "view", swap)
    total = lax.dynamic_slice_in_dim(summed, chip * piece, piece, 0)
    partners = [[(i, i ^ (2 * d)) for i in range(views)] for d in range(1, chips)]
    arrived = [
        lax.ppermute(
            lax.dynamic_slice_in_dim(summed, (chip ^ (d + 1)) * piece, piece, 0), "view", pairs
        )
        for d, pairs in enumerate(partners)
    ]
    for part in arrived:
        total = total + part
    mine = lax.dynamic_slice_in_dim(estimate, core * half + chip * piece, piece, 0)
    mine = mine * jnp.exp(total / float(views))
    own = jnp.zeros((half, ny, nx), jnp.float32)
    own = lax.dynamic_update_slice_in_dim(own, mine, chip * piece, 0)
    for d, pairs in enumerate(partners):
        part = lax.ppermute(mine, "view", pairs)
        own = lax.dynamic_update_slice_in_dim(own, part, (chip ^ (d + 1)) * piece, 0)
    their = lax.ppermute(own, "view", swap)
    return jnp.concatenate(
        [jnp.where(core == 0, own, their), jnp.where(core == 0, their, own)], axis=0
    )


def solution(mesh):
    placed = (
        P("bulk", None, None),
        P("view", "bulk", None, None),
        P("view", None, None),
        P("view"),
        P("view"),
        P("view", "bulk"),
    )
    return jax.shard_map(
        shards, mesh=mesh, in_specs=placed, out_specs=P("bulk", None, None), check_vma=False
    )
```

time: 215 us -> 50.6 us (0.24)
  the two profiles are of different devices: /device:TPU:0 before, /device:TPU:9 now
where the time goes in v1:
time: 50.6 us; the launch traced here: 50.3 us
  starting transfers between devices  21.1 us (42%)
  waiting for transfers between devices  16.1 us (32%)
  Pallas kernels  7.65 us (15%)
  local copies, waits for them, and re-layouts  2.77 us (5%)
  between operations  1.44 us (3%)
  other arithmetic  1.29 us (3%)
    ppermute x3, waiting for transfers between devices, shards(): lax.ppermute(packed[d], 'bulk', [(i, (i + d) % count) for i in range(coun...  6.85 us
    pallas_call x1, Pallas kernels, shards(): pl.pallas_call(functools.partial(forward_kernel, zb, ny, nx, planes), out...  4.68 us
    ppermute x3, starting transfers between devices, shards(): lax.ppermute(packed[d], 'bulk', [(i, (i + d) % count) for i in range(coun...  3.83 us
    ppermute x1, starting transfers between devices, shards(): their = lax.ppermute(own, 'view', swap)  3.53 us
    ppermute x3, waiting for transfers between devices, shards(): lax.ppermute(lax.dynamic_slice_in_dim(summed, (chip ^ d + 1) * piece, pie...  3.37 us
    ppermute x1, starting transfers between devices, shards(): lax.ppermute(lax.dynamic_slice_in_dim(estimate, zb - 2 * reach + reach *...  3.2 us
    ppermute x3, starting transfers between devices, shards(): lax.ppermute(lax.dynamic_slice_in_dim(summed, (chip ^ d + 1) * piece, pie...  2.71 us
    ppermute x3, starting transfers between devices, shards(): part = lax.ppermute(mine, 'view', pairs)  2.71 us
  transfers between devices with their start and end apart: 14, of which 11 were waited for; matrix products, arithmetic and copies ran while one was open for 1% of the time, Pallas kernels for 10%

profile of v1, /device:TPU:9, one launch (start us, length us, event | category | flops | bytes accessed | tf_op | source)
XLA Modules:
  0.0 50.3 jit_solution(9378829232678218718)
XLA Ops:
  0.0 1.0 %constant_dynamic-slice_fusion.3 = (f32[7,32,128]{2,1,0:T(8,128)S(1)}, f32[7,32,128]{2,1,0:T(8,128)S(1)}) fusion(f32[32,32,128]{2,1,0:T(8,128)} %estimate_ref.1, s32[]{:T(128)S(6)} %select_n.63, s32[]{:T(128)S(6)} %select_n.62), kind=kLoop, calls=%fused_computation.12 | loop fusion | bytes 458760 | tf_op jit(solution)/shard_map/dynamic_slice | solution.py:260
  1.0 3.2 %collective-permute-start = (f32[7,32,128]{2,1,0:T(8,128)S(1)}, f32[7,32,128]{2,1,0:T(8,128)S(1)}, u32[]{:S(2)}, u32[]{:S(2)}) collective-permute-start(f32[7,32,128]{2,1,0:T(8,128)S(1)} %get-tuple-element.30), channel_id=1, source_target_pairs={{0,1},{1,2},{2,3},{4,5},{5,6},{6,7},{8,9},{9,10},{10,11},{12,13},{... | collective-permute-start | bytes 344072 | tf_op jit(solution)/shard_map/ppermute | solution.py:255
  4.2 2.1 %collective-permute-start.1 = (f32[7,32,128]{2,1,0:T(8,128)S(1)}, f32[7,32,128]{2,1,0:T(8,128)S(1)}, u32[]{:S(2)}, u32[]{:S(2)}) collective-permute-start(f32[7,32,128]{2,1,0:T(8,128)S(1)} %get-tuple-element.29), channel_id=1, source_target_pairs={{1,0},{2,1},{3,2},{5,4},{6,5},{7,6},{9,8},{10,9},{11,10},{13,12},{... | collective-permute-start | bytes 344072 | tf_op jit(solution)/shard_map/ppermute | solution.py:259
  6.9 1.0 %copy-done = f32[1,32,32,128]{3,2,1,0:T(8,128)S(1)} copy-done((f32[1,32,32,128]{3,2,1,0:T(8,128)S(1)}, f32[1,32,32,128]{3,2,1,0:T(8,128)}, u32[]{:S(2)}) %copy-start) | copy-done | bytes 524312
  8.4 1.3 %collective-permute-start.3 = (f32[368,128]{1,0:T(8,128)S(1)}, f32[368,128]{1,0:T(8,128)S(1)}, u32[]{:S(2)}, u32[]{:S(2)}) collective-permute-start(f32[368,128]{1,0:T(8,128)S(1)} %get-tuple-element.20), channel_id=1, source_target_pairs={{0,1},{1,2},{2,3},{3,0},{4,5},{5,6},{6,7},{7,4},{8,9},{9,10},{10,1... | collective-permute-start | bytes 565256 | tf_op jit(solution)/shard_map/ppermute | solution.py:248
  9.8 1.1 %collective-permute-start.4 = (f32[368,128]{1,0:T(8,128)S(1)}, f32[368,128]{1,0:T(8,128)S(1)}, u32[]{:S(2)}, u32[]{:S(2)}) collective-permute-start(f32[368,128]{1,0:T(8,128)S(1)} %get-tuple-element.21), channel_id=1, source_target_pairs={{0,2},{1,3},{2,0},{3,1},{4,6},{5,7},{6,4},{7,5},{8,10},{9,11},{10,... | collective-permute-start | bytes 565256 | tf_op jit(solution)/shard_map/ppermute | solution.py:248
  10.9 1.4 %collective-permute-start.5 = (f32[368,128]{1,0:T(8,128)S(1)}, f32[368,128]{1,0:T(8,128)S(1)}, u32[]{:S(2)}, u32[]{:S(2)}) collective-permute-start(f32[368,128]{1,0:T(8,128)S(1)} %get-tuple-element.22), channel_id=1, source_target_pairs={{0,3},{1,0},{2,1},{3,2},{4,7},{5,4},{6,5},{7,6},{8,11},{9,8},{10,9... | collective-permute-start | bytes 565256 | tf_op jit(solution)/shard_map/ppermute | solution.py:248
  13.1 2.1 %collective-permute-start.2 = (f32[2,7,32,128]{3,2,1,0:T(8,128)S(1)}, f32[2,7,32,128]{3,2,1,0:T(8,128)S(1)}, u32[]{:S(2)}, u32[]{:S(2)}) collective-permute-start(f32[2,7,32,128]{3,2,1,0:T(8,128)S(1)} %pad_maximum_fusion.1), channel_id=1, source_target_pairs={{0,4},{4,0},{8,12},{12,8},{16,20},{20,16},{24,28},{28,24},{1,5},{5... | collective-permute-start | bytes 688136 | tf_op jit(solution)/shard_map/ppermute | solution.py:262
  15.5 0.9 %collective-permute-done.2.other_ref = f32[2,7,32,128]{3,2,1,0:T(8,128)S(1)} collective-permute-done((f32[2,7,32,128]{3,2,1,0:T(8,128)S(1)}, f32[2,7,32,128]{3,2,1,0:T(8,128)S(1)}, u32[]{:S(2)}, u32[]{:S(2)}) %collective-permute-start.2) | collective-permute-done | bytes 229408 | tf_op jit(solution)/shard_map/ppermute | solution.py:262
  16.4 4.7 %shard_map.64 = (f32[48,32,128]{2,1,0:T(8,128)S(1)}, bf16[256,256]{1,0:T(8,128)(2,1)S(1)}, bf16[256,256]{1,0:T(8,128)(2,1)S(1)}, bf16[256,256]{1,0:T(8,128)(2,1)S(1)}) custom-call(s32[3]{0:T(128)S(1)} %pad_add_fusion.scalar_ref, f32[3,15]{1,0:T(4,128)S(1)} %broadcast_select_fusion.2.taps_ref, f32[32,32,128]{2,1,0:T(8,128)S(1)} %copy-done.2, ...), custom_call_target="tpu_custom_call" | custom-call | tf_op jit(solution)/shard_map/pallas_call | solution.py:266
  21.1 3.6 %collective-permute-done.4.refs_2_ = f32[368,128]{1,0:T(8,128)S(1)} collective-permute-done((f32[368,128]{1,0:T(8,128)S(1)}, f32[368,128]{1,0:T(8,128)S(1)}, u32[]{:S(2)}, u32[]{:S(2)}) %collective-permute-start.4) | collective-permute-done | bytes 188448 | tf_op jit(solution)/shard_map/ppermute | solution.py:248
  24.7 3.3 %collective-permute-done.5.refs_3_ = f32[368,128]{1,0:T(8,128)S(1)} collective-permute-done((f32[368,128]{1,0:T(8,128)S(1)}, f32[368,128]{1,0:T(8,128)S(1)}, u32[]{:S(2)}, u32[]{:S(2)}) %collective-permute-start.5) | collective-permute-done | bytes 188448 | tf_op jit(solution)/shard_map/ppermute | solution.py:248
  28.6 2.5 %shard_map.66 = (f32[16,32,128]{2,1,0:T(8,128)S(1)}, f32[16,32,128]{2,1,0:T(8,128)S(1)}) custom-call(s32[3]{0:T(128)S(1)} %pad_add_fusion.scalar_ref, f32[3,15]{1,0:T(4,128)S(1)} %broadcast_select_fusion.2.taps_ref, s32[32]{0:T(128)S(1)} %bitcast.14, f32[1024,128]{1,0:T(8,128)S(1)} %bitcast.11, f32[48,32,128]{2,1,0:T(8,128)S(1)} %get-tuple-element.15.inverse_ref, ...), custom_call_target="tpu_custom_call" | custom-call | tf_op jit(solution)/shard_map/pallas_call | solution.py:281
  31.1 0.9 %collective-permute-start.6 = (f32[16,32,128]{2,1,0:T(8,128)S(1)}, f32[16,32,128]{2,1,0:T(8,128)S(1)}, u32[]{:S(2)}, u32[]{:S(2)}) collective-permute-start(f32[16,32,128]{2,1,0:T(8,128)S(1)} %get-tuple-element.24), channel_id=1, source_target_pairs={{0,4},{4,0},{8,12},{12,8},{16,20},{20,16},{24,28},{28,24},{1,5},{5... | collective-permute-start | bytes 786440 | tf_op jit(solution)/shard_map/ppermute | solution.py:295
  32.0 1.2 %collective-permute-done.6 = f32[16,32,128]{2,1,0:T(8,128)S(1)} collective-permute-done((f32[16,32,128]{2,1,0:T(8,128)S(1)}, f32[16,32,128]{2,1,0:T(8,128)S(1)}, u32[]{:S(2)}, u32[]{:S(2)}) %collective-permute-start.6) | collective-permute-done | bytes 262176 | tf_op jit(solution)/shard_map/ppermute | solution.py:295
  33.2 0.8 %collective-permute-start.7 = (f32[4,32,128]{2,1,0:T(8,128)S(1)}, f32[4,32,128]{2,1,0:T(8,128)S(1)}, u32[]{:S(2)}, u32[]{:S(2)}) collective-permute-start(f32[4,32,128]{2,1,0:T(8,128)S(1)} %get-tuple-element.31), channel_id=1, source_target_pairs={{0,8},{4,12},{8,0},{12,4},{16,24},{20,28},{24,16},{28,20},{1,9},{5... | collective-permute-start | bytes 196616 | tf_op jit(solution)/shard_map/ppermute | solution.py:299
  34.1 1.2 %collective-permute-start.8 = (f32[4,32,128]{2,1,0:T(8,128)S(1)}, f32[4,32,128]{2,1,0:T(8,128)S(1)}, u32[]{:S(2)}, u32[]{:S(2)}) collective-permute-start(f32[4,32,128]{2,1,0:T(8,128)S(1)} %get-tuple-element.33), channel_id=1, source_target_pairs={{0,16},{4,20},{8,24},{12,28},{16,0},{20,4},{24,8},{28,12},{1,17},{... | collective-permute-start | bytes 196616 | tf_op jit(solution)/shard_map/ppermute | solution.py:299
  36.4 1.1 %collective-permute-done.8 = f32[4,32,128]{2,1,0:T(8,128)S(1)} collective-permute-done((f32[4,32,128]{2,1,0:T(8,128)S(1)}, f32[4,32,128]{2,1,0:T(8,128)S(1)}, u32[]{:S(2)}, u32[]{:S(2)}) %collective-permute-start.8) | collective-permute-done | bytes 65568 | tf_op jit(solution)/shard_map/ppermute | solution.py:299
  37.5 1.8 %collective-permute-done.9 = f32[4,32,128]{2,1,0:T(8,128)S(1)} collective-permute-done((f32[4,32,128]{2,1,0:T(8,128)S(1)}, f32[4,32,128]{2,1,0:T(8,128)S(1)}, u32[]{:S(2)}, u32[]{:S(2)}) %collective-permute-start.9) | collective-permute-done | bytes 65568 | tf_op jit(solution)/shard_map/ppermute | solution.py:299
  40.5 1.6 %collective-permute-start.12 = (f32[4,32,128]{2,1,0:T(8,128)S(1)}, f32[4,32,128]{2,1,0:T(8,128)S(1)}, u32[]{:S(2)}, u32[]{:S(2)}) collective-permute-start(f32[4,32,128]{2,1,0:T(8,128)S(1)} %get-tuple-element.26), channel_id=1, source_target_pairs={{0,24},{4,28},{8,16},{12,20},{16,8},{20,12},{24,0},{28,4},{1,25},{... | collective-permute-start | bytes 196616 | tf_op jit(solution)/shard_map/ppermute | solution.py:311
  43.0 1.8 %collective-permute-done.12 = f32[4,32,128]{2,1,0:T(8,128)S(1)} collective-permute-done((f32[4,32,128]{2,1,0:T(8,128)S(1)}, f32[4,32,128]{2,1,0:T(8,128)S(1)}, u32[]{:S(2)}, u32[]{:S(2)}) %collective-permute-start.12) | collective-permute-done | bytes 65568 | tf_op jit(solution)/shard_map/ppermute | solution.py:311
  44.7 3.5 %collective-permute-start.13 = (f32[16,32,128]{2,1,0:T(8,128)S(1)}, f32[16,32,128]{2,1,0:T(8,128)S(1)}, u32[]{:S(2)}, u32[]{:S(2)}) collective-permute-start(f32[16,32,128]{2,1,0:T(8,128)S(1)} %constant_dynamic-update-slice_fusion), channel_id=1, source_target_pairs={{0,4},{4,0},{8,12},{12,8},{16,20},{20,16},{24,28},{28,24},{1,5},{5... | collective-permute-start | bytes 786440 | tf_op jit(solution)/shard_map/ppermute | solution.py:313
  48.3 1.2 %collective-permute-done.13 = f32[16,32,128]{2,1,0:T(8,128)S(1)} collective-permute-done((f32[16,32,128]{2,1,0:T(8,128)S(1)}, f32[16,32,128]{2,1,0:T(8,128)S(1)}, u32[]{:S(2)}, u32[]{:S(2)}) %collective-permute-start.13) | collective-permute-done | bytes 262176 | tf_op jit(solution)/shard_map/ppermute | solution.py:313
  49.5 0.8 %pad_maximum_fusion = f32[32,32,128]{2,1,0:T(8,128)} fusion(f32[16,32,128]{2,1,0:T(8,128)S(1)} %get-tuple-element.28, f32[16,32,128]{2,1,0:T(8,128)S(1)} %get-tuple-element.27), kind=kLoop, calls=%fused_computation | loop fusion | flops 131072 | bytes 1048576 | tf_op jit(solution)/shard_map/concatenate | solution.py:314
  (33 shorter events, 4.7 us)
Async XLA Ops:
  1.0 12.1 %collective-permute-start = (f32[7,32,128]{2,1,0:T(8,128)S(1)}, f32[7,32,128]{2,1,0:T(8,128)S(1)}, u32[]{:S(2)}, u32[]{:S(2)}) collective-permute-start(f32[7,32,128]{2,1,0:T(8,128)S(1)} %get-tuple-element.30), channel_id=1, source_target_pairs={{0,1},{1,2},{2,3},{4,5},{5,6},{6,7},{8,9},{9,10},{10,11},{12,13},{... | collective-permute-start | bytes 344072 | tf_op jit(solution)/shard_map/ppermute | solution.py:255
  4.2 8.9 %collective-permute-start.1 = (f32[7,32,128]{2,1,0:T(8,128)S(1)}, f32[7,32,128]{2,1,0:T(8,128)S(1)}, u32[]{:S(2)}, u32[]{:S(2)}) collective-permute-start(f32[7,32,128]{2,1,0:T(8,128)S(1)} %get-tuple-element.29), channel_id=1, source_target_pairs={{1,0},{2,1},{3,2},{5,4},{6,5},{7,6},{9,8},{10,9},{11,10},{13,12},{... | collective-permute-start | bytes 344072 | tf_op jit(solution)/shard_map/ppermute | solution.py:259
  6.9 1.0 %copy-start = (f32[1,32,32,128]{3,2,1,0:T(8,128)S(1)}, f32[1,32,32,128]{3,2,1,0:T(8,128)}, u32[]{:S(2)}) copy-start(f32[1,32,32,128]{3,2,1,0:T(8,128)} %param.7) | copy-start | bytes 1572868
  8.0 8.4 %copy-start.2 = (f32[32,32,128]{2,1,0:T(8,128)S(1)}, f32[32,32,128]{2,1,0:T(8,128)}, u32[]{:S(2)}) copy-start(f32[32,32,128]{2,1,0:T(8,128)} %estimate_ref.1) | copy-start | bytes 1572868
  8.4 12.7 %collective-permute-start.3 = (f32[368,128]{1,0:T(8,128)S(1)}, f32[368,128]{1,0:T(8,128)S(1)}, u32[]{:S(2)}, u32[]{:S(2)}) collective-permute-start(f32[368,128]{1,0:T(8,128)S(1)} %get-tuple-element.20), channel_id=1, source_target_pairs={{0,1},{1,2},{2,3},{3,0},{4,5},{5,6},{6,7},{7,4},{8,9},{9,10},{10,1... | collective-permute-start | bytes 565256 | tf_op jit(solution)/shard_map/ppermute | solution.py:248
  9.8 3.1 %copy-start.4 = (f32[1,3,15]{2,0,1:T(1,128)S(1)}, f32[1,3,15]{2,0,1:T(1,128)}, u32[]{:S(2)}) copy-start(f32[1,3,15]{2,0,1:T(1,128)} %param.8) | copy-start | bytes 544
  9.8 14.9 %collective-permute-start.4 = (f32[368,128]{1,0:T(8,128)S(1)}, f32[368,128]{1,0:T(8,128)S(1)}, u32[]{:S(2)}, u32[]{:S(2)}) collective-permute-start(f32[368,128]{1,0:T(8,128)S(1)} %get-tuple-element.21), channel_id=1, source_target_pairs={{0,2},{1,3},{2,0},{3,1},{4,6},{5,7},{6,4},{7,5},{8,10},{9,11},{10,... | collective-permute-start | bytes 565256 | tf_op jit(solution)/shard_map/ppermute | solution.py:248
  10.9 17.1 %collective-permute-start.5 = (f32[368,128]{1,0:T(8,128)S(1)}, f32[368,128]{1,0:T(8,128)S(1)}, u32[]{:S(2)}, u32[]{:S(2)}) collective-permute-start(f32[368,128]{1,0:T(8,128)S(1)} %get-tuple-element.22), channel_id=1, source_target_pairs={{0,3},{1,0},{2,1},{3,2},{4,7},{5,4},{6,5},{7,6},{8,11},{9,8},{10,9... | collective-permute-start | bytes 565256 | tf_op jit(solution)/shard_map/ppermute | solution.py:248
  13.1 14.8 %copy-start.1 = (f32[1,32,32,128]{3,2,1,0:T(8,128)S(1)}, f32[1,32,32,128]{3,2,1,0:T(8,128)}, u32[]{:S(2)}) copy-start(f32[1,32,32,128]{3,2,1,0:T(8,128)} %param.7) | copy-start | bytes 1572868
  13.1 3.3 %collective-permute-start.2 = (f32[2,7,32,128]{3,2,1,0:T(8,128)S(1)}, f32[2,7,32,128]{3,2,1,0:T(8,128)S(1)}, u32[]{:S(2)}, u32[]{:S(2)}) collective-permute-start(f32[2,7,32,128]{3,2,1,0:T(8,128)S(1)} %pad_maximum_fusion.1), channel_id=1, source_target_pairs={{0,4},{4,0},{8,12},{12,8},{16,20},{20,16},{24,28},{28,24},{1,5},{5... | collective-permute-start | bytes 688136 | tf_op jit(solution)/shard_map/ppermute | solution.py:262
  27.9 0.7 %copy-start.3 = (s32[1,32]{1,0:T(1,128)S(1)}, s32[1,32]{1,0:T(1,128)}, u32[]{:S(2)}) copy-start(s32[1,32]{1,0:T(1,128)} %param.11) | copy-start | bytes 388
  31.1 2.0 %collective-permute-start.6 = (f32[16,32,128]{2,1,0:T(8,128)S(1)}, f32[16,32,128]{2,1,0:T(8,128)S(1)}, u32[]{:S(2)}, u32[]{:S(2)}) collective-permute-start(f32[16,32,128]{2,1,0:T(8,128)S(1)} %get-tuple-element.24), channel_id=1, source_target_pairs={{0,4},{4,0},{8,12},{12,8},{16,20},{20,16},{24,28},{28,24},{1,5},{5... | collective-permute-start | bytes 786440 | tf_op jit(solution)/shard_map/ppermute | solution.py:295
  33.2 3.2 %collective-permute-start.7 = (f32[4,32,128]{2,1,0:T(8,128)S(1)}, f32[4,32,128]{2,1,0:T(8,128)S(1)}, u32[]{:S(2)}, u32[]{:S(2)}) collective-permute-start(f32[4,32,128]{2,1,0:T(8,128)S(1)} %get-tuple-element.31), channel_id=1, source_target_pairs={{0,8},{4,12},{8,0},{12,4},{16,24},{20,28},{24,16},{28,20},{1,9},{5... | collective-permute-start | bytes 196616 | tf_op jit(solution)/shard_map/ppermute | solution.py:299
  34.1 3.4 %collective-permute-start.8 = (f32[4,32,128]{2,1,0:T(8,128)S(1)}, f32[4,32,128]{2,1,0:T(8,128)S(1)}, u32[]{:S(2)}, u32[]{:S(2)}) collective-permute-start(f32[4,32,128]{2,1,0:T(8,128)S(1)} %get-tuple-element.33), channel_id=1, source_target_pairs={{0,16},{4,20},{8,24},{12,28},{16,0},{20,4},{24,8},{28,12},{1,17},{... | collective-permute-start | bytes 196616 | tf_op jit(solution)/shard_map/ppermute | solution.py:299
  35.3 4.0 %collective-permute-start.9 = (f32[4,32,128]{2,1,0:T(8,128)S(1)}, f32[4,32,128]{2,1,0:T(8,128)S(1)}, u32[]{:S(2)}, u32[]{:S(2)}) collective-permute-start(f32[4,32,128]{2,1,0:T(8,128)S(1)} %get-tuple-element.32), channel_id=1, source_target_pairs={{0,24},{4,28},{8,16},{12,20},{16,8},{20,12},{24,0},{28,4},{1,25},{... | collective-permute-start | bytes 196616 | tf_op jit(solution)/shard_map/ppermute | solution.py:299
  39.4 3.2 %collective-permute-start.10 = (f32[4,32,128]{2,1,0:T(8,128)S(1)}, f32[4,32,128]{2,1,0:T(8,128)S(1)}, u32[]{:S(2)}, u32[]{:S(2)}) collective-permute-start(f32[4,32,128]{2,1,0:T(8,128)S(1)} %get-tuple-element.26), channel_id=1, source_target_pairs={{0,8},{4,12},{8,0},{12,4},{16,24},{20,28},{24,16},{28,20},{1,9},{5... | collective-permute-start | bytes 196616 | tf_op jit(solution)/shard_map/ppermute | solution.py:311
  39.8 3.1 %collective-permute-start.11 = (f32[4,32,128]{2,1,0:T(8,128)S(1)}, f32[4,32,128]{2,1,0:T(8,128)S(1)}, u32[]{:S(2)}, u32[]{:S(2)}) collective-permute-start(f32[4,32,128]{2,1,0:T(8,128)S(1)} %get-tuple-element.26), channel_id=1, source_target_pairs={{0,16},{4,20},{8,24},{12,28},{16,0},{20,4},{24,8},{28,12},{1,17},{... | collective-permute-start | bytes 196616 | tf_op jit(solution)/shard_map/ppermute | solution.py:311
  40.5 4.2 %collective-permute-start.12 = (f32[4,32,128]{2,1,0:T(8,128)S(1)}, f32[4,32,128]{2,1,0:T(8,128)S(1)}, u32[]{:S(2)}, u32[]{:S(2)}) collective-permute-start(f32[4,32,128]{2,1,0:T(8,128)S(1)} %get-tuple-element.26), channel_id=1, source_target_pairs={{0,24},{4,28},{8,16},{12,20},{16,8},{20,12},{24,0},{28,4},{1,25},{... | collective-permute-start | bytes 196616 | tf_op jit(solution)/shard_map/ppermute | solution.py:311
  44.7 4.7 %collective-permute-start.13 = (f32[16,32,128]{2,1,0:T(8,128)S(1)}, f32[16,32,128]{2,1,0:T(8,128)S(1)}, u32[]{:S(2)}, u32[]{:S(2)}) collective-permute-start(f32[16,32,128]{2,1,0:T(8,128)S(1)} %constant_dynamic-update-slice_fusion), channel_id=1, source_target_pairs={{0,4},{4,0},{8,12},{12,8},{16,20},{20,16},{24,28},{28,24},{1,5},{5... | collective-permute-start | bytes 786440 | tf_op jit(solution)/shard_map/ppermute | solution.py:313

commit v2 on v1

--- a/solution.py
+++ b/solution.py
@@ -252,12 +252,13 @@
     swap = [(i, i ^ 1) for i in range(views)]
     forward = [(i, i + 1) for i in range(count - 1)]
     backward = [(i + 1, i) for i in range(count - 1)]
+    later, _ = lax.optimization_barrier((estimate, packed[1]))
     low = lax.ppermute(
-        lax.dynamic_slice_in_dim(estimate, zb - 2 * reach + reach * core, reach, 0),
+        lax.dynamic_slice_in_dim(later, zb - 2 * reach + reach * core, reach, 0),
         "bulk", forward,
     )
     high = lax.ppermute(
-        lax.dynamic_slice_in_dim(estimate, reach * core, reach, 0), "bulk", backward
+        lax.dynamic_slice_in_dim(later, reach * core, reach, 0), "bulk", backward
     )
     other = lax.ppermute(jnp.stack([low, high]), "view", swap)
 
@@ -290,26 +291,15 @@
         compiler_params=PARAMS,
     )(scalars, joined_taps, visible[0], stack, inverse, rows_high, rows_low, lanes_pair, *blocks)
 
-    chips = views // 2
-    piece = half // chips
-    summed = keep + lax.ppermute(send, "view", swap)
-    total = lax.dynamic_slice_in_dim(summed, chip * piece, piece, 0)
-    partners = [[(i, i ^ (2 * d)) for i in range(views)] for d in range(1, chips)]
-    arrived = [
-        lax.ppermute(
-            lax.dynamic_slice_in_dim(summed, (chip ^ (d + 1)) * piece, piece, 0), "view", pairs
+    total = keep + lax.ppermute(send, "view", swap)
+    bits = (views // 2).bit_length() - 1
+    for step in range(bits):
+        flips = [2 << step, 2 << ((step + bits - 1) % bits)]
+        total = total + lax.ppermute(
+            total, "view", [(i, i ^ flips[i % 2]) for i in range(views)]
         )
-        for d, pairs in enumerate(partners)
-    ]
-    for part in arrived:
-        total = total + part
-    mine = lax.dynamic_slice_in_dim(estimate, core * half + chip * piece, piece, 0)
-    mine = mine * jnp.exp(total / float(views))
-    own = jnp.zeros((half, ny, nx), jnp.float32)
-    own = lax.dynamic_update_slice_in_dim(own, mine, chip * piece, 0)
-    for d, pairs in enumerate(partners):
-        part = lax.ppermute(mine, "view", pairs)
-        own = lax.dynamic_update_slice_in_dim(own, part, (chip ^ (d + 1)) * piece, 0)
+    own = lax.dynamic_slice_in_dim(estimate, core * half, half, 0)
+    own = own * jnp.exp(total / float(views))
     their = lax.ppermute(own, "view", swap)
     return jnp.concatenate(
         [jnp.where(core == 0, own, their), jnp.where(core == 0, their, own)], axis=0

time: 50.6 us -> 46.4 us (0.917)
  the two profiles are of different devices: /device:TPU:9 before, /device:TPU:0 now
where the time goes in v2:
time: 46.4 us; the launch traced here: 46 us
  waiting for transfers between devices  19 us (41%)
  starting transfers between devices  14.8 us (32%)
  Pallas kernels  7.65 us (16%)
  local copies, waits for them, and re-layouts  1.75 us (4%)
  between operations  1.45 us (3%)
  other arithmetic  1.36 us (3%)
    ppermute x2, waiting for transfers between devices, shards(): lax.ppermute(total, 'view', [(i, i ^ flips[i % 2]) for i in range(views)])  11.2 us
    ppermute x3, starting transfers between devices, shards(): lax.ppermute(packed[d], 'bulk', [(i, (i + d) % count) for i in range(coun...  8.14 us
    pallas_call x1, Pallas kernels, shards(): pl.pallas_call(functools.partial(forward_kernel, zb, ny, nx, planes), out...  4.68 us
    ppermute x1, starting transfers between devices, shards(): lax.ppermute(lax.dynamic_slice_in_dim(later, zb - 2 * reach + reach * cor...  3.49 us
    ppermute x3, waiting for transfers between devices, shards(): lax.ppermute(packed[d], 'bulk', [(i, (i + d) % count) for i in range(coun...  2.68 us
    pallas_call x1, Pallas kernels, shards(): pl.pallas_call(functools.partial(adjoint_kernel, zb, ny, nx, count), out_...  2.53 us
    unnamed x10, local copies, waits for them, and re-layouts  1.7 us
    ppermute x2, starting transfers between devices, shards(): lax.ppermute(total, 'view', [(i, i ^ flips[i % 2]) for i in range(views)])  1.66 us
  transfers between devices with their start and end apart: 10, of which 7 were waited for; matrix products, arithmetic and copies ran while one was open for 1% of the time, Pallas kernels for 10%

profile of v2, /device:TPU:0, one launch (start us, length us, event | category | flops | bytes accessed | tf_op | source)
XLA Modules:
  0.0 46.0 jit_solution(15457718981426189819)
XLA Ops:
  0.7 1.0 %copy-done = f32[1,32,32,128]{3,2,1,0:T(8,128)S(1)} copy-done((f32[1,32,32,128]{3,2,1,0:T(8,128)S(1)}, f32[1,32,32,128]{3,2,1,0:T(8,128)}, u32[]{:S(2)}) %copy-start) | copy-done | bytes 524312
  1.7 0.4 shard_map.64
  2.2 3.1 %collective-permute-start.3 = (f32[368,128]{1,0:T(8,128)S(1)}, f32[368,128]{1,0:T(8,128)S(1)}, u32[]{:S(2)}, u32[]{:S(2)}) collective-permute-start(f32[368,128]{1,0:T(8,128)S(1)} %get-tuple-element.16), channel_id=1, source_target_pairs={{0,1},{1,2},{2,3},{3,0},{4,5},{5,6},{6,7},{7,4},{8,9},{9,10},{10,1... | collective-permute-start | bytes 565256 | tf_op jit(solution)/shard_map/ppermute | solution.py:248
  5.3 3.5 %collective-permute-start = (f32[7,32,128]{2,1,0:T(8,128)S(1)}, f32[7,32,128]{2,1,0:T(8,128)S(1)}, u32[]{:S(2)}, u32[]{:S(2)}) collective-permute-start(f32[7,32,128]{2,1,0:T(8,128)S(1)} %get-tuple-element.30), channel_id=1, source_target_pairs={{0,1},{1,2},{2,3},{4,5},{5,6},{6,7},{8,9},{9,10},{10,11},{12,13},{... | collective-permute-start | bytes 344072 | tf_op jit(solution)/shard_map/ppermute | solution.py:256
  8.7 1.3 %collective-permute-start.1 = (f32[7,32,128]{2,1,0:T(8,128)S(1)}, f32[7,32,128]{2,1,0:T(8,128)S(1)}, u32[]{:S(2)}, u32[]{:S(2)}) collective-permute-start(f32[7,32,128]{2,1,0:T(8,128)S(1)} %get-tuple-element.29), channel_id=1, source_target_pairs={{1,0},{2,1},{3,2},{5,4},{6,5},{7,6},{9,8},{10,9},{11,10},{13,12},{... | collective-permute-start | bytes 344072 | tf_op jit(solution)/shard_map/ppermute | solution.py:260
  10.1 3.7 %collective-permute-start.4 = (f32[368,128]{1,0:T(8,128)S(1)}, f32[368,128]{1,0:T(8,128)S(1)}, u32[]{:S(2)}, u32[]{:S(2)}) collective-permute-start(f32[368,128]{1,0:T(8,128)S(1)} %get-tuple-element.23), channel_id=1, source_target_pairs={{0,2},{1,3},{2,0},{3,1},{4,6},{5,7},{6,4},{7,5},{8,10},{9,11},{10,... | collective-permute-start | bytes 565256 | tf_op jit(solution)/shard_map/ppermute | solution.py:248
  13.8 1.4 %collective-permute-start.5 = (f32[368,128]{1,0:T(8,128)S(1)}, f32[368,128]{1,0:T(8,128)S(1)}, u32[]{:S(2)}, u32[]{:S(2)}) collective-permute-start(f32[368,128]{1,0:T(8,128)S(1)} %get-tuple-element.24), channel_id=1, source_target_pairs={{0,3},{1,0},{2,1},{3,2},{4,7},{5,4},{6,5},{7,6},{8,11},{9,8},{10,9... | collective-permute-start | bytes 565256 | tf_op jit(solution)/shard_map/ppermute | solution.py:248
  15.8 0.1 reduce_sum.9
  15.9 0.1 bitcast_divide_fusion
  16.0 0.8 %collective-permute-done.1.high_ref = f32[7,32,128]{2,1,0:T(8,128)S(1)} collective-permute-done((f32[7,32,128]{2,1,0:T(8,128)S(1)}, f32[7,32,128]{2,1,0:T(8,128)S(1)}, u32[]{:S(2)}, u32[]{:S(2)}) %collective-permute-start.1) | collective-permute-done | bytes 114720 | tf_op jit(solution)/shard_map/ppermute | solution.py:260
  16.8 0.1 pad_add_fusion.scalar_ref
  16.9 0.1 broadcast_select_fusion.2.taps_ref
  17.0 1.3 %collective-permute-done.2.other_ref = f32[2,7,32,128]{3,2,1,0:T(8,128)S(1)} collective-permute-done((f32[2,7,32,128]{3,2,1,0:T(8,128)S(1)}, f32[2,7,32,128]{3,2,1,0:T(8,128)S(1)}, u32[]{:S(2)}, u32[]{:S(2)}) %collective-permute-start.2) | collective-permute-done | bytes 229408 | tf_op jit(solution)/shard_map/ppermute | solution.py:263
  18.3 4.7 %shard_map.65 = (f32[48,32,128]{2,1,0:T(8,128)S(1)}, bf16[256,256]{1,0:T(8,128)(2,1)S(1)}, bf16[256,256]{1,0:T(8,128)(2,1)S(1)}, bf16[256,256]{1,0:T(8,128)(2,1)S(1)}) custom-call(s32[3]{0:T(128)S(1)} %pad_add_fusion.scalar_ref, f32[3,15]{1,0:T(4,128)S(1)} %broadcast_select_fusion.2.taps_ref, f32[32,32,128]{2,1,0:T(8,128)S(1)} %copy-done.2, ...), custom_call_target="tpu_custom_call" | custom-call | tf_op jit(solution)/shard_map/pallas_call | solution.py:267
  23.0 2.7 %collective-permute-done.4.refs_2_ = f32[368,128]{1,0:T(8,128)S(1)} collective-permute-done((f32[368,128]{1,0:T(8,128)S(1)}, f32[368,128]{1,0:T(8,128)S(1)}, u32[]{:S(2)}, u32[]{:S(2)}) %collective-permute-start.4) | collective-permute-done | bytes 188448 | tf_op jit(solution)/shard_map/ppermute | solution.py:248
  25.7 0.6 %copy-done.3 = s32[1,32]{1,0:T(1,128)S(1)} copy-done((s32[1,32]{1,0:T(1,128)S(1)}, s32[1,32]{1,0:T(1,128)}, u32[]{:S(2)}) %copy-start.3) | copy-done | bytes 152
  26.3 2.5 %shard_map.66 = (f32[16,32,128]{2,1,0:T(8,128)S(1)}, f32[16,32,128]{2,1,0:T(8,128)S(1)}) custom-call(s32[3]{0:T(128)S(1)} %pad_add_fusion.scalar_ref, f32[3,15]{1,0:T(4,128)S(1)} %broadcast_select_fusion.2.taps_ref, s32[32]{0:T(128)S(1)} %bitcast.14, f32[1024,128]{1,0:T(8,128)S(1)} %bitcast.11, f32[48,32,128]{2,1,0:T(8,128)S(1)} %get-tuple-element.18.inverse_ref, ...), custom_call_target="tpu_custom_call" | custom-call | tf_op jit(solution)/shard_map/pallas_call | solution.py:282
  29.0 1.5 %collective-permute-done.6 = f32[16,32,128]{2,1,0:T(8,128)S(1)} collective-permute-done((f32[16,32,128]{2,1,0:T(8,128)S(1)}, f32[16,32,128]{2,1,0:T(8,128)S(1)}, u32[]{:S(2)}, u32[]{:S(2)}) %collective-permute-start.6) | collective-permute-done | bytes 262176 | tf_op jit(solution)/shard_map/ppermute | solution.py:294
  30.5 0.7 %collective-permute-start.7 = (f32[16,32,128]{2,1,0:T(8,128)S(1)}, f32[16,32,128]{2,1,0:T(8,128)S(1)}, u32[]{:S(2)}, u32[]{:S(2)}) collective-permute-start(f32[16,32,128]{2,1,0:T(8,128)S(1)} %add.28), channel_id=1, source_target_pairs={{0,8},{4,20},{8,0},{12,28},{16,24},{20,4},{24,16},{28,12},{1,9},{5... | collective-permute-start | bytes 786440 | tf_op jit(solution)/shard_map/ppermute | solution.py:298
  31.2 5.8 %collective-permute-done.7 = f32[16,32,128]{2,1,0:T(8,128)S(1)} collective-permute-done((f32[16,32,128]{2,1,0:T(8,128)S(1)}, f32[16,32,128]{2,1,0:T(8,128)S(1)}, u32[]{:S(2)}, u32[]{:S(2)}) %collective-permute-start.7) | collective-permute-done | bytes 262176 | tf_op jit(solution)/shard_map/ppermute | solution.py:298
  37.0 1.0 %collective-permute-start.8 = (f32[16,32,128]{2,1,0:T(8,128)S(1)}, f32[16,32,128]{2,1,0:T(8,128)S(1)}, u32[]{:S(2)}, u32[]{:S(2)}) collective-permute-start(f32[16,32,128]{2,1,0:T(8,128)S(1)} %add.29), channel_id=1, source_target_pairs={{0,16},{4,12},{8,24},{12,4},{16,0},{20,28},{24,8},{28,20},{1,17},{... | collective-permute-start | bytes 786440 | tf_op jit(solution)/shard_map/ppermute | solution.py:298
  38.0 5.4 %collective-permute-done.8 = f32[16,32,128]{2,1,0:T(8,128)S(1)} collective-permute-done((f32[16,32,128]{2,1,0:T(8,128)S(1)}, f32[16,32,128]{2,1,0:T(8,128)S(1)}, u32[]{:S(2)}, u32[]{:S(2)}) %collective-permute-start.8) | collective-permute-done | bytes 262176 | tf_op jit(solution)/shard_map/ppermute | solution.py:298
  43.6 1.5 %collective-permute-done.9 = f32[16,32,128]{2,1,0:T(8,128)S(1)} collective-permute-done((f32[16,32,128]{2,1,0:T(8,128)S(1)}, f32[16,32,128]{2,1,0:T(8,128)S(1)}, u32[]{:S(2)}, u32[]{:S(2)}) %collective-permute-start.9) | collective-permute-done | bytes 262176 | tf_op jit(solution)/shard_map/ppermute | solution.py:303
  45.2 0.8 %pad_maximum_fusion = f32[32,32,128]{2,1,0:T(8,128)} fusion(f32[16,32,128]{2,1,0:T(8,128)S(1)} %get-tuple-element.28, f32[16,32,128]{2,1,0:T(8,128)S(1)} %get-tuple-element.27), kind=kLoop, calls=%fused_computation | loop fusion | flops 131072 | bytes 1048576 | tf_op jit(solution)/shard_map/concatenate | solution.py:304
  (21 shorter events, 0.5 us)
Async XLA Ops:
  0.7 1.0 %copy-start = (f32[1,32,32,128]{3,2,1,0:T(8,128)S(1)}, f32[1,32,32,128]{3,2,1,0:T(8,128)}, u32[]{:S(2)}) copy-start(f32[1,32,32,128]{3,2,1,0:T(8,128)} %param.7) | copy-start | bytes 1572868
  1.7 3.5 %copy-start.2 = (f32[32,32,128]{2,1,0:T(8,128)S(1)}, f32[32,32,128]{2,1,0:T(8,128)}, u32[]{:S(2)}) copy-start(f32[32,32,128]{2,1,0:T(8,128)} %estimate_ref.1) | copy-start | bytes 1572868
  2.2 20.9 %collective-permute-start.3 = (f32[368,128]{1,0:T(8,128)S(1)}, f32[368,128]{1,0:T(8,128)S(1)}, u32[]{:S(2)}, u32[]{:S(2)}) collective-permute-start(f32[368,128]{1,0:T(8,128)S(1)} %get-tuple-element.16), channel_id=1, source_target_pairs={{0,1},{1,2},{2,3},{3,0},{4,5},{5,6},{6,7},{7,4},{8,9},{9,10},{10,1... | collective-permute-start | bytes 565256 | tf_op jit(solution)/shard_map/ppermute | solution.py:248
  5.3 10.7 %collective-permute-start = (f32[7,32,128]{2,1,0:T(8,128)S(1)}, f32[7,32,128]{2,1,0:T(8,128)S(1)}, u32[]{:S(2)}, u32[]{:S(2)}) collective-permute-start(f32[7,32,128]{2,1,0:T(8,128)S(1)} %get-tuple-element.30), channel_id=1, source_target_pairs={{0,1},{1,2},{2,3},{4,5},{5,6},{6,7},{8,9},{9,10},{10,11},{12,13},{... | collective-permute-start | bytes 344072 | tf_op jit(solution)/shard_map/ppermute | solution.py:256
  8.7 8.0 %collective-permute-start.1 = (f32[7,32,128]{2,1,0:T(8,128)S(1)}, f32[7,32,128]{2,1,0:T(8,128)S(1)}, u32[]{:S(2)}, u32[]{:S(2)}) collective-permute-start(f32[7,32,128]{2,1,0:T(8,128)S(1)} %get-tuple-element.29), channel_id=1, source_target_pairs={{1,0},{2,1},{3,2},{5,4},{6,5},{7,6},{9,8},{10,9},{11,10},{13,12},{... | collective-permute-start | bytes 344072 | tf_op jit(solution)/shard_map/ppermute | solution.py:260
  10.0 5.7 %copy-start.4 = (f32[1,3,15]{2,0,1:T(1,128)S(1)}, f32[1,3,15]{2,0,1:T(1,128)}, u32[]{:S(2)}) copy-start(f32[1,3,15]{2,0,1:T(1,128)} %param.8) | copy-start | bytes 544
  10.1 15.6 %collective-permute-start.4 = (f32[368,128]{1,0:T(8,128)S(1)}, f32[368,128]{1,0:T(8,128)S(1)}, u32[]{:S(2)}, u32[]{:S(2)}) collective-permute-start(f32[368,128]{1,0:T(8,128)S(1)} %get-tuple-element.23), channel_id=1, source_target_pairs={{0,2},{1,3},{2,0},{3,1},{4,6},{5,7},{6,4},{7,5},{8,10},{9,11},{10,... | collective-permute-start | bytes 565256 | tf_op jit(solution)/shard_map/ppermute | solution.py:248
  13.8 11.9 %collective-permute-start.5 = (f32[368,128]{1,0:T(8,128)S(1)}, f32[368,128]{1,0:T(8,128)S(1)}, u32[]{:S(2)}, u32[]{:S(2)}) collective-permute-start(f32[368,128]{1,0:T(8,128)S(1)} %get-tuple-element.24), channel_id=1, source_target_pairs={{0,3},{1,0},{2,1},{3,2},{4,7},{5,4},{6,5},{7,6},{8,11},{9,8},{10,9... | collective-permute-start | bytes 565256 | tf_op jit(solution)/shard_map/ppermute | solution.py:248
  16.8 8.9 %copy-start.1 = (f32[1,32,32,128]{3,2,1,0:T(8,128)S(1)}, f32[1,32,32,128]{3,2,1,0:T(8,128)}, u32[]{:S(2)}) copy-start(f32[1,32,32,128]{3,2,1,0:T(8,128)} %param.7) | copy-start | bytes 1572868
  16.8 1.6 %collective-permute-start.2 = (f32[2,7,32,128]{3,2,1,0:T(8,128)S(1)}, f32[2,7,32,128]{3,2,1,0:T(8,128)S(1)}, u32[]{:S(2)}, u32[]{:S(2)}) collective-permute-start(f32[2,7,32,128]{3,2,1,0:T(8,128)S(1)} %pad_maximum_fusion.1), channel_id=1, source_target_pairs={{0,4},{4,0},{8,12},{12,8},{16,20},{20,16},{24,28},{28,24},{1,5},{5... | collective-permute-start | bytes 688136 | tf_op jit(solution)/shard_map/ppermute | solution.py:263
  25.7 0.7 %copy-start.3 = (s32[1,32]{1,0:T(1,128)S(1)}, s32[1,32]{1,0:T(1,128)}, u32[]{:S(2)}) copy-start(s32[1,32]{1,0:T(1,128)} %param.11) | copy-start | bytes 388
  28.9 1.6 %collective-permute-start.6 = (f32[16,32,128]{2,1,0:T(8,128)S(1)}, f32[16,32,128]{2,1,0:T(8,128)S(1)}, u32[]{:S(2)}, u32[]{:S(2)}) collective-permute-start(f32[16,32,128]{2,1,0:T(8,128)S(1)} %get-tuple-element.26), channel_id=1, source_target_pairs={{0,4},{4,0},{8,12},{12,8},{16,20},{20,16},{24,28},{28,24},{1,5},{5... | collective-permute-start | bytes 786440 | tf_op jit(solution)/shard_map/ppermute | solution.py:294
  30.5 6.4 %collective-permute-start.7 = (f32[16,32,128]{2,1,0:T(8,128)S(1)}, f32[16,32,128]{2,1,0:T(8,128)S(1)}, u32[]{:S(2)}, u32[]{:S(2)}) collective-permute-start(f32[16,32,128]{2,1,0:T(8,128)S(1)} %add.28), channel_id=1, source_target_pairs={{0,8},{4,20},{8,0},{12,28},{16,24},{20,4},{24,16},{28,12},{1,9},{5... | collective-permute-start | bytes 786440 | tf_op jit(solution)/shard_map/ppermute | solution.py:298
  37.0 6.4 %collective-permute-start.8 = (f32[16,32,128]{2,1,0:T(8,128)S(1)}, f32[16,32,128]{2,1,0:T(8,128)S(1)}, u32[]{:S(2)}, u32[]{:S(2)}) collective-permute-start(f32[16,32,128]{2,1,0:T(8,128)S(1)} %add.29), channel_id=1, source_target_pairs={{0,16},{4,12},{8,24},{12,4},{16,0},{20,28},{24,8},{28,20},{1,17},{... | collective-permute-start | bytes 786440 | tf_op jit(solution)/shard_map/ppermute | solution.py:298
  43.5 1.6 %collective-permute-start.9 = (f32[16,32,128]{2,1,0:T(8,128)S(1)}, f32[16,32,128]{2,1,0:T(8,128)S(1)}, u32[]{:S(2)}, u32[]{:S(2)}) collective-permute-start(f32[16,32,128]{2,1,0:T(8,128)S(1)} %exponential_multiply_fusion), channel_id=1, source_target_pairs={{0,4},{4,0},{8,12},{12,8},{16,20},{20,16},{24,28},{28,24},{1,5},{5... | collective-permute-start | bytes 786440 | tf_op jit(solution)/shard_map/ppermute | solution.py:303

commit v3 on v0

v3 whole, which is shorter than its diff:
```python
import functools

import jax
import jax.numpy as jnp
from jax import lax
from jax.experimental import pallas as pl
from jax.experimental.pallas import tpu as pltpu
from jax.sharding import PartitionSpec as P

LANES = 128
ROWS = 8
WIDE = 256
VMEM = pl.BlockSpec(memory_space=pltpu.VMEM)
SMEM = pl.BlockSpec(memory_space=pltpu.SMEM)
COST = pl.CostEstimate(flops=2**29, bytes_accessed=2**21, transcendentals=2**16)
PARAMS = pltpu.CompilerParams(vmem_limit_bytes=40 * 1024 * 1024)


def struct(shape, dtype=jnp.float32):
    return jax.ShapeDtypeStruct(shape, dtype)


def halves(values):
    high = values.astype(jnp.bfloat16)
    low = (values - high.astype(jnp.float32)).astype(jnp.bfloat16)
    return high, low


def dot(left, right):
    return jnp.dot(left, right, preferred_element_type=jnp.float32)


def blur_rows(left_high, left_low, values):
    width = values.shape[1]
    high, low = halves(values)
    both = dot(left_high, jnp.concatenate([high, low], axis=1))
    return both[:, :width] + both[:, width:] + dot(left_low, high)


def blur_lanes(right, values):
    width = values.shape[1]
    out = dot(jnp.concatenate(halves(values), axis=1), right)
    return out[:, :width] + out[:, width:]


def lanes_matrix(taps_ref, row, extent, adjoint):
    taps = taps_ref.shape[1]
    source = lax.broadcasted_iota(jnp.int32, (extent, extent), 0)
    target = lax.broadcasted_iota(jnp.int32, (extent, extent), 1)
    offset = (target - source if adjoint else source - target) + taps // 2
    matrix = jnp.zeros((extent, extent), jnp.float32)
    for t in range(taps):
        matrix = jnp.where(offset == t, taps_ref[row, t], matrix)
    high, low = halves(matrix)
    pair = jnp.concatenate([high, low], axis=1)
    return jnp.concatenate([pair, pair], axis=0)


def rows_matrix(taps_ref, row, period, moved, adjoint):
    taps = taps_ref.shape[1]
    target = lax.broadcasted_iota(jnp.int32, (period, WIDE), 0)
    source = lax.broadcasted_iota(jnp.int32, (period, WIDE), 1)
    ahead = target - source if adjoint else source - target
    offset = jnp.bitwise_and(ahead + taps // 2 + moved, period - 1)
    block = jnp.zeros((period, WIDE), jnp.float32)
    for t in range(taps):
        block = jnp.where(offset == t, taps_ref[row, t], block)
    plane = source // period
    return halves(
        jnp.concatenate([jnp.where(plane == p, block, 0.0) for p in range(WIDE // period)], axis=0)
    )


def blur_planes(source_ref, splats, base, group):
    ny, nx = source_ref.shape[1:]
    taps = len(splats)
    columns = []
    for tile in range(nx // LANES):
        lanes = slice(tile * LANES, (tile + 1) * LANES)
        places = []
        for row in range(ny // ROWS):
            rows = slice(row * ROWS, (row + 1) * ROWS)
            source = [source_ref[base + i, rows, lanes] for i in range(group + taps - 1)]
            sums = []
            for plane in range(group):
                total = splats[0] * source[plane]
                for t in range(1, taps):
                    total = total + splats[t] * source[plane + t]
                sums.append(total)
            places.append(sums)
        columns.append(
            jnp.concatenate([sums[plane] for plane in range(group) for sums in places], axis=0)
        )
    return columns[0] if len(columns) == 1 else jnp.concatenate(columns, axis=1)


def pack_kernel(zb, ny, nx, count, image_ref, *refs):
    sends, (turned_ref, tile_ref) = refs[:count], refs[count:]
    reach = 7
    b = lax.axis_index("bulk")
    groups = ny // ROWS
    extent = (zb + 2 * reach) * ROWS
    edge = jnp.zeros((reach * ROWS, LANES), jnp.float32)
    turned_ref[: reach * ROWS] = edge
    turned_ref[(reach + nx) * ROWS :] = edge
    for tile in range(nx // LANES):
        if nx > LANES:
            tile_ref[...] = image_ref[:, tile * LANES : (tile + 1) * LANES]
            source = tile_ref
        else:
            source = image_ref
        for low in range(ROWS):
            pieces = [
                source[pl.ds(ROWS * group + low, zb, stride=ny), :] for group in range(groups)
            ]
            block = jnp.concatenate(pieces, axis=0).T
            turned_ref[pl.ds((tile * LANES + reach) * ROWS + low, LANES, stride=ROWS), :] = block
    for k in range(count):
        start = jnp.bitwise_xor(b, k) * (zb * ROWS)
        sends[k][...] = turned_ref[pl.ds(pl.multiple_of(start, ROWS), extent), :]


def forward_kernel(zb, ny, nx, planes, scalar_ref, taps_ref, visible_ref, estimate_ref, near1_ref,
                   near2_ref, other_ref, inverse_ref, rows_high_ref, rows_low_ref, lanes_ref,
                   weight_ref, splat_ref, flag_ref,
                   wide_ref):
    taps = taps_ref.shape[1]
    reach = taps // 2
    moved, core = scalar_ref[0], scalar_ref[1]
    flag_ref[...] = jnp.full((ROWS, LANES), scalar_ref[2], jnp.int32)
    wide_ref[2 * reach : 2 * reach + zb] = estimate_ref[...]
    odd = lax.rem(lax.axis_index("bulk"), 2)
    for side, (near_ref, far_side) in enumerate(((near1_ref, 1 - odd), (near2_ref, odd))):
        first = far_side * (2 * reach + zb)
        wide_ref[pl.ds(first + reach * core, reach)] = near_ref[...]
        wide_ref[pl.ds(first + reach * (1 - core), reach)] = other_ref[side]
    rest = planes - zb - 2 * reach
    wide_ref[4 * reach + zb :] = jnp.zeros((rest, ny, nx), jnp.float32)

    rows_high, rows_low = rows_matrix(taps_ref, 1, ny, moved, False)
    lanes = lanes_matrix(taps_ref, 2, nx, False)
    group = WIDE // ny

    tile = (ROWS, LANES)
    splats = [jnp.full(tile, taps_ref[0, t], jnp.float32) for t in range(taps)]
    for t in range(taps):
        splat_ref[taps - 1 - t] = splats[t]
    for base in range(0, planes, group):
        values = blur_planes(wide_ref, splats, base, group)
        values = blur_lanes(lanes, blur_rows(rows_high, rows_low, values))
        inverse_ref[base : base + group] = (1.0 / values).reshape(group, ny, nx)
    high, low = rows_matrix(taps_ref, 1, ny, moved, True)
    rows_high_ref[...] = high
    rows_low_ref[...] = low
    lanes_ref[...] = lanes_matrix(taps_ref, 2, nx, True)
    for plane in range(zb):
        weight = jnp.where(visible_ref[plane] == 1, 1.0, 0.0)
        weight_ref[plane] = jnp.full((ROWS, LANES), weight, jnp.float32)


def neighbours(count):
    return [k for k in range(1, count) if k & (k + 1) == 0]


def beside_in(b, k):
    low = jnp.bitwise_and(b, k)
    return jnp.logical_or(low == k // 2, low == k // 2 + 1)


def ratio_kernel(zb, ny, nx, count, flag_ref, weight_ref, splat_ref, image_ref, inverse_ref,
                 rows_high_ref, rows_low_ref, lanes_ref, *refs):
    blocks, (send_ref, keep_ref, ratio_ref, placed_ref) = refs[:count], refs[count:]
    reach = splat_ref.shape[0] // 2
    b = lax.axis_index("bulk")
    groups = ny // ROWS
    planes = zb + 2 * reach
    turned = flag_ref[...] == 1
    for k in range(count):
        placed_ref[jnp.bitwise_xor(b, k)] = blocks[k][: planes * ROWS]
    odd = lax.rem(b, 2) == 1
    spot = lax.broadcasted_iota(jnp.int32, (ROWS, LANES), 1) // zb
    outside = {0: b > 0, reach + zb: b < count - 1}
    for tile in range(nx // LANES):
        lanes = slice(tile * LANES, (tile + 1) * LANES)
        for plane in range(planes):
            place = slice(plane * ROWS, (plane + 1) * ROWS)
            pieces = [placed_ref[groups * tile + c, place] for c in range(groups)]
            for g in range(groups):
                rows = slice(g * ROWS, (g + 1) * ROWS)
                value = None
                for c in range(groups):
                    shift = (zb * (c - g)) % LANES
                    moved = pltpu.roll(pieces[c], shift, 1) if shift else pieces[c]
                    value = moved if value is None else jnp.where(spot == c, moved, value)
                if reach <= plane < reach + zb:
                    start = (plane - reach) * ny + g * ROWS
                    straight = image_ref[start : start + ROWS, lanes]
                else:
                    side = 0 if plane < reach else reach + zb
                    start = (tile * reach + plane - side) * ny + g * ROWS
                    beside = [blocks[k][start : start + ROWS] for k in neighbours(count)]
                    far = beside[1]
                    for k, value2 in zip(neighbours(count)[2:], beside[2:]):
                        far = jnp.where(beside_in(b, k), value2, far)
                    straight = jnp.where(odd == (side == 0), beside[0], far)
                    straight = jnp.where(outside[side], straight, 0.0)
                value = jnp.where(turned, value, straight)
                ratio_ref[plane, rows, lanes] = value * inverse_ref[plane, rows, lanes]

    adjoint_kernel(0, weight_ref, splat_ref, ratio_ref, rows_high_ref, rows_low_ref, lanes_ref,
                   send_ref, keep_ref)


def adjoint_kernel(part, weight_ref, splat_ref, ratio_ref, rows_high_ref, rows_low_ref, lanes_ref,
                   send_ref, keep_ref):
    core = lax.rem(lax.axis_index("view"), 2)
    splats = [splat_ref[t] for t in range(splat_ref.shape[0])]
    rows_high, rows_low, lanes_pair = rows_high_ref[...], rows_low_ref[...], lanes_ref[...]
    size, ny, nx = send_ref.shape
    group = WIDE // ny
    for out_ref, side in ((send_ref, 1 - core), (keep_ref, core)):
        for first in range(0, size, group):
            base = (2 * part + side) * size + first
            values = blur_planes(ratio_ref, splats, base, group)
            values = blur_lanes(lanes_pair, blur_rows(rows_high, rows_low, values))
            logs = jnp.log(values).reshape(group, ny // ROWS, ROWS, nx)
            for plane in range(group):
                weight = weight_ref[base + plane]
                for tile in range(nx // LANES):
                    lanes = slice(tile * LANES, (tile + 1) * LANES)
                    for row in range(ny // ROWS):
                        out_ref[first + plane, row * ROWS : (row + 1) * ROWS, lanes] = (
                            weight * logs[plane, row, :, lanes]
                        )


def shards(estimate, image, psf, perm, shift, visible):
    zb, ny, nx = estimate.shape
    views, count = lax.axis_size("view"), lax.axis_size("bulk")
    view = lax.axis_index("view")
    core, chip = view % 2, view // 2
    taps = psf.shape[2]
    reach = taps // 2
    kernels = psf[0] / jnp.sum(psf[0], axis=1, keepdims=True)
    stack = image[0].reshape(zb * ny, nx)

    tiles = nx // LANES
    halo = reach * ny
    extent = (zb + 2 * reach) * ROWS
    packed = list(pl.pallas_call(
        functools.partial(pack_kernel, zb, ny, nx, count),
        out_shape=[struct((extent, LANES))] * count,
        in_specs=[VMEM],
        out_specs=[VMEM] * count,
        scratch_shapes=[
            pltpu.VMEM(((nx + 2 * reach) * ROWS, LANES), jnp.float32),
            pltpu.VMEM((zb * ny, LANES), jnp.float32),
        ],
        compiler_params=PARAMS,
    )(stack))
    late_perm, _ = lax.optimization_barrier((perm, packed[1]))
    length = max(extent, halo * tiles)

    bulk = lax.axis_index("bulk")
    even = bulk % 2 == 0

    def beside(first):
        planes = lax.dynamic_slice_in_dim(stack, first, halo, 0).reshape(halo, tiles, LANES)
        planes = jnp.swapaxes(planes, 0, 1).reshape(halo * tiles, LANES)
        return jnp.pad(planes, ((0, length - halo * tiles), (0, 0)))

    for k in neighbours(count):
        block = jnp.pad(packed[k], ((0, length - extent), (0, 0)))
        above = even if k == 1 else jnp.logical_not(even)
        start = jnp.where(above, (zb - reach) * ny, 0)
        packed[k] = jnp.where(late_perm[0] == 1, block, beside(start))
    blocks = {0: packed[0]}
    for k in range(count - 1, 0, -1):
        blocks[k] = lax.ppermute(packed[k], "bulk", [(i, i ^ k) for i in range(count)])
    blocks = [blocks[k] for k in range(count)]

    joined_taps = jnp.where(late_perm[0] == 1, kernels[::-1], kernels)
    scalars = jnp.stack([shift[0], core.astype(jnp.int32), late_perm[0]])

    swap = [(i, i ^ 1) for i in range(views)]
    later, *_ = lax.optimization_barrier((estimate, packed[count - 1]))
    near = []
    for k in neighbours(count):
        above = even if k == 1 else jnp.logical_not(even)
        start = jnp.where(above, zb - 2 * reach, 0) + reach * core
        pairs = [(i, i ^ k) for i in range(count) if abs(i - (i ^ k)) == 1]
        near.append(
            lax.ppermute(lax.dynamic_slice_in_dim(later, start, reach, 0), "bulk", pairs)
        )
    near = [near[0], sum(near[2:], near[1])]
    other = lax.ppermute(jnp.stack(near), "view", swap)

    group = WIDE // ny
    planes = -(-(zb + 2 * reach) // group) * group
    inverse, rows_high, rows_low, lanes_pair, weight, splats, flags = pl.pallas_call(
        functools.partial(forward_kernel, zb, ny, nx, planes),
        out_shape=[
            struct((planes, ny, nx)),
            struct((WIDE, WIDE), jnp.bfloat16),
            struct((WIDE, WIDE), jnp.bfloat16),
            struct((2 * nx, 2 * nx), jnp.bfloat16),
            struct((zb, ROWS, LANES)),
            struct((taps, ROWS, LANES)),
            struct((ROWS, LANES), jnp.int32),
        ],
        in_specs=[SMEM] * 3 + [VMEM] * 4,
        out_specs=[VMEM] * 7,
        scratch_shapes=[pltpu.VMEM((planes + 2 * reach, ny, nx), jnp.float32)],
        compiler_params=PARAMS,
    )(scalars, joined_taps, visible[0], estimate, *near, other)

    parts = 2
    size = zb // (2 * parts)
    matrices = (rows_high, rows_low, lanes_pair)
    first = pl.pallas_call(
        functools.partial(ratio_kernel, zb, ny, nx, count),
        out_shape=[struct((size, ny, nx))] * 2 + [struct((zb + 2 * reach, ny, nx))],
        in_specs=[VMEM] * (8 + count),
        out_specs=[VMEM] * 3,
        scratch_shapes=[
            pltpu.VMEM((count, (zb + 2 * reach) * ROWS, LANES), jnp.float32),
        ],
        compiler_params=PARAMS,
    )(flags, weight, splats, stack, inverse, *matrices, *blocks)
    total = [first[1] + lax.ppermute(first[0], "view", swap)]
    for part in range(1, parts):
        held, total[-1] = lax.optimization_barrier((weight, total[-1]))
        send, keep = pl.pallas_call(
            functools.partial(adjoint_kernel, part),
            out_shape=[struct((size, ny, nx))] * 2,
            in_specs=[VMEM] * 6,
            out_specs=[VMEM] * 2,
            cost_estimate=COST,
            compiler_params=PARAMS,
        )(held, splats, first[2], *matrices)
        total.append(keep + lax.ppermute(send, "view", swap))

    bits = (views // 2).bit_length() - 1
    result = []
    for part in range(parts):
        for step in range(bits):
            flips = [2 << step, 2 << ((step + bits - 1) % bits)]
            total[part] = total[part] + lax.ppermute(
                total[part], "view", [(i, i ^ flips[i % 2]) for i in range(views)]
            )
        own = lax.dynamic_slice_in_dim(estimate, (2 * part + core) * size, size, 0)
        own = own * jnp.exp(total[part] / float(views))
        their = lax.ppermute(own, "view", swap)
        result += [jnp.where(core == 0, own, their), jnp.where(core == 0, their, own)]
    return jnp.concatenate(result, axis=0)


def solution(mesh):
    placed = (
        P("bulk", None, None),
        P("view", "bulk", None, None),
        P("view", None, None),
        P("view"),
        P("view"),
        P("view", "bulk"),
    )
    return jax.shard_map(
        shards, mesh=mesh, in_specs=placed, out_specs=P("bulk", None, None), check_vma=False
    )
```

time: 215 us -> 43.9 us (0.20)
  other arithmetic: 72.6 us -> 1.4 us
  waiting for transfers between devices: 85.9 us -> 16.9 us
  local copies, waits for them, and re-layouts: 22.8 us -> 1.13 us
  between operations: 15 us -> 1.53 us
  Pallas kernels: 0 us -> 5.17 us
    psum x1 -> x0, waiting for transfers between devices: 54 us -> none  [shards(): log_total = lax.psum(log_terms, 'view')]
    add x5 -> x4, other arithmetic: 52 us -> 0.08 us  [the longest x2 0.04 us: shards(): total[part]]
    all_to_all x2 -> x0, waiting for transfers between devices: 22.7 us -> none  [the longest x1 12.2 us: shards(): lax.all_to_all(estimate, 'bulk', split_axis=2, concat_axis=0, tiled=True)]
    div x1 -> x0, other arithmetic: 11.4 us -> none  [shards(): correction = adjoint(stack / blurred, kernels[:, ::-1])]
    ppermute x4 -> x14, starting transfers between devices: 7.29 us -> 17.5 us  [the longest x3 9.96 us: shards(): lax.ppermute(packed[k], 'bulk', [(i, i ^ k) for i in range(count)])]
    all_to_all x2 -> x0, starting transfers between devices: 9.79 us -> none  [the longest x1 6.32 us: shards(): lax.all_to_all(estimate, 'bulk', split_axis=2, concat_axis=0, tiled=True)]
    all_to_all x5 -> x0, local copies, waits for them, and re-layouts: 9.12 us -> none  [the longest x3 4.83 us: shards(): lax.all_to_all(estimate, 'bulk', split_axis=2, concat_axis=0, tiled=True)]
    ppermute x4 -> x14, waiting for transfers between devices: 9.16 us -> 16.9 us  [the longest x3 6.54 us: shards(): lax.ppermute(packed[k], 'bulk', [(i, i ^ k) for i in range(count)])]
  transfers between devices with their start and end apart: 7 -> 14, of which waited for: 6 -> 10; matrix products, arithmetic and copies ran while one was open for 1% -> 1% of each run, Pallas kernels for 0% -> 6%
where the time goes in v3:
time: 43.9 us; the launch traced here: 43.7 us
  starting transfers between devices  17.5 us (40%)
  waiting for transfers between devices  16.9 us (38%)
  Pallas kernels  5.17 us (12%)
  between operations  1.53 us (3%)
  other arithmetic  1.4 us (3%)
  local copies, waits for them, and re-layouts  1.13 us (3%)
    ppermute x3, starting transfers between devices, shards(): lax.ppermute(packed[k], 'bulk', [(i, i ^ k) for i in range(count)])  9.96 us
    ppermute x3, waiting for transfers between devices, shards(): lax.ppermute(packed[k], 'bulk', [(i, i ^ k) for i in range(count)])  6.54 us
    ppermute x4, starting transfers between devices, shards(): lax.ppermute(total[part], 'view', [(i, i ^ flips[i % 2]) for i in range(v...  5.89 us
    ppermute x4, waiting for transfers between devices, shards(): lax.ppermute(total[part], 'view', [(i, i ^ flips[i % 2]) for i in range(v...  5.67 us
    pallas_call x1, Pallas kernels, shards(): pl.pallas_call(functools.partial(forward_kernel, zb, ny, nx, planes), out...  2.71 us
    ppermute x1, waiting for transfers between devices, shards(): total = [first[1] + lax.ppermute(first[0], 'view', swap)]  1.33 us
    ppermute x1, waiting for transfers between devices, shards(): other = lax.ppermute(jnp.stack(near), 'view', swap)  1.3 us
    pallas_call x1, Pallas kernels, shards(): pl.pallas_call(functools.partial(ratio_kernel, zb, ny, nx, count), out_sh...  1.25 us
  transfers between devices with their start and end apart: 14, of which 10 were waited for; matrix products, arithmetic and copies ran while one was open for 1% of the time, Pallas kernels for 6%

profile of v3, /device:TPU:0, one launch (start us, length us, event | category | flops | bytes accessed | tf_op | source)
XLA Modules:
  0.0 43.7 jit_solution(3554304339111733511)
XLA Ops:
  0.0 1.0 %copy-done = f32[1,32,32,128]{3,2,1,0:T(8,128)S(1)} copy-done((f32[1,32,32,128]{3,2,1,0:T(8,128)S(1)}, f32[1,32,32,128]{3,2,1,0:T(8,128)}, u32[]{:S(2)}) %copy-start) | copy-done | bytes 524312
  1.0 0.4 %shard_map.64 = (f32[368,128]{1,0:T(8,128)S(1)}, f32[368,128]{1,0:T(8,128)S(1)}, f32[368,128]{1,0:T(8,128)S(1)}, f32[368,128]{1,0:T(8,128)S(1)}) custom-call(f32[1024,128]{1,0:T(8,128)S(1)} %bitcast.10), custom_call_target="tpu_custom_call" | custom-call | tf_op jit(solution)/shard_map/pallas_call | solution.py:250
  2.3 5.1 %collective-permute-start.5 = (f32[368,128]{1,0:T(8,128)S(1)}, f32[368,128]{1,0:T(8,128)S(1)}, u32[]{:S(2)}, u32[]{:S(2)}) collective-permute-start(f32[368,128]{1,0:T(8,128)S(1)} %pad_select_fusion.1), channel_id=1, source_target_pairs={{0,3},{1,2},{2,1},{3,0},{4,7},{5,6},{6,5},{7,4},{8,11},{9,10},{10,... | collective-permute-start | bytes 565256 | tf_op jit(solution)/shard_map/ppermute | solution.py:279
  7.5 0.7 %collective-permute-start.1 = (f32[7,32,128]{2,1,0:T(8,128)S(1)}, f32[7,32,128]{2,1,0:T(8,128)S(1)}, u32[]{:S(2)}, u32[]{:S(2)}) collective-permute-start(f32[7,32,128]{2,1,0:T(8,128)S(1)} %get-tuple-element.49), channel_id=1, source_target_pairs={{1,2},{2,1},{5,6},{6,5},{9,10},{10,9},{13,14},{14,13},{17,18},{18,... | collective-permute-start | bytes 344072 | tf_op jit(solution)/shard_map/ppermute | solution.py:293
  8.2 3.3 %collective-permute-start.3 = (f32[368,128]{1,0:T(8,128)S(1)}, f32[368,128]{1,0:T(8,128)S(1)}, u32[]{:S(2)}, u32[]{:S(2)}) collective-permute-start(f32[368,128]{1,0:T(8,128)S(1)} %pad_select_fusion), channel_id=1, source_target_pairs={{0,1},{1,0},{2,3},{3,2},{4,5},{5,4},{6,7},{7,6},{8,9},{9,8},{10,11... | collective-permute-start | bytes 565256 | tf_op jit(solution)/shard_map/ppermute | solution.py:279
  11.5 1.5 %collective-permute-start.4 = (f32[368,128]{1,0:T(8,128)S(1)}, f32[368,128]{1,0:T(8,128)S(1)}, u32[]{:S(2)}, u32[]{:S(2)}) collective-permute-start(f32[368,128]{1,0:T(8,128)S(1)} %get-tuple-element.37), channel_id=1, source_target_pairs={{0,2},{1,3},{2,0},{3,1},{4,6},{5,7},{6,4},{7,5},{8,10},{9,11},{10,... | collective-permute-start | bytes 565256 | tf_op jit(solution)/shard_map/ppermute | solution.py:279
  13.9 1.1 %collective-permute-done.near1_ref = f32[7,32,128]{2,1,0:T(8,128)S(1)} collective-permute-done((f32[7,32,128]{2,1,0:T(8,128)S(1)}, f32[7,32,128]{2,1,0:T(8,128)S(1)}, u32[]{:S(2)}, u32[]{:S(2)}) %collective-permute-start) | collective-permute-done | bytes 114720 | tf_op jit(solution)/shard_map/ppermute | solution.py:293
  15.3 1.3 %collective-permute-done.2.other_ref = f32[2,7,32,128]{3,2,1,0:T(8,128)S(1)} collective-permute-done((f32[2,7,32,128]{3,2,1,0:T(8,128)S(1)}, f32[2,7,32,128]{3,2,1,0:T(8,128)S(1)}, u32[]{:S(2)}, u32[]{:S(2)}) %collective-permute-start.2) | collective-permute-done | bytes 229408 | tf_op jit(solution)/shard_map/ppermute | solution.py:296
  16.6 2.7 %shard_map.65 = (f32[48,32,128]{2,1,0:T(8,128)S(1)}, bf16[256,256]{1,0:T(8,128)(2,1)S(1)}, bf16[256,256]{1,0:T(8,128)(2,1)S(1)}, bf16[256,256]{1,0:T(8,128)(2,1)...) custom-call(s32[3]{0:T(128)S(1)} %pad_add_fusion.scalar_ref, ...), custom_call_target="tpu_custom_call" | custom-call | tf_op jit(solution)/shard_map/pallas_call | solution.py:300
  19.5 6.3 %collective-permute-done.4.refs_2_ = f32[368,128]{1,0:T(8,128)S(1)} collective-permute-done((f32[368,128]{1,0:T(8,128)S(1)}, f32[368,128]{1,0:T(8,128)S(1)}, u32[]{:S(2)}, u32[]{:S(2)}) %collective-permute-start.4) | collective-permute-done | bytes 188448 | tf_op jit(solution)/shard_map/ppermute | solution.py:279
  25.8 1.3 %shard_map.66 = (f32[8,32,128]{2,1,0:T(8,128)S(1)}, f32[8,32,128]{2,1,0:T(8,128)S(1)}, f32[46,32,128]{2,1,0:T(8,128)S(1)}) custom-call(s32[8,128]{1,0:T(8,128)S(1)} %get-tuple-element.30.flag_ref, f32[32,8,128]{2,1,0:T(8,128)S(1)} %get-tuple-element.41.weight_ref, f32[15,8,128]{2,1,0:T(8,128)S(1)} %get-tuple-element.31.splat_ref, f32[1024,128]{1,0:T(8,128)S(1)} %bitcast.12, ...), custom_call_target="tpu_custom_call" | custom-call | tf_op jit(solution)/shard_map/pallas_call | solution.py:320
  27.2 1.3 %collective-permute-done.6 = f32[8,32,128]{2,1,0:T(8,128)S(1)} collective-permute-done((f32[8,32,128]{2,1,0:T(8,128)S(1)}, f32[8,32,128]{2,1,0:T(8,128)S(1)}, u32[]{:S(2)}, u32[]{:S(2)}) %collective-permute-start.6) | collective-permute-done | bytes 131104 | tf_op jit(solution)/shard_map/ppermute | solution.py:330
  28.5 0.8 %shard_map.67 = (f32[8,32,128]{2,1,0:T(8,128)S(1)}, f32[8,32,128]{2,1,0:T(8,128)S(1)}) custom-call(f32[32,8,128]{2,1,0:T(8,128)S(1)} %get-tuple-element.41.weight_ref, f32[15,8,128]{2,1,0:T(8,128)S(1)} %get-tuple-element.31.splat_ref, f32[46,32,128]{2,1,0:T(8,128)S(1)} %get-tuple-element.42.ratio_ref, bf16[256,256]{1,0:T(8,128)(2,1)S(1)} %get-tuple-element.33.rows_high_ref, ...), custom_call_target="tpu_custom_call" | custom-call | flops 536870912 | bytes 2097152 | tf_op jit(solution)/shard_map/pallas_call | solution.py:333
  29.3 0.2 collective-permute-start.10
  29.5 1.5 %collective-permute-start.7 = (f32[8,32,128]{2,1,0:T(8,128)S(1)}, f32[8,32,128]{2,1,0:T(8,128)S(1)}, u32[]{:S(2)}, u32[]{:S(2)}) collective-permute-start(f32[8,32,128]{2,1,0:T(8,128)S(1)} %add.59), channel_id=1, source_target_pairs={{0,8},{4,20},{8,0},{12,28},{16,24},{20,4},{24,16},{28,12},{1,9},{5... | collective-permute-start | bytes 393224 | tf_op jit(solution)/shard_map/ppermute | solution.py:348
  31.0 1.3 %collective-permute-start.11 = (f32[8,32,128]{2,1,0:T(8,128)S(1)}, f32[8,32,128]{2,1,0:T(8,128)S(1)}, u32[]{:S(2)}, u32[]{:S(2)}) collective-permute-start(f32[8,32,128]{2,1,0:T(8,128)S(1)} %add.64), channel_id=1, source_target_pairs={{0,8},{4,20},{8,0},{12,28},{16,24},{20,4},{24,16},{28,12},{1,9},{5... | collective-permute-start | bytes 393224 | tf_op jit(solution)/shard_map/ppermute | solution.py:348
  32.3 2.2 %collective-permute-done.7 = f32[8,32,128]{2,1,0:T(8,128)S(1)} collective-permute-done((f32[8,32,128]{2,1,0:T(8,128)S(1)}, f32[8,32,128]{2,1,0:T(8,128)S(1)}, u32[]{:S(2)}, u32[]{:S(2)}) %collective-permute-start.7) | collective-permute-done | bytes 131104 | tf_op jit(solution)/shard_map/ppermute | solution.py:348
  34.5 1.6 %collective-permute-start.8 = (f32[8,32,128]{2,1,0:T(8,128)S(1)}, f32[8,32,128]{2,1,0:T(8,128)S(1)}, u32[]{:S(2)}, u32[]{:S(2)}) collective-permute-start(f32[8,32,128]{2,1,0:T(8,128)S(1)} %add.60), channel_id=1, source_target_pairs={{0,16},{4,12},{8,24},{12,4},{16,0},{20,28},{24,8},{28,20},{1,17},{... | collective-permute-start | bytes 393224 | tf_op jit(solution)/shard_map/ppermute | solution.py:348
  36.1 1.6 %collective-permute-start.12 = (f32[8,32,128]{2,1,0:T(8,128)S(1)}, f32[8,32,128]{2,1,0:T(8,128)S(1)}, u32[]{:S(2)}, u32[]{:S(2)}) collective-permute-start(f32[8,32,128]{2,1,0:T(8,128)S(1)} %add.65), channel_id=1, source_target_pairs={{0,16},{4,12},{8,24},{12,4},{16,0},{20,28},{24,8},{28,20},{1,17},{... | collective-permute-start | bytes 393224 | tf_op jit(solution)/shard_map/ppermute | solution.py:348
  37.7 1.9 %collective-permute-done.8 = f32[8,32,128]{2,1,0:T(8,128)S(1)} collective-permute-done((f32[8,32,128]{2,1,0:T(8,128)S(1)}, f32[8,32,128]{2,1,0:T(8,128)S(1)}, u32[]{:S(2)}, u32[]{:S(2)}) %collective-permute-start.8) | collective-permute-done | bytes 131104 | tf_op jit(solution)/shard_map/ppermute | solution.py:348
  39.5 1.6 %collective-permute-done.12 = f32[8,32,128]{2,1,0:T(8,128)S(1)} collective-permute-done((f32[8,32,128]{2,1,0:T(8,128)S(1)}, f32[8,32,128]{2,1,0:T(8,128)S(1)}, u32[]{:S(2)}, u32[]{:S(2)}) %collective-permute-start.12) | collective-permute-done | bytes 131104 | tf_op jit(solution)/shard_map/ppermute | solution.py:348
  41.3 0.5 %collective-permute-start.13 = (f32[8,32,128]{2,1,0:T(8,128)S(1)}, f32[8,32,128]{2,1,0:T(8,128)S(1)}, u32[]{:S(2)}, u32[]{:S(2)}) collective-permute-start(f32[8,32,128]{2,1,0:T(8,128)S(1)} %get-tuple-element.46), channel_id=1, source_target_pairs={{0,4},{4,0},{8,12},{12,8},{16,20},{20,16},{24,28},{28,24},{1,5},{5... | collective-permute-start | bytes 393224 | tf_op jit(solution)/shard_map/ppermute | solution.py:353
  41.8 0.8 %collective-permute-done.9 = f32[8,32,128]{2,1,0:T(8,128)S(1)} collective-permute-done((f32[8,32,128]{2,1,0:T(8,128)S(1)}, f32[8,32,128]{2,1,0:T(8,128)S(1)}, u32[]{:S(2)}, u32[]{:S(2)}) %collective-permute-start.9) | collective-permute-done | bytes 131104 | tf_op jit(solution)/shard_map/ppermute | solution.py:353
  42.8 0.8 %pad_maximum_fusion = f32[32,32,128]{2,1,0:T(8,128)} fusion(f32[8,32,128]{2,1,0:T(8,128)S(1)} %get-tuple-element.54, f32[8,32,128]{2,1,0:T(8,128)S(1)} %get-tuple-element.53, f32[8,32,128]{2,1,0:T(8,128)S(1)} %get-tuple-element.52, f32[8,32,128]{2,1,0:T(8,128)S(1)} %get-tuple-element.51), kind=kLoop, calls=%fused_computation | loop fusion | flops 393216 | bytes 1048576 | tf_op jit(solution)/shard_map/concatenate | solution.py:355
  (36 shorter events, 1.3 us)
Async XLA Ops:
  0.0 1.0 %copy-start = (f32[1,32,32,128]{3,2,1,0:T(8,128)S(1)}, f32[1,32,32,128]{3,2,1,0:T(8,128)}, u32[]{:S(2)}) copy-start(f32[1,32,32,128]{3,2,1,0:T(8,128)} %param.7) | copy-start | bytes 1572868
  1.5 5.9 %copy-start.2 = (f32[32,32,128]{2,1,0:T(8,128)S(1)}, f32[32,32,128]{2,1,0:T(8,128)}, u32[]{:S(2)}) copy-start(f32[32,32,128]{2,1,0:T(8,128)} %estimate_ref.1) | copy-start | bytes 1572868
  2.3 17.2 %collective-permute-start.5 = (f32[368,128]{1,0:T(8,128)S(1)}, f32[368,128]{1,0:T(8,128)S(1)}, u32[]{:S(2)}, u32[]{:S(2)}) collective-permute-start(f32[368,128]{1,0:T(8,128)S(1)} %pad_select_fusion.1), channel_id=1, source_target_pairs={{0,3},{1,2},{2,1},{3,0},{4,7},{5,6},{6,5},{7,4},{8,11},{9,10},{10,... | collective-permute-start | bytes 565256 | tf_op jit(solution)/shard_map/ppermute | solution.py:279
  7.4 7.6 %collective-permute-start = (f32[7,32,128]{2,1,0:T(8,128)S(1)}, f32[7,32,128]{2,1,0:T(8,128)S(1)}, u32[]{:S(2)}, u32[]{:S(2)}) collective-permute-start(f32[7,32,128]{2,1,0:T(8,128)S(1)} %get-tuple-element.50), channel_id=1, source_target_pairs={{0,1},{1,0},{2,3},{3,2},{4,5},{5,4},{6,7},{7,6},{8,9},{9,8},{10,11... | collective-permute-start | bytes 344072 | tf_op jit(solution)/shard_map/ppermute | solution.py:293
  7.5 7.5 %collective-permute-start.1 = (f32[7,32,128]{2,1,0:T(8,128)S(1)}, f32[7,32,128]{2,1,0:T(8,128)S(1)}, u32[]{:S(2)}, u32[]{:S(2)}) collective-permute-start(f32[7,32,128]{2,1,0:T(8,128)S(1)} %get-tuple-element.49), channel_id=1, source_target_pairs={{1,2},{2,1},{5,6},{6,5},{9,10},{10,9},{13,14},{14,13},{17,18},{18,... | collective-permute-start | bytes 344072 | tf_op jit(solution)/shard_map/ppermute | solution.py:293
  8.2 5.5 %copy-start.4 = (f32[1,3,15]{2,0,1:T(1,128)S(1)}, f32[1,3,15]{2,0,1:T(1,128)}, u32[]{:S(2)}) copy-start(f32[1,3,15]{2,0,1:T(1,128)} %param.8) | copy-start | bytes 544
  8.2 11.3 %collective-permute-start.3 = (f32[368,128]{1,0:T(8,128)S(1)}, f32[368,128]{1,0:T(8,128)S(1)}, u32[]{:S(2)}, u32[]{:S(2)}) collective-permute-start(f32[368,128]{1,0:T(8,128)S(1)} %pad_select_fusion), channel_id=1, source_target_pairs={{0,1},{1,0},{2,3},{3,2},{4,5},{5,4},{6,7},{7,6},{8,9},{9,8},{10,11... | collective-permute-start | bytes 565256 | tf_op jit(solution)/shard_map/ppermute | solution.py:279
  11.5 14.3 %collective-permute-start.4 = (f32[368,128]{1,0:T(8,128)S(1)}, f32[368,128]{1,0:T(8,128)S(1)}, u32[]{:S(2)}, u32[]{:S(2)}) collective-permute-start(f32[368,128]{1,0:T(8,128)S(1)} %get-tuple-element.37), channel_id=1, source_target_pairs={{0,2},{1,3},{2,0},{3,1},{4,6},{5,7},{6,4},{7,5},{8,10},{9,11},{10,... | collective-permute-start | bytes 565256 | tf_op jit(solution)/shard_map/ppermute | solution.py:279
  15.0 1.6 %copy-start.3 = (s32[1,32]{1,0:T(1,128)S(1)}, s32[1,32]{1,0:T(1,128)}, u32[]{:S(2)}) copy-start(s32[1,32]{1,0:T(1,128)} %param.11) | copy-start | bytes 388
  15.0 10.8 %copy-start.1 = (f32[1,32,32,128]{3,2,1,0:T(8,128)S(1)}, f32[1,32,32,128]{3,2,1,0:T(8,128)}, u32[]{:S(2)}) copy-start(f32[1,32,32,128]{3,2,1,0:T(8,128)} %param.7) | copy-start | bytes 1572868
  15.0 1.6 %collective-permute-start.2 = (f32[2,7,32,128]{3,2,1,0:T(8,128)S(1)}, f32[2,7,32,128]{3,2,1,0:T(8,128)S(1)}, u32[]{:S(2)}, u32[]{:S(2)}) collective-permute-start(f32[2,7,32,128]{3,2,1,0:T(8,128)S(1)} %pad_maximum_fusion.1), channel_id=1, source_target_pairs={{0,4},{4,0},{8,12},{12,8},{16,20},{20,16},{24,28},{28,24},{1,5},{5... | collective-permute-start | bytes 688136 | tf_op jit(solution)/shard_map/ppermute | solution.py:296
  27.1 1.4 %collective-permute-start.6 = (f32[8,32,128]{2,1,0:T(8,128)S(1)}, f32[8,32,128]{2,1,0:T(8,128)S(1)}, u32[]{:S(2)}, u32[]{:S(2)}) collective-permute-start(f32[8,32,128]{2,1,0:T(8,128)S(1)} %get-tuple-element.39), channel_id=1, source_target_pairs={{0,4},{4,0},{8,12},{12,8},{16,20},{20,16},{24,28},{28,24},{1,5},{5... | collective-permute-start | bytes 393224 | tf_op jit(solution)/shard_map/ppermute | solution.py:330
  29.3 1.7 %collective-permute-start.10 = (f32[8,32,128]{2,1,0:T(8,128)S(1)}, f32[8,32,128]{2,1,0:T(8,128)S(1)}, u32[]{:S(2)}, u32[]{:S(2)}) collective-permute-start(f32[8,32,128]{2,1,0:T(8,128)S(1)} %get-tuple-element.44), channel_id=1, source_target_pairs={{0,4},{4,0},{8,12},{12,8},{16,20},{20,16},{24,28},{28,24},{1,5},{5... | collective-permute-start | bytes 393224 | tf_op jit(solution)/shard_map/ppermute | solution.py:341
  29.5 5.0 %collective-permute-start.7 = (f32[8,32,128]{2,1,0:T(8,128)S(1)}, f32[8,32,128]{2,1,0:T(8,128)S(1)}, u32[]{:S(2)}, u32[]{:S(2)}) collective-permute-start(f32[8,32,128]{2,1,0:T(8,128)S(1)} %add.59), channel_id=1, source_target_pairs={{0,8},{4,20},{8,0},{12,28},{16,24},{20,4},{24,16},{28,12},{1,9},{5... | collective-permute-start | bytes 393224 | tf_op jit(solution)/shard_map/ppermute | solution.py:348
  31.0 5.1 %collective-permute-start.11 = (f32[8,32,128]{2,1,0:T(8,128)S(1)}, f32[8,32,128]{2,1,0:T(8,128)S(1)}, u32[]{:S(2)}, u32[]{:S(2)}) collective-permute-start(f32[8,32,128]{2,1,0:T(8,128)S(1)} %add.64), channel_id=1, source_target_pairs={{0,8},{4,20},{8,0},{12,28},{16,24},{20,4},{24,16},{28,12},{1,9},{5... | collective-permute-start | bytes 393224 | tf_op jit(solution)/shard_map/ppermute | solution.py:348
  34.5 5.0 %collective-permute-start.8 = (f32[8,32,128]{2,1,0:T(8,128)S(1)}, f32[8,32,128]{2,1,0:T(8,128)S(1)}, u32[]{:S(2)}, u32[]{:S(2)}) collective-permute-start(f32[8,32,128]{2,1,0:T(8,128)S(1)} %add.60), channel_id=1, source_target_pairs={{0,16},{4,12},{8,24},{12,4},{16,0},{20,28},{24,8},{28,20},{1,17},{... | collective-permute-start | bytes 393224 | tf_op jit(solution)/shard_map/ppermute | solution.py:348
  36.1 5.0 %collective-permute-start.12 = (f32[8,32,128]{2,1,0:T(8,128)S(1)}, f32[8,32,128]{2,1,0:T(8,128)S(1)}, u32[]{:S(2)}, u32[]{:S(2)}) collective-permute-start(f32[8,32,128]{2,1,0:T(8,128)S(1)} %add.65), channel_id=1, source_target_pairs={{0,16},{4,12},{8,24},{12,4},{16,0},{20,28},{24,8},{28,20},{1,17},{... | collective-permute-start | bytes 393224 | tf_op jit(solution)/shard_map/ppermute | solution.py:348
  41.2 1.4 %collective-permute-start.9 = (f32[8,32,128]{2,1,0:T(8,128)S(1)}, f32[8,32,128]{2,1,0:T(8,128)S(1)}, u32[]{:S(2)}, u32[]{:S(2)}) collective-permute-start(f32[8,32,128]{2,1,0:T(8,128)S(1)} %get-tuple-element.45), channel_id=1, source_target_pairs={{0,4},{4,0},{8,12},{12,8},{16,20},{20,16},{24,28},{28,24},{1,5},{5... | collective-permute-start | bytes 393224 | tf_op jit(solution)/shard_map/ppermute | solution.py:353
  41.3 1.5 %collective-permute-start.13 = (f32[8,32,128]{2,1,0:T(8,128)S(1)}, f32[8,32,128]{2,1,0:T(8,128)S(1)}, u32[]{:S(2)}, u32[]{:S(2)}) collective-permute-start(f32[8,32,128]{2,1,0:T(8,128)S(1)} %get-tuple-element.46), channel_id=1, source_target_pairs={{0,4},{4,0},{8,12},{12,8},{16,20},{20,16},{24,28},{28,24},{1,5},{5... | collective-permute-start | bytes 393224 | tf_op jit(solution)/shard_map/ppermute | solution.py:353

commit v4 on v3

--- a/solution.py
+++ b/solution.py
@@ -120,8 +120,8 @@
         sends[k][...] = turned_ref[pl.ds(pl.multiple_of(start, ROWS), extent), :]
 
 
-def forward_kernel(zb, ny, nx, planes, scalar_ref, taps_ref, visible_ref, estimate_ref, near1_ref,
-                   near2_ref, other_ref, inverse_ref, rows_high_ref, rows_low_ref, lanes_ref,
+def forward_kernel(zb, ny, nx, planes, scalar_ref, taps_ref, visible_ref, estimate_ref, near_ref,
+                   other_ref, inverse_ref, rows_high_ref, rows_low_ref, lanes_ref,
                    weight_ref, splat_ref, flag_ref,
                    wide_ref):
     taps = taps_ref.shape[1]
@@ -129,11 +129,11 @@
     moved, core = scalar_ref[0], scalar_ref[1]
     flag_ref[...] = jnp.full((ROWS, LANES), scalar_ref[2], jnp.int32)
     wide_ref[2 * reach : 2 * reach + zb] = estimate_ref[...]
-    odd = lax.rem(lax.axis_index("bulk"), 2)
-    for side, (near_ref, far_side) in enumerate(((near1_ref, 1 - odd), (near2_ref, odd))):
-        first = far_side * (2 * reach + zb)
-        wide_ref[pl.ds(first + reach * core, reach)] = near_ref[...]
-        wide_ref[pl.ds(first + reach * (1 - core), reach)] = other_ref[side]
+    b, count = lax.axis_index("bulk"), lax.axis_size("bulk")
+    above = jnp.bitwise_xor(lax.rem(b, 2), 1 - core)
+    for block_ref, side in ((near_ref, above), (other_ref, 1 - above)):
+        inside = jnp.logical_and(b + 2 * side - 1 >= 0, b + 2 * side - 1 < count)
+        wide_ref[pl.ds((2 * reach + zb) * side, 2 * reach)] = jnp.where(inside, block_ref[...], 0.0)
     rest = planes - zb - 2 * reach
     wide_ref[4 * reach + zb :] = jnp.zeros((rest, ny, nx), jnp.float32)
 
@@ -274,6 +274,7 @@
         above = even if k == 1 else jnp.logical_not(even)
         start = jnp.where(above, (zb - reach) * ny, 0)
         packed[k] = jnp.where(late_perm[0] == 1, block, beside(start))
+    packed[count - 1], _ = lax.optimization_barrier((packed[count - 1], packed[2]))
     blocks = {0: packed[0]}
     for k in range(count - 1, 0, -1):
         blocks[k] = lax.ppermute(packed[k], "bulk", [(i, i ^ k) for i in range(count)])
@@ -283,17 +284,18 @@
     scalars = jnp.stack([shift[0], core.astype(jnp.int32), late_perm[0]])
 
     swap = [(i, i ^ 1) for i in range(views)]
-    later, *_ = lax.optimization_barrier((estimate, packed[count - 1]))
-    near = []
-    for k in neighbours(count):
-        above = even if k == 1 else jnp.logical_not(even)
-        start = jnp.where(above, zb - 2 * reach, 0) + reach * core
-        pairs = [(i, i ^ k) for i in range(count) if abs(i - (i ^ k)) == 1]
-        near.append(
-            lax.ppermute(lax.dynamic_slice_in_dim(later, start, reach, 0), "bulk", pairs)
-        )
-    near = [near[0], sum(near[2:], near[1])]
-    other = lax.ppermute(jnp.stack(near), "view", swap)
+    later = estimate
+    def beside_of(v, i):
+        there = i ^ 1 if v % 2 == 0 else ((i + 1) ^ 1) - 1
+        return there if 0 <= there < count else i
+
+    start = jnp.where(even == (core == 0), zb - 2 * reach, 0)
+    near = lax.ppermute(
+        lax.dynamic_slice_in_dim(later, start, 2 * reach, 0),
+        ("view", "bulk"),
+        [(v * count + i, v * count + beside_of(v, i)) for v in range(views) for i in range(count)],
+    )
+    other = lax.ppermute(near, "view", swap)
 
     group = WIDE // ny
     planes = -(-(zb + 2 * reach) // group) * group
@@ -308,11 +310,11 @@
             struct((taps, ROWS, LANES)),
             struct((ROWS, LANES), jnp.int32),
         ],
-        in_specs=[SMEM] * 3 + [VMEM] * 4,
+        in_specs=[SMEM] * 3 + [VMEM] * 3,
         out_specs=[VMEM] * 7,
         scratch_shapes=[pltpu.VMEM((planes + 2 * reach, ny, nx), jnp.float32)],
         compiler_params=PARAMS,
-    )(scalars, joined_taps, visible[0], estimate, *near, other)
+    )(scalars, joined_taps, visible[0], estimate, near, other)
 
     parts = 2
     size = zb // (2 * parts)
@@ -329,7 +331,7 @@
     )(flags, weight, splats, stack, inverse, *matrices, *blocks)
     total = [first[1] + lax.ppermute(first[0], "view", swap)]
     for part in range(1, parts):
-        held, total[-1] = lax.optimization_barrier((weight, total[-1]))
+        held = weight
         send, keep = pl.pallas_call(
             functools.partial(adjoint_kernel, part),
             out_shape=[struct((size, ny, nx))] * 2,
@@ -348,7 +350,8 @@
             total[part] = total[part] + lax.ppermute(
                 total[part], "view", [(i, i ^ flips[i % 2]) for i in range(views)]
             )
-        own = lax.dynamic_slice_in_dim(estimate, (2 * part + core) * size, size, 0)
+        held = estimate if not part else lax.optimization_barrier((estimate, own))[0]
+        own = lax.dynamic_slice_in_dim(held, (2 * part + core) * size, size, 0)
         own = own * jnp.exp(total[part] / float(views))
         their = lax.ppermute(own, "view", swap)
         result += [jnp.where(core == 0, own, their), jnp.where(core == 0, their, own)]

time: 43.9 us -> 41.2 us (0.938)
  starting transfers between devices: 17.5 us -> 15 us
  waiting for transfers between devices: 16.9 us -> 15.5 us
  local copies, waits for them, and re-layouts: 1.13 us -> 2.06 us
    ppermute x3, starting transfers between devices: 9.96 us -> 3.67 us  [shards(): lax.ppermute(packed[k], 'bulk', [(i, i ^ k) for i in range(count)])]
    ppermute x3 -> x2, starting transfers between devices: 0.81 us -> 4.93 us  [the longest x1 4.93 us: shards(): lax.ppermute(lax.dynamic_slice_in_dim(later, start, 2 * reach, 0), ('view...]
    ppermute x1, waiting for transfers between devices: 1.33 us -> 0.01 us  [shards(): total = [first[1] + lax.ppermute(first[0], 'view', swap)]]
    ppermute x3 -> x2, waiting for transfers between devices: 2.38 us -> 1.31 us  [the longest x1 1.31 us: shards(): other = lax.ppermute(near, 'view', swap)]
    dynamic_slice x1, local copies, waits for them, and re-layouts: 0.02 us -> 0.95 us  [shards(): lax.dynamic_slice_in_dim(later, start, 2 * reach, 0)]
    ppermute x3, waiting for transfers between devices: 6.54 us -> 7.02 us  [shards(): lax.ppermute(packed[k], 'bulk', [(i, i ^ k) for i in range(count)])]
  transfers between devices with their start and end apart: 14 -> 13, of which waited for: 10 -> 8; matrix products, arithmetic and copies ran while one was open for 1% -> 1% of each run, Pallas kernels for 6% -> 10%
where the time goes in v4:
time: 41.2 us; the launch traced here: 40.7 us
  waiting for transfers between devices  15.5 us (38%)
  starting transfers between devices  15 us (36%)
  Pallas kernels  5.21 us (13%)
  local copies, waits for them, and re-layouts  2.06 us (5%)
  between operations  1.49 us (4%)
  other arithmetic  1.39 us (3%)
    ppermute x3, waiting for transfers between devices, shards(): lax.ppermute(packed[k], 'bulk', [(i, i ^ k) for i in range(count)])  7.02 us
    ppermute x4, waiting for transfers between devices, shards(): lax.ppermute(total[part], 'view', [(i, i ^ flips[i % 2]) for i in range(v...  5.86 us
    ppermute x4, starting transfers between devices, shards(): lax.ppermute(total[part], 'view', [(i, i ^ flips[i % 2]) for i in range(v...  5.65 us
    ppermute x1, starting transfers between devices, shards(): lax.ppermute(lax.dynamic_slice_in_dim(later, start, 2 * reach, 0), ('view...  4.93 us
    ppermute x3, starting transfers between devices, shards(): lax.ppermute(packed[k], 'bulk', [(i, i ^ k) for i in range(count)])  3.67 us
    pallas_call x1, Pallas kernels, shards(): pl.pallas_call(functools.partial(forward_kernel, zb, ny, nx, planes), out...  2.75 us
    ppermute x1, waiting for transfers between devices, shards(): other = lax.ppermute(near, 'view', swap)  1.31 us
    ppermute x2, waiting for transfers between devices, shards(): their = lax.ppermute(own, 'view', swap)  1.3 us
  transfers between devices with their start and end apart: 13, of which 8 were waited for; matrix products, arithmetic and copies ran while one was open for 1% of the time, Pallas kernels for 10%

profile of v4, /device:TPU:0, one launch (start us, length us, event | category | flops | bytes accessed | tf_op | source)
XLA Modules:
  0.0 40.7 jit_solution(307516054694356522)
XLA Ops:
  0.0 1.0 %constant_dynamic-slice_fusion.2 = f32[14,32,128]{2,1,0:T(8,128)S(1)} fusion(f32[32,32,128]{2,1,0:T(8,128)} %estimate_ref.1, s32[]{:T(128)S(6)} %select_n.76), kind=kLoop, calls=%fused_computation.12 | loop fusion | bytes 458756 | tf_op jit(solution)/shard_map/dynamic_slice | solution.py:294
  1.0 4.9 %collective-permute-start = (f32[14,32,128]{2,1,0:T(8,128)S(1)}, f32[14,32,128]{2,1,0:T(8,128)S(1)}, u32[]{:S(2)}, u32[]{:S(2)}) collective-permute-start(f32[14,32,128]{2,1,0:T(8,128)S(1)} %constant_dynamic-slice_fusion.2), channel_id=1, source_target_pairs={{0,1},{1,0},{2,3},{3,2},{4,4},{5,6},{6,5},{7,7},{8,9},{9,8},{10,11... | collective-permute-start | bytes 688136 | tf_op jit(solution)/shard_map/ppermute | solution.py:293
  5.9 1.0 %copy-done = f32[1,32,32,128]{3,2,1,0:T(8,128)S(1)} copy-done((f32[1,32,32,128]{3,2,1,0:T(8,128)S(1)}, f32[1,32,32,128]{3,2,1,0:T(8,128)}, u32[]{:S(2)}) %copy-start) | copy-done | bytes 524312
  6.9 0.4 %shard_map.64 = (f32[368,128]{1,0:T(8,128)S(1)}, f32[368,128]{1,0:T(8,128)S(1)}, f32[368,128]{1,0:T(8,128)S(1)}, f32[368,128]{1,0:T(8,128)S(1)}) custom-call(f32[1024,128]{1,0:T(8,128)S(1)} %bitcast.8), custom_call_target="tpu_custom_call" | custom-call | tf_op jit(solution)/shard_map/pallas_call | solution.py:250
  7.4 2.7 %collective-permute-start.3 = (f32[368,128]{1,0:T(8,128)S(1)}, f32[368,128]{1,0:T(8,128)S(1)}, u32[]{:S(2)}, u32[]{:S(2)}) collective-permute-start(f32[368,128]{1,0:T(8,128)S(1)} %get-tuple-element.34), channel_id=1, source_target_pairs={{0,2},{1,3},{2,0},{3,1},{4,6},{5,7},{6,4},{7,5},{8,10},{9,11},{10,... | collective-permute-start | bytes 565256 | tf_op jit(solution)/shard_map/ppermute | solution.py:280
  10.9 0.9 %collective-permute-start.2 = (f32[368,128]{1,0:T(8,128)S(1)}, f32[368,128]{1,0:T(8,128)S(1)}, u32[]{:S(2)}, u32[]{:S(2)}) collective-permute-start(f32[368,128]{1,0:T(8,128)S(1)} %pad_select_fusion.1), channel_id=1, source_target_pairs={{0,1},{1,0},{2,3},{3,2},{4,5},{5,4},{6,7},{7,6},{8,9},{9,8},{10,11... | collective-permute-start | bytes 565256 | tf_op jit(solution)/shard_map/ppermute | solution.py:280
  12.5 0.1 reduce_sum.9
  12.9 1.3 %collective-permute-done.1.other_ref = f32[14,32,128]{2,1,0:T(8,128)S(1)} collective-permute-done((f32[14,32,128]{2,1,0:T(8,128)S(1)}, f32[14,32,128]{2,1,0:T(8,128)S(1)}, u32[]{:S(2)}, u32[]{:S(2)}) %collective-permute-start.1) | collective-permute-done | bytes 229408 | tf_op jit(solution)/shard_map/ppermute | solution.py:298
  14.2 2.7 %shard_map.65 = (f32[48,32,128]{2,1,0:T(8,128)S(1)}, bf16[256,256]{1,0:T(8,128)(2,1)S(1)}, bf16[256,256]{1,0:T(8,128)(2,1)S(1)}, bf16[256,256]{1,0:T(8,128)(2,1)...) custom-call(s32[3]{0:T(128)S(1)} %pad_add_fusion.scalar_ref, ...), custom_call_target="tpu_custom_call" | custom-call | tf_op jit(solution)/shard_map/pallas_call | solution.py:302
  16.9 4.3 %collective-permute-done.4.refs_3_ = f32[368,128]{1,0:T(8,128)S(1)} collective-permute-done((f32[368,128]{1,0:T(8,128)S(1)}, f32[368,128]{1,0:T(8,128)S(1)}, u32[]{:S(2)}, u32[]{:S(2)}) %collective-permute-start.4) | collective-permute-done | bytes 188448 | tf_op jit(solution)/shard_map/ppermute | solution.py:280
  21.3 2.2 %collective-permute-done.2.refs_1_ = f32[368,128]{1,0:T(8,128)S(1)} collective-permute-done((f32[368,128]{1,0:T(8,128)S(1)}, f32[368,128]{1,0:T(8,128)S(1)}, u32[]{:S(2)}, u32[]{:S(2)}) %collective-permute-start.2) | collective-permute-done | bytes 188448 | tf_op jit(solution)/shard_map/ppermute | solution.py:280
  23.5 0.5 %collective-permute-done.3.refs_2_ = f32[368,128]{1,0:T(8,128)S(1)} collective-permute-done((f32[368,128]{1,0:T(8,128)S(1)}, f32[368,128]{1,0:T(8,128)S(1)}, u32[]{:S(2)}, u32[]{:S(2)}) %collective-permute-start.3) | collective-permute-done | bytes 188448 | tf_op jit(solution)/shard_map/ppermute | solution.py:280
  24.0 1.3 %shard_map.66 = (f32[8,32,128]{2,1,0:T(8,128)S(1)}, f32[8,32,128]{2,1,0:T(8,128)S(1)}, f32[46,32,128]{2,1,0:T(8,128)S(1)}) custom-call(s32[8,128]{1,0:T(8,128)S(1)} %get-tuple-element.26.flag_ref, f32[32,8,128]{2,1,0:T(8,128)S(1)} %get-tuple-element.27.weight_ref, f32[15,8,128]{2,1,0:T(8,128)S(1)} %get-tuple-element.28.splat_ref, f32[1024,128]{1,0:T(8,128)S(1)} %bitcast.10, ...), custom_call_target="tpu_custom_call" | custom-call | tf_op jit(solution)/shard_map/pallas_call | solution.py:322
  25.3 0.8 %shard_map.67 = (f32[8,32,128]{2,1,0:T(8,128)S(1)}, f32[8,32,128]{2,1,0:T(8,128)S(1)}) custom-call(f32[32,8,128]{2,1,0:T(8,128)S(1)} %get-tuple-element.27.weight_ref, f32[15,8,128]{2,1,0:T(8,128)S(1)} %get-tuple-element.28.splat_ref, f32[46,32,128]{2,1,0:T(8,128)S(1)} %get-tuple-element.40.ratio_ref, bf16[256,256]{1,0:T(8,128)(2,1)S(1)} %get-tuple-element.30.rows_high_ref, ...), custom_call_target="tpu_custom_call" | custom-call | flops 536870912 | bytes 2097152 | tf_op jit(solution)/shard_map/pallas_call | solution.py:335
  26.1 0.6 %collective-permute-start.9 = (f32[8,32,128]{2,1,0:T(8,128)S(1)}, f32[8,32,128]{2,1,0:T(8,128)S(1)}, u32[]{:S(2)}, u32[]{:S(2)}) collective-permute-start(f32[8,32,128]{2,1,0:T(8,128)S(1)} %get-tuple-element.42), channel_id=1, source_target_pairs={{0,4},{4,0},{8,12},{12,8},{16,20},{20,16},{24,28},{28,24},{1,5},{5... | collective-permute-start | bytes 393224 | tf_op jit(solution)/shard_map/ppermute | solution.py:343
  26.7 1.6 %collective-permute-start.6 = (f32[8,32,128]{2,1,0:T(8,128)S(1)}, f32[8,32,128]{2,1,0:T(8,128)S(1)}, u32[]{:S(2)}, u32[]{:S(2)}) collective-permute-start(f32[8,32,128]{2,1,0:T(8,128)S(1)} %add.44), channel_id=1, source_target_pairs={{0,8},{4,20},{8,0},{12,28},{16,24},{20,4},{24,16},{28,12},{1,9},{5... | collective-permute-start | bytes 393224 | tf_op jit(solution)/shard_map/ppermute | solution.py:350
  28.3 0.9 %collective-permute-start.10 = (f32[8,32,128]{2,1,0:T(8,128)S(1)}, f32[8,32,128]{2,1,0:T(8,128)S(1)}, u32[]{:S(2)}, u32[]{:S(2)}) collective-permute-start(f32[8,32,128]{2,1,0:T(8,128)S(1)} %add.49), channel_id=1, source_target_pairs={{0,8},{4,20},{8,0},{12,28},{16,24},{20,4},{24,16},{28,12},{1,9},{5... | collective-permute-start | bytes 393224 | tf_op jit(solution)/shard_map/ppermute | solution.py:350
  29.2 2.5 %collective-permute-done.6 = f32[8,32,128]{2,1,0:T(8,128)S(1)} collective-permute-done((f32[8,32,128]{2,1,0:T(8,128)S(1)}, f32[8,32,128]{2,1,0:T(8,128)S(1)}, u32[]{:S(2)}, u32[]{:S(2)}) %collective-permute-start.6) | collective-permute-done | bytes 131104 | tf_op jit(solution)/shard_map/ppermute | solution.py:350
  31.7 1.6 %collective-permute-start.7 = (f32[8,32,128]{2,1,0:T(8,128)S(1)}, f32[8,32,128]{2,1,0:T(8,128)S(1)}, u32[]{:S(2)}, u32[]{:S(2)}) collective-permute-start(f32[8,32,128]{2,1,0:T(8,128)S(1)} %add.45), channel_id=1, source_target_pairs={{0,16},{4,12},{8,24},{12,4},{16,0},{20,28},{24,8},{28,20},{1,17},{... | collective-permute-start | bytes 393224 | tf_op jit(solution)/shard_map/ppermute | solution.py:350
  33.3 1.6 %collective-permute-start.11 = (f32[8,32,128]{2,1,0:T(8,128)S(1)}, f32[8,32,128]{2,1,0:T(8,128)S(1)}, u32[]{:S(2)}, u32[]{:S(2)}) collective-permute-start(f32[8,32,128]{2,1,0:T(8,128)S(1)} %add.50), channel_id=1, source_target_pairs={{0,16},{4,12},{8,24},{12,4},{16,0},{20,28},{24,8},{28,20},{1,17},{... | collective-permute-start | bytes 393224 | tf_op jit(solution)/shard_map/ppermute | solution.py:350
  34.9 1.9 %collective-permute-done.7 = f32[8,32,128]{2,1,0:T(8,128)S(1)} collective-permute-done((f32[8,32,128]{2,1,0:T(8,128)S(1)}, f32[8,32,128]{2,1,0:T(8,128)S(1)}, u32[]{:S(2)}, u32[]{:S(2)}) %collective-permute-start.7) | collective-permute-done | bytes 131104 | tf_op jit(solution)/shard_map/ppermute | solution.py:350
  36.9 1.5 %collective-permute-done.11 = f32[8,32,128]{2,1,0:T(8,128)S(1)} collective-permute-done((f32[8,32,128]{2,1,0:T(8,128)S(1)}, f32[8,32,128]{2,1,0:T(8,128)S(1)}, u32[]{:S(2)}, u32[]{:S(2)}) %collective-permute-start.11) | collective-permute-done | bytes 131104 | tf_op jit(solution)/shard_map/ppermute | solution.py:350
  38.5 1.3 %collective-permute-done.12 = f32[8,32,128]{2,1,0:T(8,128)S(1)} collective-permute-done((f32[8,32,128]{2,1,0:T(8,128)S(1)}, f32[8,32,128]{2,1,0:T(8,128)S(1)}, u32[]{:S(2)}, u32[]{:S(2)}) %collective-permute-start.12) | collective-permute-done | bytes 131104 | tf_op jit(solution)/shard_map/ppermute | solution.py:356
  39.8 0.8 %pad_maximum_fusion = f32[32,32,128]{2,1,0:T(8,128)} fusion(f32[8,32,128]{2,1,0:T(8,128)S(1)} %get-tuple-element.48, f32[8,32,128]{2,1,0:T(8,128)S(1)} %get-tuple-element.47, f32[8,32,128]{2,1,0:T(8,128)S(1)} %get-tuple-element.46, f32[8,32,128]{2,1,0:T(8,128)S(1)} %get-tuple-element.45), kind=kLoop, calls=%fused_computation | loop fusion | flops 393216 | bytes 1048576 | tf_op jit(solution)/shard_map/concatenate | solution.py:358
  (34 shorter events, 0.8 us)
Async XLA Ops:
  1.0 11.7 %collective-permute-start = (f32[14,32,128]{2,1,0:T(8,128)S(1)}, f32[14,32,128]{2,1,0:T(8,128)S(1)}, u32[]{:S(2)}, u32[]{:S(2)}) collective-permute-start(f32[14,32,128]{2,1,0:T(8,128)S(1)} %constant_dynamic-slice_fusion.2), channel_id=1, source_target_pairs={{0,1},{1,0},{2,3},{3,2},{4,4},{5,6},{6,5},{7,7},{8,9},{9,8},{10,11... | collective-permute-start | bytes 688136 | tf_op jit(solution)/shard_map/ppermute | solution.py:293
  5.9 1.0 %copy-start = (f32[1,32,32,128]{3,2,1,0:T(8,128)S(1)}, f32[1,32,32,128]{3,2,1,0:T(8,128)}, u32[]{:S(2)}) copy-start(f32[1,32,32,128]{3,2,1,0:T(8,128)} %param.7) | copy-start | bytes 1572868
  6.9 3.8 %copy-start.1 = (f32[1,32,32,128]{3,2,1,0:T(8,128)S(1)}, f32[1,32,32,128]{3,2,1,0:T(8,128)}, u32[]{:S(2)}) copy-start(f32[1,32,32,128]{3,2,1,0:T(8,128)} %param.7) | copy-start | bytes 1572868
  7.4 16.6 %collective-permute-start.3 = (f32[368,128]{1,0:T(8,128)S(1)}, f32[368,128]{1,0:T(8,128)S(1)}, u32[]{:S(2)}, u32[]{:S(2)}) collective-permute-start(f32[368,128]{1,0:T(8,128)S(1)} %get-tuple-element.34), channel_id=1, source_target_pairs={{0,2},{1,3},{2,0},{3,1},{4,6},{5,7},{6,4},{7,5},{8,10},{9,11},{10,... | collective-permute-start | bytes 565256 | tf_op jit(solution)/shard_map/ppermute | solution.py:280
  10.7 3.5 %copy-start.2 = (f32[32,32,128]{2,1,0:T(8,128)S(1)}, f32[32,32,128]{2,1,0:T(8,128)}, u32[]{:S(2)}) copy-start(f32[32,32,128]{2,1,0:T(8,128)} %estimate_ref.1) | copy-start | bytes 1572868
  10.8 10.5 %collective-permute-start.4 = (f32[368,128]{1,0:T(8,128)S(1)}, f32[368,128]{1,0:T(8,128)S(1)}, u32[]{:S(2)}, u32[]{:S(2)}) collective-permute-start(f32[368,128]{1,0:T(8,128)S(1)} %pad_select_fusion), channel_id=1, source_target_pairs={{0,3},{1,2},{2,1},{3,0},{4,7},{5,6},{6,5},{7,4},{8,11},{9,10},{10,... | collective-permute-start | bytes 565256 | tf_op jit(solution)/shard_map/ppermute | solution.py:280
  10.9 1.6 %copy-start.4 = (f32[1,3,15]{2,0,1:T(1,128)S(1)}, f32[1,3,15]{2,0,1:T(1,128)}, u32[]{:S(2)}) copy-start(f32[1,3,15]{2,0,1:T(1,128)} %param.8) | copy-start | bytes 544
  10.9 12.6 %collective-permute-start.2 = (f32[368,128]{1,0:T(8,128)S(1)}, f32[368,128]{1,0:T(8,128)S(1)}, u32[]{:S(2)}, u32[]{:S(2)}) collective-permute-start(f32[368,128]{1,0:T(8,128)S(1)} %pad_select_fusion.1), channel_id=1, source_target_pairs={{0,1},{1,0},{2,3},{3,2},{4,5},{5,4},{6,7},{7,6},{8,9},{9,8},{10,11... | collective-permute-start | bytes 565256 | tf_op jit(solution)/shard_map/ppermute | solution.py:280
  12.7 1.5 %collective-permute-start.1 = (f32[14,32,128]{2,1,0:T(8,128)S(1)}, f32[14,32,128]{2,1,0:T(8,128)S(1)}, u32[]{:S(2)}, u32[]{:S(2)}) collective-permute-start(f32[14,32,128]{2,1,0:T(8,128)S(1)} %collective-permute-done.near_ref), channel_id=1, source_target_pairs={{0,4},{4,0},{8,12},{12,8},{16,20},{20,16},{24,28},{28,24},{1,5},{5... | collective-permute-start | bytes 688136 | tf_op jit(solution)/shard_map/ppermute | solution.py:298
  12.9 1.3 %copy-start.3 = (s32[1,32]{1,0:T(1,128)S(1)}, s32[1,32]{1,0:T(1,128)}, u32[]{:S(2)}) copy-start(s32[1,32]{1,0:T(1,128)} %param.11) | copy-start | bytes 388
  25.2 1.4 %collective-permute-start.5 = (f32[8,32,128]{2,1,0:T(8,128)S(1)}, f32[8,32,128]{2,1,0:T(8,128)S(1)}, u32[]{:S(2)}, u32[]{:S(2)}) collective-permute-start(f32[8,32,128]{2,1,0:T(8,128)S(1)} %get-tuple-element.38), channel_id=1, source_target_pairs={{0,4},{4,0},{8,12},{12,8},{16,20},{20,16},{24,28},{28,24},{1,5},{5... | collective-permute-start | bytes 393224 | tf_op jit(solution)/shard_map/ppermute | solution.py:332
  26.1 2.1 %collective-permute-start.9 = (f32[8,32,128]{2,1,0:T(8,128)S(1)}, f32[8,32,128]{2,1,0:T(8,128)S(1)}, u32[]{:S(2)}, u32[]{:S(2)}) collective-permute-start(f32[8,32,128]{2,1,0:T(8,128)S(1)} %get-tuple-element.42), channel_id=1, source_target_pairs={{0,4},{4,0},{8,12},{12,8},{16,20},{20,16},{24,28},{28,24},{1,5},{5... | collective-permute-start | bytes 393224 | tf_op jit(solution)/shard_map/ppermute | solution.py:343
  26.7 5.0 %collective-permute-start.6 = (f32[8,32,128]{2,1,0:T(8,128)S(1)}, f32[8,32,128]{2,1,0:T(8,128)S(1)}, u32[]{:S(2)}, u32[]{:S(2)}) collective-permute-start(f32[8,32,128]{2,1,0:T(8,128)S(1)} %add.44), channel_id=1, source_target_pairs={{0,8},{4,20},{8,0},{12,28},{16,24},{20,4},{24,16},{28,12},{1,9},{5... | collective-permute-start | bytes 393224 | tf_op jit(solution)/shard_map/ppermute | solution.py:350
  28.3 5.1 %collective-permute-start.10 = (f32[8,32,128]{2,1,0:T(8,128)S(1)}, f32[8,32,128]{2,1,0:T(8,128)S(1)}, u32[]{:S(2)}, u32[]{:S(2)}) collective-permute-start(f32[8,32,128]{2,1,0:T(8,128)S(1)} %add.49), channel_id=1, source_target_pairs={{0,8},{4,20},{8,0},{12,28},{16,24},{20,4},{24,16},{28,12},{1,9},{5... | collective-permute-start | bytes 393224 | tf_op jit(solution)/shard_map/ppermute | solution.py:350
  31.7 5.0 %collective-permute-start.7 = (f32[8,32,128]{2,1,0:T(8,128)S(1)}, f32[8,32,128]{2,1,0:T(8,128)S(1)}, u32[]{:S(2)}, u32[]{:S(2)}) collective-permute-start(f32[8,32,128]{2,1,0:T(8,128)S(1)} %add.45), channel_id=1, source_target_pairs={{0,16},{4,12},{8,24},{12,4},{16,0},{20,28},{24,8},{28,20},{1,17},{... | collective-permute-start | bytes 393224 | tf_op jit(solution)/shard_map/ppermute | solution.py:350
  33.3 5.0 %collective-permute-start.11 = (f32[8,32,128]{2,1,0:T(8,128)S(1)}, f32[8,32,128]{2,1,0:T(8,128)S(1)}, u32[]{:S(2)}, u32[]{:S(2)}) collective-permute-start(f32[8,32,128]{2,1,0:T(8,128)S(1)} %add.50), channel_id=1, source_target_pairs={{0,16},{4,12},{8,24},{12,4},{16,0},{20,28},{24,8},{28,20},{1,17},{... | collective-permute-start | bytes 393224 | tf_op jit(solution)/shard_map/ppermute | solution.py:350
  36.8 1.7 %collective-permute-start.8 = (f32[8,32,128]{2,1,0:T(8,128)S(1)}, f32[8,32,128]{2,1,0:T(8,128)S(1)}, u32[]{:S(2)}, u32[]{:S(2)}) collective-permute-start(f32[8,32,128]{2,1,0:T(8,128)S(1)} %exponential_multiply_fusion.1), channel_id=1, source_target_pairs={{0,4},{4,0},{8,12},{12,8},{16,20},{20,16},{24,28},{28,24},{1,5},{5... | collective-permute-start | bytes 393224 | tf_op jit(solution)/shard_map/ppermute | solution.py:356
  38.4 1.4 %collective-permute-start.12 = (f32[8,32,128]{2,1,0:T(8,128)S(1)}, f32[8,32,128]{2,1,0:T(8,128)S(1)}, u32[]{:S(2)}, u32[]{:S(2)}) collective-permute-start(f32[8,32,128]{2,1,0:T(8,128)S(1)} %exponential_multiply_fusion), channel_id=1, source_target_pairs={{0,4},{4,0},{8,12},{12,8},{16,20},{20,16},{24,28},{28,24},{1,5},{5... | collective-permute-start | bytes 393224 | tf_op jit(solution)/shard_map/ppermute | solution.py:356

commit v5 on v4

--- a/solution.py
+++ b/solution.py
@@ -284,17 +284,21 @@
     scalars = jnp.stack([shift[0], core.astype(jnp.int32), late_perm[0]])
 
     swap = [(i, i ^ 1) for i in range(views)]
-    later = estimate
     def beside_of(v, i):
         there = i ^ 1 if v % 2 == 0 else ((i + 1) ^ 1) - 1
         return there if 0 <= there < count else i
 
-    start = jnp.where(even == (core == 0), zb - 2 * reach, 0)
-    near = lax.ppermute(
-        lax.dynamic_slice_in_dim(later, start, 2 * reach, 0),
+    side = chip % 2
+    start = jnp.where(even == (core == 0), zb - 2 * reach, 0) + reach * side
+    quarter = lax.ppermute(
+        lax.dynamic_slice_in_dim(estimate, start, reach, 0),
         ("view", "bulk"),
         [(v * count + i, v * count + beside_of(v, i)) for v in range(views) for i in range(count)],
     )
+    across = lax.ppermute(quarter, "view", [(v, v ^ 2) for v in range(views)])
+    near = jnp.concatenate([
+        jnp.where(side == 0, quarter, across), jnp.where(side == 0, across, quarter)
+    ])
     other = lax.ppermute(near, "view", swap)
 
     group = WIDE // ny

time: 41.2 us -> 40.9 us (level)
  starting transfers between devices: 15 us -> 16.7 us
  waiting for transfers between devices: 15.5 us -> 13.8 us
    ppermute x3, waiting for transfers between devices: 7.02 us -> 2.14 us  [shards(): lax.ppermute(packed[k], 'bulk', [(i, i ^ k) for i in range(count)])]
    ppermute x1 -> x2, waiting for transfers between devices: 0.01 us -> 3.23 us  [the longest x1 3.23 us: shards(): across = lax.ppermute(quarter, 'view', [(v, v ^ 2) for v in range(views)])]
    ppermute x1 -> x2, starting transfers between devices: 4.93 us -> 6.47 us  [the longest x1 4.93 us: shards(): lax.ppermute(lax.dynamic_slice_in_dim(estimate, start, reach, 0), ('view'...]
  transfers between devices with their start and end apart: 13 -> 14, of which waited for: 8 -> 7; matrix products, arithmetic and copies ran while one was open for 1% -> 2% of each run, Pallas kernels for 10% -> 10%
where the time goes in v5:
time: 40.9 us; the launch traced here: 40.6 us
  starting transfers between devices  16.7 us (41%)
  waiting for transfers between devices  13.8 us (34%)
  Pallas kernels  5.21 us (13%)
  local copies, waits for them, and re-layouts  2.01 us (5%)
  between operations  1.51 us (4%)
  other arithmetic  1.43 us (3%)
    ppermute x4, waiting for transfers between devices, shards(): lax.ppermute(total[part], 'view', [(i, i ^ flips[i % 2]) for i in range(v...  5.84 us
    ppermute x4, starting transfers between devices, shards(): lax.ppermute(total[part], 'view', [(i, i ^ flips[i % 2]) for i in range(v...  5.7 us
    ppermute x1, starting transfers between devices, shards(): lax.ppermute(lax.dynamic_slice_in_dim(estimate, start, reach, 0), ('view'...  4.93 us
    ppermute x3, starting transfers between devices, shards(): lax.ppermute(packed[k], 'bulk', [(i, i ^ k) for i in range(count)])  3.66 us
    ppermute x1, waiting for transfers between devices, shards(): across = lax.ppermute(quarter, 'view', [(v, v ^ 2) for v in range(views)])  3.23 us
    pallas_call x1, Pallas kernels, shards(): pl.pallas_call(functools.partial(forward_kernel, zb, ny, nx, planes), out...  2.75 us
    ppermute x3, waiting for transfers between devices, shards(): lax.ppermute(packed[k], 'bulk', [(i, i ^ k) for i in range(count)])  2.14 us
    ppermute x1, starting transfers between devices, shards(): across = lax.ppermute(quarter, 'view', [(v, v ^ 2) for v in range(views)])  1.55 us
  transfers between devices with their start and end apart: 14, of which 7 were waited for; matrix products, arithmetic and copies ran while one was open for 2% of the time, Pallas kernels for 10%

profile of v5, /device:TPU:0, one launch (start us, length us, event | category | flops | bytes accessed | tf_op | source)
XLA Modules:
  0.0 40.6 jit_solution(1128210471729695823)
XLA Ops:
  0.0 0.9 %constant_dynamic-slice_fusion.2 = f32[7,32,128]{2,1,0:T(8,128)S(1)} fusion(f32[32,32,128]{2,1,0:T(8,128)} %estimate_ref.1, s32[]{:T(128)S(6)} %select_n.102), kind=kLoop, calls=%fused_computation.15 | loop fusion | bytes 229380 | tf_op jit(solution)/shard_map/dynamic_slice | solution.py:294
  0.9 4.9 %collective-permute-start = (f32[7,32,128]{2,1,0:T(8,128)S(1)}, f32[7,32,128]{2,1,0:T(8,128)S(1)}, u32[]{:S(2)}, u32[]{:S(2)}) collective-permute-start(f32[7,32,128]{2,1,0:T(8,128)S(1)} %constant_dynamic-slice_fusion.2), channel_id=1, source_target_pairs={{0,1},{1,0},{2,3},{3,2},{4,4},{5,6},{6,5},{7,7},{8,9},{9,8},{10,11... | collective-permute-start | bytes 344072 | tf_op jit(solution)/shard_map/ppermute | solution.py:293
  5.9 1.0 %copy-done = f32[1,32,32,128]{3,2,1,0:T(8,128)S(1)} copy-done((f32[1,32,32,128]{3,2,1,0:T(8,128)S(1)}, f32[1,32,32,128]{3,2,1,0:T(8,128)}, u32[]{:S(2)}) %copy-start) | copy-done | bytes 524312
  6.9 0.4 %shard_map.64 = (f32[368,128]{1,0:T(8,128)S(1)}, f32[368,128]{1,0:T(8,128)S(1)}, f32[368,128]{1,0:T(8,128)S(1)}, f32[368,128]{1,0:T(8,128)S(1)}) custom-call(f32[1024,128]{1,0:T(8,128)S(1)} %bitcast.8), custom_call_target="tpu_custom_call" | custom-call | tf_op jit(solution)/shard_map/pallas_call | solution.py:250
  7.3 2.7 %collective-permute-start.4 = (f32[368,128]{1,0:T(8,128)S(1)}, f32[368,128]{1,0:T(8,128)S(1)}, u32[]{:S(2)}, u32[]{:S(2)}) collective-permute-start(f32[368,128]{1,0:T(8,128)S(1)} %get-tuple-element.34), channel_id=1, source_target_pairs={{0,2},{1,3},{2,0},{3,1},{4,6},{5,7},{6,4},{7,5},{8,10},{9,11},{10,... | collective-permute-start | bytes 565256 | tf_op jit(solution)/shard_map/ppermute | solution.py:280
  10.8 0.9 %collective-permute-start.3 = (f32[368,128]{1,0:T(8,128)S(1)}, f32[368,128]{1,0:T(8,128)S(1)}, u32[]{:S(2)}, u32[]{:S(2)}) collective-permute-start(f32[368,128]{1,0:T(8,128)S(1)} %pad_select_fusion.1), channel_id=1, source_target_pairs={{0,1},{1,0},{2,3},{3,2},{4,5},{5,4},{6,7},{7,6},{8,9},{9,8},{10,11... | collective-permute-start | bytes 565256 | tf_op jit(solution)/shard_map/ppermute | solution.py:280
  12.4 0.1 reduce_sum.9
  12.6 1.5 %collective-permute-start.1 = (f32[7,32,128]{2,1,0:T(8,128)S(1)}, f32[7,32,128]{2,1,0:T(8,128)S(1)}, u32[]{:S(2)}, u32[]{:S(2)}) collective-permute-start(f32[7,32,128]{2,1,0:T(8,128)S(1)} %collective-permute-done), channel_id=1, source_target_pairs={{0,8},{4,12},{8,0},{12,4},{16,24},{20,28},{24,16},{28,20},{1,9},{5... | collective-permute-start | bytes 344072 | tf_op jit(solution)/shard_map/ppermute | solution.py:298
  14.2 3.2 %collective-permute-done.1 = f32[7,32,128]{2,1,0:T(8,128)S(1)} collective-permute-done((f32[7,32,128]{2,1,0:T(8,128)S(1)}, f32[7,32,128]{2,1,0:T(8,128)S(1)}, u32[]{:S(2)}, u32[]{:S(2)}) %collective-permute-start.1) | collective-permute-done | bytes 114720 | tf_op jit(solution)/shard_map/ppermute | solution.py:298
  17.7 1.3 %collective-permute-done.2.other_ref = f32[14,32,128]{2,1,0:T(8,128)S(1)} collective-permute-done((f32[14,32,128]{2,1,0:T(8,128)S(1)}, f32[14,32,128]{2,1,0:T(8,128)S(1)}, u32[]{:S(2)}, u32[]{:S(2)}) %collective-permute-start.2) | collective-permute-done | bytes 229408 | tf_op jit(solution)/shard_map/ppermute | solution.py:302
  19.0 2.8 %shard_map.65 = (f32[48,32,128]{2,1,0:T(8,128)S(1)}, bf16[256,256]{1,0:T(8,128)(2,1)S(1)}, bf16[256,256]{1,0:T(8,128)(2,1)S(1)}, bf16[256,256]{1,0:T(8,128)(2,1)...) custom-call(s32[3]{0:T(128)S(1)} %pad_add_fusion.scalar_ref, ...), custom_call_target="tpu_custom_call" | custom-call | tf_op jit(solution)/shard_map/pallas_call | solution.py:306
  21.8 2.1 %collective-permute-done.3.refs_1_ = f32[368,128]{1,0:T(8,128)S(1)} collective-permute-done((f32[368,128]{1,0:T(8,128)S(1)}, f32[368,128]{1,0:T(8,128)S(1)}, u32[]{:S(2)}, u32[]{:S(2)}) %collective-permute-start.3) | collective-permute-done | bytes 188448 | tf_op jit(solution)/shard_map/ppermute | solution.py:280
  23.9 1.3 %shard_map.66 = (f32[8,32,128]{2,1,0:T(8,128)S(1)}, f32[8,32,128]{2,1,0:T(8,128)S(1)}, f32[46,32,128]{2,1,0:T(8,128)S(1)}) custom-call(s32[8,128]{1,0:T(8,128)S(1)} %get-tuple-element.26.flag_ref, f32[32,8,128]{2,1,0:T(8,128)S(1)} %get-tuple-element.27.weight_ref, f32[15,8,128]{2,1,0:T(8,128)S(1)} %get-tuple-element.28.splat_ref, f32[1024,128]{1,0:T(8,128)S(1)} %bitcast.10, ...), custom_call_target="tpu_custom_call" | custom-call | tf_op jit(solution)/shard_map/pallas_call | solution.py:326
  25.3 0.8 %shard_map.67 = (f32[8,32,128]{2,1,0:T(8,128)S(1)}, f32[8,32,128]{2,1,0:T(8,128)S(1)}) custom-call(f32[32,8,128]{2,1,0:T(8,128)S(1)} %get-tuple-element.27.weight_ref, f32[15,8,128]{2,1,0:T(8,128)S(1)} %get-tuple-element.28.splat_ref, f32[46,32,128]{2,1,0:T(8,128)S(1)} %get-tuple-element.40.ratio_ref, bf16[256,256]{1,0:T(8,128)(2,1)S(1)} %get-tuple-element.30.rows_high_ref, ...), custom_call_target="tpu_custom_call" | custom-call | flops 536870912 | bytes 2097152 | tf_op jit(solution)/shard_map/pallas_call | solution.py:339
  26.0 0.5 %collective-permute-start.10 = (f32[8,32,128]{2,1,0:T(8,128)S(1)}, f32[8,32,128]{2,1,0:T(8,128)S(1)}, u32[]{:S(2)}, u32[]{:S(2)}) collective-permute-start(f32[8,32,128]{2,1,0:T(8,128)S(1)} %get-tuple-element.42), channel_id=1, source_target_pairs={{0,4},{4,0},{8,12},{12,8},{16,20},{20,16},{24,28},{28,24},{1,5},{5... | collective-permute-start | bytes 393224 | tf_op jit(solution)/shard_map/ppermute | solution.py:347
  26.6 1.6 %collective-permute-start.7 = (f32[8,32,128]{2,1,0:T(8,128)S(1)}, f32[8,32,128]{2,1,0:T(8,128)S(1)}, u32[]{:S(2)}, u32[]{:S(2)}) collective-permute-start(f32[8,32,128]{2,1,0:T(8,128)S(1)} %add.56), channel_id=1, source_target_pairs={{0,8},{4,20},{8,0},{12,28},{16,24},{20,4},{24,16},{28,12},{1,9},{5... | collective-permute-start | bytes 393224 | tf_op jit(solution)/shard_map/ppermute | solution.py:354
  28.2 0.9 %collective-permute-start.11 = (f32[8,32,128]{2,1,0:T(8,128)S(1)}, f32[8,32,128]{2,1,0:T(8,128)S(1)}, u32[]{:S(2)}, u32[]{:S(2)}) collective-permute-start(f32[8,32,128]{2,1,0:T(8,128)S(1)} %add.61), channel_id=1, source_target_pairs={{0,8},{4,20},{8,0},{12,28},{16,24},{20,4},{24,16},{28,12},{1,9},{5... | collective-permute-start | bytes 393224 | tf_op jit(solution)/shard_map/ppermute | solution.py:354
  29.2 2.5 %collective-permute-done.7 = f32[8,32,128]{2,1,0:T(8,128)S(1)} collective-permute-done((f32[8,32,128]{2,1,0:T(8,128)S(1)}, f32[8,32,128]{2,1,0:T(8,128)S(1)}, u32[]{:S(2)}, u32[]{:S(2)}) %collective-permute-start.7) | collective-permute-done | bytes 131104 | tf_op jit(solution)/shard_map/ppermute | solution.py:354
  31.7 1.6 %collective-permute-start.8 = (f32[8,32,128]{2,1,0:T(8,128)S(1)}, f32[8,32,128]{2,1,0:T(8,128)S(1)}, u32[]{:S(2)}, u32[]{:S(2)}) collective-permute-start(f32[8,32,128]{2,1,0:T(8,128)S(1)} %add.57), channel_id=1, source_target_pairs={{0,16},{4,12},{8,24},{12,4},{16,0},{20,28},{24,8},{28,20},{1,17},{... | collective-permute-start | bytes 393224 | tf_op jit(solution)/shard_map/ppermute | solution.py:354
  33.3 1.6 %collective-permute-start.12 = (f32[8,32,128]{2,1,0:T(8,128)S(1)}, f32[8,32,128]{2,1,0:T(8,128)S(1)}, u32[]{:S(2)}, u32[]{:S(2)}) collective-permute-start(f32[8,32,128]{2,1,0:T(8,128)S(1)} %add.62), channel_id=1, source_target_pairs={{0,16},{4,12},{8,24},{12,4},{16,0},{20,28},{24,8},{28,20},{1,17},{... | collective-permute-start | bytes 393224 | tf_op jit(solution)/shard_map/ppermute | solution.py:354
  34.9 1.8 %collective-permute-done.8 = f32[8,32,128]{2,1,0:T(8,128)S(1)} collective-permute-done((f32[8,32,128]{2,1,0:T(8,128)S(1)}, f32[8,32,128]{2,1,0:T(8,128)S(1)}, u32[]{:S(2)}, u32[]{:S(2)}) %collective-permute-start.8) | collective-permute-done | bytes 131104 | tf_op jit(solution)/shard_map/ppermute | solution.py:354
  36.8 1.5 %collective-permute-done.12 = f32[8,32,128]{2,1,0:T(8,128)S(1)} collective-permute-done((f32[8,32,128]{2,1,0:T(8,128)S(1)}, f32[8,32,128]{2,1,0:T(8,128)S(1)}, u32[]{:S(2)}, u32[]{:S(2)}) %collective-permute-start.12) | collective-permute-done | bytes 131104 | tf_op jit(solution)/shard_map/ppermute | solution.py:354
  38.5 1.3 %collective-permute-done.13 = f32[8,32,128]{2,1,0:T(8,128)S(1)} collective-permute-done((f32[8,32,128]{2,1,0:T(8,128)S(1)}, f32[8,32,128]{2,1,0:T(8,128)S(1)}, u32[]{:S(2)}, u32[]{:S(2)}) %collective-permute-start.13) | collective-permute-done | bytes 131104 | tf_op jit(solution)/shard_map/ppermute | solution.py:360
  39.8 0.8 %pad_maximum_fusion = f32[32,32,128]{2,1,0:T(8,128)} fusion(f32[8,32,128]{2,1,0:T(8,128)S(1)} %get-tuple-element.48, f32[8,32,128]{2,1,0:T(8,128)S(1)} %get-tuple-element.47, f32[8,32,128]{2,1,0:T(8,128)S(1)} %get-tuple-element.46, f32[8,32,128]{2,1,0:T(8,128)S(1)} %get-tuple-element.45), kind=kLoop, calls=%fused_computation | loop fusion | flops 393216 | bytes 1048576 | tf_op jit(solution)/shard_map/concatenate | solution.py:362
  (38 shorter events, 0.9 us)
Async XLA Ops:
  0.9 11.6 %collective-permute-start = (f32[7,32,128]{2,1,0:T(8,128)S(1)}, f32[7,32,128]{2,1,0:T(8,128)S(1)}, u32[]{:S(2)}, u32[]{:S(2)}) collective-permute-start(f32[7,32,128]{2,1,0:T(8,128)S(1)} %constant_dynamic-slice_fusion.2), channel_id=1, source_target_pairs={{0,1},{1,0},{2,3},{3,2},{4,4},{5,6},{6,5},{7,7},{8,9},{9,8},{10,11... | collective-permute-start | bytes 344072 | tf_op jit(solution)/shard_map/ppermute | solution.py:293
  5.8 1.0 %copy-start = (f32[1,32,32,128]{3,2,1,0:T(8,128)S(1)}, f32[1,32,32,128]{3,2,1,0:T(8,128)}, u32[]{:S(2)}) copy-start(f32[1,32,32,128]{3,2,1,0:T(8,128)} %param.7) | copy-start | bytes 1572868
  6.9 3.8 %copy-start.1 = (f32[1,32,32,128]{3,2,1,0:T(8,128)S(1)}, f32[1,32,32,128]{3,2,1,0:T(8,128)}, u32[]{:S(2)}) copy-start(f32[1,32,32,128]{3,2,1,0:T(8,128)} %param.7) | copy-start | bytes 1572868
  7.3 16.6 %collective-permute-start.4 = (f32[368,128]{1,0:T(8,128)S(1)}, f32[368,128]{1,0:T(8,128)S(1)}, u32[]{:S(2)}, u32[]{:S(2)}) collective-permute-start(f32[368,128]{1,0:T(8,128)S(1)} %get-tuple-element.34), channel_id=1, source_target_pairs={{0,2},{1,3},{2,0},{3,1},{4,6},{5,7},{6,4},{7,5},{8,10},{9,11},{10,... | collective-permute-start | bytes 565256 | tf_op jit(solution)/shard_map/ppermute | solution.py:280
  10.7 11.1 %collective-permute-start.5 = (f32[368,128]{1,0:T(8,128)S(1)}, f32[368,128]{1,0:T(8,128)S(1)}, u32[]{:S(2)}, u32[]{:S(2)}) collective-permute-start(f32[368,128]{1,0:T(8,128)S(1)} %pad_select_fusion), channel_id=1, source_target_pairs={{0,3},{1,2},{2,1},{3,0},{4,7},{5,6},{6,5},{7,4},{8,11},{9,10},{10,... | collective-permute-start | bytes 565256 | tf_op jit(solution)/shard_map/ppermute | solution.py:280
  10.8 1.6 %copy-start.4 = (f32[1,3,15]{2,0,1:T(1,128)S(1)}, f32[1,3,15]{2,0,1:T(1,128)}, u32[]{:S(2)}) copy-start(f32[1,3,15]{2,0,1:T(1,128)} %param.8) | copy-start | bytes 544
  10.8 8.2 %copy-start.2 = (f32[32,32,128]{2,1,0:T(8,128)S(1)}, f32[32,32,128]{2,1,0:T(8,128)}, u32[]{:S(2)}) copy-start(f32[32,32,128]{2,1,0:T(8,128)} %estimate_ref.1) | copy-start | bytes 1572868
  10.8 13.1 %collective-permute-start.3 = (f32[368,128]{1,0:T(8,128)S(1)}, f32[368,128]{1,0:T(8,128)S(1)}, u32[]{:S(2)}, u32[]{:S(2)}) collective-permute-start(f32[368,128]{1,0:T(8,128)S(1)} %pad_select_fusion.1), channel_id=1, source_target_pairs={{0,1},{1,0},{2,3},{3,2},{4,5},{5,4},{6,7},{7,6},{8,9},{9,8},{10,11... | collective-permute-start | bytes 565256 | tf_op jit(solution)/shard_map/ppermute | solution.py:280
  12.6 4.8 %collective-permute-start.1 = (f32[7,32,128]{2,1,0:T(8,128)S(1)}, f32[7,32,128]{2,1,0:T(8,128)S(1)}, u32[]{:S(2)}, u32[]{:S(2)}) collective-permute-start(f32[7,32,128]{2,1,0:T(8,128)S(1)} %collective-permute-done), channel_id=1, source_target_pairs={{0,8},{4,12},{8,0},{12,4},{16,24},{20,28},{24,16},{28,20},{1,9},{5... | collective-permute-start | bytes 344072 | tf_op jit(solution)/shard_map/ppermute | solution.py:298
  17.4 1.6 %collective-permute-start.2 = (f32[14,32,128]{2,1,0:T(8,128)S(1)}, f32[14,32,128]{2,1,0:T(8,128)S(1)}, u32[]{:S(2)}, u32[]{:S(2)}) collective-permute-start(f32[14,32,128]{2,1,0:T(8,128)S(1)} %pad_maximum_fusion.1.near_ref), channel_id=1, source_target_pairs={{0,4},{4,0},{8,12},{12,8},{16,20},{20,16},{24,28},{28,24},{1,5},{5... | collective-permute-start | bytes 688136 | tf_op jit(solution)/shard_map/ppermute | solution.py:302
  17.7 1.3 %copy-start.3 = (s32[1,32]{1,0:T(1,128)S(1)}, s32[1,32]{1,0:T(1,128)}, u32[]{:S(2)}) copy-start(s32[1,32]{1,0:T(1,128)} %param.11) | copy-start | bytes 388
  25.2 1.4 %collective-permute-start.6 = (f32[8,32,128]{2,1,0:T(8,128)S(1)}, f32[8,32,128]{2,1,0:T(8,128)S(1)}, u32[]{:S(2)}, u32[]{:S(2)}) collective-permute-start(f32[8,32,128]{2,1,0:T(8,128)S(1)} %get-tuple-element.38), channel_id=1, source_target_pairs={{0,4},{4,0},{8,12},{12,8},{16,20},{20,16},{24,28},{28,24},{1,5},{5... | collective-permute-start | bytes 393224 | tf_op jit(solution)/shard_map/ppermute | solution.py:336
  26.0 2.2 %collective-permute-start.10 = (f32[8,32,128]{2,1,0:T(8,128)S(1)}, f32[8,32,128]{2,1,0:T(8,128)S(1)}, u32[]{:S(2)}, u32[]{:S(2)}) collective-permute-start(f32[8,32,128]{2,1,0:T(8,128)S(1)} %get-tuple-element.42), channel_id=1, source_target_pairs={{0,4},{4,0},{8,12},{12,8},{16,20},{20,16},{24,28},{28,24},{1,5},{5... | collective-permute-start | bytes 393224 | tf_op jit(solution)/shard_map/ppermute | solution.py:347
  26.6 5.0 %collective-permute-start.7 = (f32[8,32,128]{2,1,0:T(8,128)S(1)}, f32[8,32,128]{2,1,0:T(8,128)S(1)}, u32[]{:S(2)}, u32[]{:S(2)}) collective-permute-start(f32[8,32,128]{2,1,0:T(8,128)S(1)} %add.56), channel_id=1, source_target_pairs={{0,8},{4,20},{8,0},{12,28},{16,24},{20,4},{24,16},{28,12},{1,9},{5... | collective-permute-start | bytes 393224 | tf_op jit(solution)/shard_map/ppermute | solution.py:354
  28.2 5.1 %collective-permute-start.11 = (f32[8,32,128]{2,1,0:T(8,128)S(1)}, f32[8,32,128]{2,1,0:T(8,128)S(1)}, u32[]{:S(2)}, u32[]{:S(2)}) collective-permute-start(f32[8,32,128]{2,1,0:T(8,128)S(1)} %add.61), channel_id=1, source_target_pairs={{0,8},{4,20},{8,0},{12,28},{16,24},{20,4},{24,16},{28,12},{1,9},{5... | collective-permute-start | bytes 393224 | tf_op jit(solution)/shard_map/ppermute | solution.py:354
  31.7 5.0 %collective-permute-start.8 = (f32[8,32,128]{2,1,0:T(8,128)S(1)}, f32[8,32,128]{2,1,0:T(8,128)S(1)}, u32[]{:S(2)}, u32[]{:S(2)}) collective-permute-start(f32[8,32,128]{2,1,0:T(8,128)S(1)} %add.57), channel_id=1, source_target_pairs={{0,16},{4,12},{8,24},{12,4},{16,0},{20,28},{24,8},{28,20},{1,17},{... | collective-permute-start | bytes 393224 | tf_op jit(solution)/shard_map/ppermute | solution.py:354
  33.3 5.0 %collective-permute-start.12 = (f32[8,32,128]{2,1,0:T(8,128)S(1)}, f32[8,32,128]{2,1,0:T(8,128)S(1)}, u32[]{:S(2)}, u32[]{:S(2)}) collective-permute-start(f32[8,32,128]{2,1,0:T(8,128)S(1)} %add.62), channel_id=1, source_target_pairs={{0,16},{4,12},{8,24},{12,4},{16,0},{20,28},{24,8},{28,20},{1,17},{... | collective-permute-start | bytes 393224 | tf_op jit(solution)/shard_map/ppermute | solution.py:354
  36.7 1.7 %collective-permute-start.9 = (f32[8,32,128]{2,1,0:T(8,128)S(1)}, f32[8,32,128]{2,1,0:T(8,128)S(1)}, u32[]{:S(2)}, u32[]{:S(2)}) collective-permute-start(f32[8,32,128]{2,1,0:T(8,128)S(1)} %exponential_multiply_fusion.1), channel_id=1, source_target_pairs={{0,4},{4,0},{8,12},{12,8},{16,20},{20,16},{24,28},{28,24},{1,5},{5... | collective-permute-start | bytes 393224 | tf_op jit(solution)/shard_map/ppermute | solution.py:360
  38.4 1.4 %collective-permute-start.13 = (f32[8,32,128]{2,1,0:T(8,128)S(1)}, f32[8,32,128]{2,1,0:T(8,128)S(1)}, u32[]{:S(2)}, u32[]{:S(2)}) collective-permute-start(f32[8,32,128]{2,1,0:T(8,128)S(1)} %exponential_multiply_fusion), channel_id=1, source_target_pairs={{0,4},{4,0},{8,12},{12,8},{16,20},{20,16},{24,28},{28,24},{1,5},{5... | collective-permute-start | bytes 393224 | tf_op jit(solution)/shard_map/ppermute | solution.py:360

commit v6 on v5

--- a/solution.py
+++ b/solution.py
@@ -274,7 +274,7 @@
         above = even if k == 1 else jnp.logical_not(even)
         start = jnp.where(above, (zb - reach) * ny, 0)
         packed[k] = jnp.where(late_perm[0] == 1, block, beside(start))
-    packed[count - 1], _ = lax.optimization_barrier((packed[count - 1], packed[2]))
+    packed[1], _ = lax.optimization_barrier((packed[1], packed[2]))
     blocks = {0: packed[0]}
     for k in range(count - 1, 0, -1):
         blocks[k] = lax.ppermute(packed[k], "bulk", [(i, i ^ k) for i in range(count)])

time: 40.9 us -> 40.7 us (level)
  waiting for transfers between devices: 13.8 us -> 12.6 us
  starting transfers between devices: 16.7 us -> 17.7 us
    ppermute x3, waiting for transfers between devices: 2.14 us -> 0.97 us  [shards(): lax.ppermute(packed[k], 'bulk', [(i, i ^ k) for i in range(count)])]
    ppermute x3, starting transfers between devices: 3.66 us -> 4.58 us  [shards(): lax.ppermute(packed[k], 'bulk', [(i, i ^ k) for i in range(count)])]
where the time goes in v6:
time: 40.7 us; the launch traced here: 40.4 us
  starting transfers between devices  17.7 us (43%)
  waiting for transfers between devices  12.6 us (31%)
  Pallas kernels  5.19 us (13%)
  local copies, waits for them, and re-layouts  2.01 us (5%)
  between operations  1.49 us (4%)
  other arithmetic  1.42 us (3%)
    ppermute x4, starting transfers between devices, shards(): lax.ppermute(total[part], 'view', [(i, i ^ flips[i % 2]) for i in range(v...  5.82 us
    ppermute x4, waiting for transfers between devices, shards(): lax.ppermute(total[part], 'view', [(i, i ^ flips[i % 2]) for i in range(v...  5.78 us
    ppermute x1, starting transfers between devices, shards(): lax.ppermute(lax.dynamic_slice_in_dim(estimate, start, reach, 0), ('view'...  4.93 us
    ppermute x3, starting transfers between devices, shards(): lax.ppermute(packed[k], 'bulk', [(i, i ^ k) for i in range(count)])  4.58 us
    ppermute x1, waiting for transfers between devices, shards(): across = lax.ppermute(quarter, 'view', [(v, v ^ 2) for v in range(views)])  3.23 us
    pallas_call x1, Pallas kernels, shards(): pl.pallas_call(functools.partial(forward_kernel, zb, ny, nx, planes), out...  2.74 us
    ppermute x1, starting transfers between devices, shards(): across = lax.ppermute(quarter, 'view', [(v, v ^ 2) for v in range(views)])  1.55 us
    ppermute x2, waiting for transfers between devices, shards(): their = lax.ppermute(own, 'view', swap)  1.3 us
  transfers between devices with their start and end apart: 14, of which 7 were waited for; matrix products, arithmetic and copies ran while one was open for 2% of the time, Pallas kernels for 10%

profile of v6, /device:TPU:0, one launch (start us, length us, event | category | flops | bytes accessed | tf_op | source)
XLA Modules:
  0.0 40.4 jit_solution(18393285016958297619)
XLA Ops:
  0.0 0.9 %constant_dynamic-slice_fusion.2 = f32[7,32,128]{2,1,0:T(8,128)S(1)} fusion(f32[32,32,128]{2,1,0:T(8,128)} %estimate_ref.1, s32[]{:T(128)S(6)} %select_n.102), kind=kLoop, calls=%fused_computation.15 | loop fusion | bytes 229380 | tf_op jit(solution)/shard_map/dynamic_slice | solution.py:294
  0.9 4.9 %collective-permute-start = (f32[7,32,128]{2,1,0:T(8,128)S(1)}, f32[7,32,128]{2,1,0:T(8,128)S(1)}, u32[]{:S(2)}, u32[]{:S(2)}) collective-permute-start(f32[7,32,128]{2,1,0:T(8,128)S(1)} %constant_dynamic-slice_fusion.2), channel_id=1, source_target_pairs={{0,1},{1,0},{2,3},{3,2},{4,4},{5,6},{6,5},{7,7},{8,9},{9,8},{10,11... | collective-permute-start | bytes 344072 | tf_op jit(solution)/shard_map/ppermute | solution.py:293
  5.9 1.0 %copy-done = f32[1,32,32,128]{3,2,1,0:T(8,128)S(1)} copy-done((f32[1,32,32,128]{3,2,1,0:T(8,128)S(1)}, f32[1,32,32,128]{3,2,1,0:T(8,128)}, u32[]{:S(2)}) %copy-start) | copy-done | bytes 524312
  6.9 0.4 %shard_map.64 = (f32[368,128]{1,0:T(8,128)S(1)}, f32[368,128]{1,0:T(8,128)S(1)}, f32[368,128]{1,0:T(8,128)S(1)}, f32[368,128]{1,0:T(8,128)S(1)}) custom-call(f32[1024,128]{1,0:T(8,128)S(1)} %bitcast.8), custom_call_target="tpu_custom_call" | custom-call | tf_op jit(solution)/shard_map/pallas_call | solution.py:250
  7.3 2.7 %collective-permute-start.4 = (f32[368,128]{1,0:T(8,128)S(1)}, f32[368,128]{1,0:T(8,128)S(1)}, u32[]{:S(2)}, u32[]{:S(2)}) collective-permute-start(f32[368,128]{1,0:T(8,128)S(1)} %get-tuple-element.34), channel_id=1, source_target_pairs={{0,2},{1,3},{2,0},{3,1},{4,6},{5,7},{6,4},{7,5},{8,10},{9,11},{10,... | collective-permute-start | bytes 565256 | tf_op jit(solution)/shard_map/ppermute | solution.py:280
  10.7 0.5 %collective-permute-start.3 = (f32[368,128]{1,0:T(8,128)S(1)}, f32[368,128]{1,0:T(8,128)S(1)}, u32[]{:S(2)}, u32[]{:S(2)}) collective-permute-start(f32[368,128]{1,0:T(8,128)S(1)} %pad_select_fusion.1), channel_id=1, source_target_pairs={{0,1},{1,0},{2,3},{3,2},{4,5},{5,4},{6,7},{7,6},{8,9},{9,8},{10,11... | collective-permute-start | bytes 565256 | tf_op jit(solution)/shard_map/ppermute | solution.py:280
  11.3 1.4 %collective-permute-start.5 = (f32[368,128]{1,0:T(8,128)S(1)}, f32[368,128]{1,0:T(8,128)S(1)}, u32[]{:S(2)}, u32[]{:S(2)}) collective-permute-start(f32[368,128]{1,0:T(8,128)S(1)} %pad_select_fusion), channel_id=1, source_target_pairs={{0,3},{1,2},{2,1},{3,0},{4,7},{5,6},{6,5},{7,4},{8,11},{9,10},{10,... | collective-permute-start | bytes 565256 | tf_op jit(solution)/shard_map/ppermute | solution.py:280
  13.5 1.5 %collective-permute-start.1 = (f32[7,32,128]{2,1,0:T(8,128)S(1)}, f32[7,32,128]{2,1,0:T(8,128)S(1)}, u32[]{:S(2)}, u32[]{:S(2)}) collective-permute-start(f32[7,32,128]{2,1,0:T(8,128)S(1)} %collective-permute-done), channel_id=1, source_target_pairs={{0,8},{4,12},{8,0},{12,4},{16,24},{20,28},{24,16},{28,20},{1,9},{5... | collective-permute-start | bytes 344072 | tf_op jit(solution)/shard_map/ppermute | solution.py:298
  15.1 3.2 %collective-permute-done.1 = f32[7,32,128]{2,1,0:T(8,128)S(1)} collective-permute-done((f32[7,32,128]{2,1,0:T(8,128)S(1)}, f32[7,32,128]{2,1,0:T(8,128)S(1)}, u32[]{:S(2)}, u32[]{:S(2)}) %collective-permute-start.1) | collective-permute-done | bytes 114720 | tf_op jit(solution)/shard_map/ppermute | solution.py:298
  18.6 1.3 %collective-permute-done.2.other_ref = f32[14,32,128]{2,1,0:T(8,128)S(1)} collective-permute-done((f32[14,32,128]{2,1,0:T(8,128)S(1)}, f32[14,32,128]{2,1,0:T(8,128)S(1)}, u32[]{:S(2)}, u32[]{:S(2)}) %collective-permute-start.2) | collective-permute-done | bytes 229408 | tf_op jit(solution)/shard_map/ppermute | solution.py:302
  19.9 2.7 %shard_map.65 = (f32[48,32,128]{2,1,0:T(8,128)S(1)}, bf16[256,256]{1,0:T(8,128)(2,1)S(1)}, bf16[256,256]{1,0:T(8,128)(2,1)S(1)}, bf16[256,256]{1,0:T(8,128)(2,1)...) custom-call(s32[3]{0:T(128)S(1)} %pad_add_fusion.scalar_ref, ...), custom_call_target="tpu_custom_call" | custom-call | tf_op jit(solution)/shard_map/pallas_call | solution.py:306
  22.7 1.0 %collective-permute-done.5.refs_3_ = f32[368,128]{1,0:T(8,128)S(1)} collective-permute-done((f32[368,128]{1,0:T(8,128)S(1)}, f32[368,128]{1,0:T(8,128)S(1)}, u32[]{:S(2)}, u32[]{:S(2)}) %collective-permute-start.5) | collective-permute-done | bytes 188448 | tf_op jit(solution)/shard_map/ppermute | solution.py:280
  23.6 1.3 %shard_map.66 = (f32[8,32,128]{2,1,0:T(8,128)S(1)}, f32[8,32,128]{2,1,0:T(8,128)S(1)}, f32[46,32,128]{2,1,0:T(8,128)S(1)}) custom-call(s32[8,128]{1,0:T(8,128)S(1)} %get-tuple-element.26.flag_ref, f32[32,8,128]{2,1,0:T(8,128)S(1)} %get-tuple-element.27.weight_ref, f32[15,8,128]{2,1,0:T(8,128)S(1)} %get-tuple-element.28.splat_ref, f32[1024,128]{1,0:T(8,128)S(1)} %bitcast.10, ...), custom_call_target="tpu_custom_call" | custom-call | tf_op jit(solution)/shard_map/pallas_call | solution.py:326
  25.0 0.7 %shard_map.67 = (f32[8,32,128]{2,1,0:T(8,128)S(1)}, f32[8,32,128]{2,1,0:T(8,128)S(1)}) custom-call(f32[32,8,128]{2,1,0:T(8,128)S(1)} %get-tuple-element.27.weight_ref, f32[15,8,128]{2,1,0:T(8,128)S(1)} %get-tuple-element.28.splat_ref, f32[46,32,128]{2,1,0:T(8,128)S(1)} %get-tuple-element.40.ratio_ref, bf16[256,256]{1,0:T(8,128)(2,1)S(1)} %get-tuple-element.30.rows_high_ref, ...), custom_call_target="tpu_custom_call" | custom-call | flops 536870912 | bytes 2097152 | tf_op jit(solution)/shard_map/pallas_call | solution.py:339
  25.8 0.5 %collective-permute-start.10 = (f32[8,32,128]{2,1,0:T(8,128)S(1)}, f32[8,32,128]{2,1,0:T(8,128)S(1)}, u32[]{:S(2)}, u32[]{:S(2)}) collective-permute-start(f32[8,32,128]{2,1,0:T(8,128)S(1)} %get-tuple-element.42), channel_id=1, source_target_pairs={{0,4},{4,0},{8,12},{12,8},{16,20},{20,16},{24,28},{28,24},{1,5},{5... | collective-permute-start | bytes 393224 | tf_op jit(solution)/shard_map/ppermute | solution.py:347
  26.3 1.6 %collective-permute-start.7 = (f32[8,32,128]{2,1,0:T(8,128)S(1)}, f32[8,32,128]{2,1,0:T(8,128)S(1)}, u32[]{:S(2)}, u32[]{:S(2)}) collective-permute-start(f32[8,32,128]{2,1,0:T(8,128)S(1)} %add.56), channel_id=1, source_target_pairs={{0,8},{4,20},{8,0},{12,28},{16,24},{20,4},{24,16},{28,12},{1,9},{5... | collective-permute-start | bytes 393224 | tf_op jit(solution)/shard_map/ppermute | solution.py:354
  28.0 0.9 %collective-permute-start.11 = (f32[8,32,128]{2,1,0:T(8,128)S(1)}, f32[8,32,128]{2,1,0:T(8,128)S(1)}, u32[]{:S(2)}, u32[]{:S(2)}) collective-permute-start(f32[8,32,128]{2,1,0:T(8,128)S(1)} %add.61), channel_id=1, source_target_pairs={{0,8},{4,20},{8,0},{12,28},{16,24},{20,4},{24,16},{28,12},{1,9},{5... | collective-permute-start | bytes 393224 | tf_op jit(solution)/shard_map/ppermute | solution.py:354
  29.0 2.4 %collective-permute-done.7 = f32[8,32,128]{2,1,0:T(8,128)S(1)} collective-permute-done((f32[8,32,128]{2,1,0:T(8,128)S(1)}, f32[8,32,128]{2,1,0:T(8,128)S(1)}, u32[]{:S(2)}, u32[]{:S(2)}) %collective-permute-start.7) | collective-permute-done | bytes 131104 | tf_op jit(solution)/shard_map/ppermute | solution.py:354
  31.4 1.7 %collective-permute-start.8 = (f32[8,32,128]{2,1,0:T(8,128)S(1)}, f32[8,32,128]{2,1,0:T(8,128)S(1)}, u32[]{:S(2)}, u32[]{:S(2)}) collective-permute-start(f32[8,32,128]{2,1,0:T(8,128)S(1)} %add.57), channel_id=1, source_target_pairs={{0,16},{4,12},{8,24},{12,4},{16,0},{20,28},{24,8},{28,20},{1,17},{... | collective-permute-start | bytes 393224 | tf_op jit(solution)/shard_map/ppermute | solution.py:354
  33.1 1.6 %collective-permute-start.12 = (f32[8,32,128]{2,1,0:T(8,128)S(1)}, f32[8,32,128]{2,1,0:T(8,128)S(1)}, u32[]{:S(2)}, u32[]{:S(2)}) collective-permute-start(f32[8,32,128]{2,1,0:T(8,128)S(1)} %add.62), channel_id=1, source_target_pairs={{0,16},{4,12},{8,24},{12,4},{16,0},{20,28},{24,8},{28,20},{1,17},{... | collective-permute-start | bytes 393224 | tf_op jit(solution)/shard_map/ppermute | solution.py:354
  34.6 1.8 %collective-permute-done.8 = f32[8,32,128]{2,1,0:T(8,128)S(1)} collective-permute-done((f32[8,32,128]{2,1,0:T(8,128)S(1)}, f32[8,32,128]{2,1,0:T(8,128)S(1)}, u32[]{:S(2)}, u32[]{:S(2)}) %collective-permute-start.8) | collective-permute-done | bytes 131104 | tf_op jit(solution)/shard_map/ppermute | solution.py:354
  36.5 1.6 %collective-permute-done.12 = f32[8,32,128]{2,1,0:T(8,128)S(1)} collective-permute-done((f32[8,32,128]{2,1,0:T(8,128)S(1)}, f32[8,32,128]{2,1,0:T(8,128)S(1)}, u32[]{:S(2)}, u32[]{:S(2)}) %collective-permute-start.12) | collective-permute-done | bytes 131104 | tf_op jit(solution)/shard_map/ppermute | solution.py:354
  38.3 1.3 %collective-permute-done.13 = f32[8,32,128]{2,1,0:T(8,128)S(1)} collective-permute-done((f32[8,32,128]{2,1,0:T(8,128)S(1)}, f32[8,32,128]{2,1,0:T(8,128)S(1)}, u32[]{:S(2)}, u32[]{:S(2)}) %collective-permute-start.13) | collective-permute-done | bytes 131104 | tf_op jit(solution)/shard_map/ppermute | solution.py:360
  39.6 0.8 %pad_maximum_fusion = f32[32,32,128]{2,1,0:T(8,128)} fusion(f32[8,32,128]{2,1,0:T(8,128)S(1)} %get-tuple-element.48, f32[8,32,128]{2,1,0:T(8,128)S(1)} %get-tuple-element.47, f32[8,32,128]{2,1,0:T(8,128)S(1)} %get-tuple-element.46, f32[8,32,128]{2,1,0:T(8,128)S(1)} %get-tuple-element.45), kind=kLoop, calls=%fused_computation | loop fusion | flops 393216 | bytes 1048576 | tf_op jit(solution)/shard_map/concatenate | solution.py:362
  (38 shorter events, 1.0 us)
Async XLA Ops:
  0.9 12.5 %collective-permute-start = (f32[7,32,128]{2,1,0:T(8,128)S(1)}, f32[7,32,128]{2,1,0:T(8,128)S(1)}, u32[]{:S(2)}, u32[]{:S(2)}) collective-permute-start(f32[7,32,128]{2,1,0:T(8,128)S(1)} %constant_dynamic-slice_fusion.2), channel_id=1, source_target_pairs={{0,1},{1,0},{2,3},{3,2},{4,4},{5,6},{6,5},{7,7},{8,9},{9,8},{10,11... | collective-permute-start | bytes 344072 | tf_op jit(solution)/shard_map/ppermute | solution.py:293
  5.8 1.0 %copy-start = (f32[1,32,32,128]{3,2,1,0:T(8,128)S(1)}, f32[1,32,32,128]{3,2,1,0:T(8,128)}, u32[]{:S(2)}) copy-start(f32[1,32,32,128]{3,2,1,0:T(8,128)} %param.7) | copy-start | bytes 1572868
  6.9 3.8 %copy-start.1 = (f32[1,32,32,128]{3,2,1,0:T(8,128)S(1)}, f32[1,32,32,128]{3,2,1,0:T(8,128)}, u32[]{:S(2)}) copy-start(f32[1,32,32,128]{3,2,1,0:T(8,128)} %param.7) | copy-start | bytes 1572868
  7.3 16.3 %collective-permute-start.4 = (f32[368,128]{1,0:T(8,128)S(1)}, f32[368,128]{1,0:T(8,128)S(1)}, u32[]{:S(2)}, u32[]{:S(2)}) collective-permute-start(f32[368,128]{1,0:T(8,128)S(1)} %get-tuple-element.34), channel_id=1, source_target_pairs={{0,2},{1,3},{2,0},{3,1},{4,6},{5,7},{6,4},{7,5},{8,10},{9,11},{10,... | collective-permute-start | bytes 565256 | tf_op jit(solution)/shard_map/ppermute | solution.py:280
  10.7 11.9 %collective-permute-start.3 = (f32[368,128]{1,0:T(8,128)S(1)}, f32[368,128]{1,0:T(8,128)S(1)}, u32[]{:S(2)}, u32[]{:S(2)}) collective-permute-start(f32[368,128]{1,0:T(8,128)S(1)} %pad_select_fusion.1), channel_id=1, source_target_pairs={{0,1},{1,0},{2,3},{3,2},{4,5},{5,4},{6,7},{7,6},{8,9},{9,8},{10,11... | collective-permute-start | bytes 565256 | tf_op jit(solution)/shard_map/ppermute | solution.py:280
  11.2 2.1 %copy-start.4 = (f32[1,3,15]{2,0,1:T(1,128)S(1)}, f32[1,3,15]{2,0,1:T(1,128)}, u32[]{:S(2)}) copy-start(f32[1,3,15]{2,0,1:T(1,128)} %param.8) | copy-start | bytes 544
  11.3 8.7 %copy-start.2 = (f32[32,32,128]{2,1,0:T(8,128)S(1)}, f32[32,32,128]{2,1,0:T(8,128)}, u32[]{:S(2)}) copy-start(f32[32,32,128]{2,1,0:T(8,128)} %estimate_ref.1) | copy-start | bytes 1572868
  11.3 12.4 %collective-permute-start.5 = (f32[368,128]{1,0:T(8,128)S(1)}, f32[368,128]{1,0:T(8,128)S(1)}, u32[]{:S(2)}, u32[]{:S(2)}) collective-permute-start(f32[368,128]{1,0:T(8,128)S(1)} %pad_select_fusion), channel_id=1, source_target_pairs={{0,3},{1,2},{2,1},{3,0},{4,7},{5,6},{6,5},{7,4},{8,11},{9,10},{10,... | collective-permute-start | bytes 565256 | tf_op jit(solution)/shard_map/ppermute | solution.py:280
  13.5 4.8 %collective-permute-start.1 = (f32[7,32,128]{2,1,0:T(8,128)S(1)}, f32[7,32,128]{2,1,0:T(8,128)S(1)}, u32[]{:S(2)}, u32[]{:S(2)}) collective-permute-start(f32[7,32,128]{2,1,0:T(8,128)S(1)} %collective-permute-done), channel_id=1, source_target_pairs={{0,8},{4,12},{8,0},{12,4},{16,24},{20,28},{24,16},{28,20},{1,9},{5... | collective-permute-start | bytes 344072 | tf_op jit(solution)/shard_map/ppermute | solution.py:298
  18.3 1.6 %collective-permute-start.2 = (f32[14,32,128]{2,1,0:T(8,128)S(1)}, f32[14,32,128]{2,1,0:T(8,128)S(1)}, u32[]{:S(2)}, u32[]{:S(2)}) collective-permute-start(f32[14,32,128]{2,1,0:T(8,128)S(1)} %pad_maximum_fusion.1.near_ref), channel_id=1, source_target_pairs={{0,4},{4,0},{8,12},{12,8},{16,20},{20,16},{24,28},{28,24},{1,5},{5... | collective-permute-start | bytes 688136 | tf_op jit(solution)/shard_map/ppermute | solution.py:302
  18.6 1.3 %copy-start.3 = (s32[1,32]{1,0:T(1,128)S(1)}, s32[1,32]{1,0:T(1,128)}, u32[]{:S(2)}) copy-start(s32[1,32]{1,0:T(1,128)} %param.11) | copy-start | bytes 388
  24.9 1.4 %collective-permute-start.6 = (f32[8,32,128]{2,1,0:T(8,128)S(1)}, f32[8,32,128]{2,1,0:T(8,128)S(1)}, u32[]{:S(2)}, u32[]{:S(2)}) collective-permute-start(f32[8,32,128]{2,1,0:T(8,128)S(1)} %get-tuple-element.38), channel_id=1, source_target_pairs={{0,4},{4,0},{8,12},{12,8},{16,20},{20,16},{24,28},{28,24},{1,5},{5... | collective-permute-start | bytes 393224 | tf_op jit(solution)/shard_map/ppermute | solution.py:336
  25.8 2.2 %collective-permute-start.10 = (f32[8,32,128]{2,1,0:T(8,128)S(1)}, f32[8,32,128]{2,1,0:T(8,128)S(1)}, u32[]{:S(2)}, u32[]{:S(2)}) collective-permute-start(f32[8,32,128]{2,1,0:T(8,128)S(1)} %get-tuple-element.42), channel_id=1, source_target_pairs={{0,4},{4,0},{8,12},{12,8},{16,20},{20,16},{24,28},{28,24},{1,5},{5... | collective-permute-start | bytes 393224 | tf_op jit(solution)/shard_map/ppermute | solution.py:347
  26.3 5.0 %collective-permute-start.7 = (f32[8,32,128]{2,1,0:T(8,128)S(1)}, f32[8,32,128]{2,1,0:T(8,128)S(1)}, u32[]{:S(2)}, u32[]{:S(2)}) collective-permute-start(f32[8,32,128]{2,1,0:T(8,128)S(1)} %add.56), channel_id=1, source_target_pairs={{0,8},{4,20},{8,0},{12,28},{16,24},{20,4},{24,16},{28,12},{1,9},{5... | collective-permute-start | bytes 393224 | tf_op jit(solution)/shard_map/ppermute | solution.py:354
  28.0 5.1 %collective-permute-start.11 = (f32[8,32,128]{2,1,0:T(8,128)S(1)}, f32[8,32,128]{2,1,0:T(8,128)S(1)}, u32[]{:S(2)}, u32[]{:S(2)}) collective-permute-start(f32[8,32,128]{2,1,0:T(8,128)S(1)} %add.61), channel_id=1, source_target_pairs={{0,8},{4,20},{8,0},{12,28},{16,24},{20,4},{24,16},{28,12},{1,9},{5... | collective-permute-start | bytes 393224 | tf_op jit(solution)/shard_map/ppermute | solution.py:354
  31.4 5.0 %collective-permute-start.8 = (f32[8,32,128]{2,1,0:T(8,128)S(1)}, f32[8,32,128]{2,1,0:T(8,128)S(1)}, u32[]{:S(2)}, u32[]{:S(2)}) collective-permute-start(f32[8,32,128]{2,1,0:T(8,128)S(1)} %add.57), channel_id=1, source_target_pairs={{0,16},{4,12},{8,24},{12,4},{16,0},{20,28},{24,8},{28,20},{1,17},{... | collective-permute-start | bytes 393224 | tf_op jit(solution)/shard_map/ppermute | solution.py:354
  33.1 5.0 %collective-permute-start.12 = (f32[8,32,128]{2,1,0:T(8,128)S(1)}, f32[8,32,128]{2,1,0:T(8,128)S(1)}, u32[]{:S(2)}, u32[]{:S(2)}) collective-permute-start(f32[8,32,128]{2,1,0:T(8,128)S(1)} %add.62), channel_id=1, source_target_pairs={{0,16},{4,12},{8,24},{12,4},{16,0},{20,28},{24,8},{28,20},{1,17},{... | collective-permute-start | bytes 393224 | tf_op jit(solution)/shard_map/ppermute | solution.py:354
  36.5 1.8 %collective-permute-start.9 = (f32[8,32,128]{2,1,0:T(8,128)S(1)}, f32[8,32,128]{2,1,0:T(8,128)S(1)}, u32[]{:S(2)}, u32[]{:S(2)}) collective-permute-start(f32[8,32,128]{2,1,0:T(8,128)S(1)} %exponential_multiply_fusion.1), channel_id=1, source_target_pairs={{0,4},{4,0},{8,12},{12,8},{16,20},{20,16},{24,28},{28,24},{1,5},{5... | collective-permute-start | bytes 393224 | tf_op jit(solution)/shard_map/ppermute | solution.py:360
  38.2 1.4 %collective-permute-start.13 = (f32[8,32,128]{2,1,0:T(8,128)S(1)}, f32[8,32,128]{2,1,0:T(8,128)S(1)}, u32[]{:S(2)}, u32[]{:S(2)}) collective-permute-start(f32[8,32,128]{2,1,0:T(8,128)S(1)} %exponential_multiply_fusion), channel_id=1, source_target_pairs={{0,4},{4,0},{8,12},{12,8},{16,20},{20,16},{24,28},{28,24},{1,5},{5... | collective-permute-start | bytes 393224 | tf_op jit(solution)/shard_map/ppermute | solution.py:360

commit v7 on v6

--- a/solution.py
+++ b/solution.py
@@ -12,7 +12,7 @@
 WIDE = 256
 VMEM = pl.BlockSpec(memory_space=pltpu.VMEM)
 SMEM = pl.BlockSpec(memory_space=pltpu.SMEM)
-COST = pl.CostEstimate(flops=2**29, bytes_accessed=2**21, transcendentals=2**16)
+COST = pl.CostEstimate(flops=2**29, bytes_accessed=2**23, transcendentals=2**16)
 PARAMS = pltpu.CompilerParams(vmem_limit_bytes=40 * 1024 * 1024)
 
 
@@ -256,6 +256,7 @@
             pltpu.VMEM(((nx + 2 * reach) * ROWS, LANES), jnp.float32),
             pltpu.VMEM((zb * ny, LANES), jnp.float32),
         ],
+        cost_estimate=COST,
         compiler_params=PARAMS,
     )(stack))
     late_perm, _ = lax.optimization_barrier((perm, packed[1]))
@@ -317,6 +318,7 @@
         in_specs=[SMEM] * 3 + [VMEM] * 3,
         out_specs=[VMEM] * 7,
         scratch_shapes=[pltpu.VMEM((planes + 2 * reach, ny, nx), jnp.float32)],
+        cost_estimate=COST,
         compiler_params=PARAMS,
     )(scalars, joined_taps, visible[0], estimate, near, other)
 
@@ -331,6 +333,7 @@
         scratch_shapes=[
             pltpu.VMEM((count, (zb + 2 * reach) * ROWS, LANES), jnp.float32),
         ],
+        cost_estimate=COST,
         compiler_params=PARAMS,
     )(flags, weight, splats, stack, inverse, *matrices, *blocks)
     total = [first[1] + lax.ppermute(first[0], "view", swap)]
@@ -342,7 +345,7 @@
             in_specs=[VMEM] * 6,
             out_specs=[VMEM] * 2,
             cost_estimate=COST,
-            compiler_params=PARAMS,
+        compiler_params=PARAMS,
         )(held, splats, first[2], *matrices)
         total.append(keep + lax.ppermute(send, "view", swap))
 

time: 40.7 us -> 40.7 us (level)
    ppermute x3, waiting for transfers between devices: 0.97 us -> 1.63 us  [shards(): lax.ppermute(packed[k], 'bulk', [(i, i ^ k) for i in range(count)])]
    ppermute x1, waiting for transfers between devices: 1.3 us -> 0.66 us  [shards(): other = lax.ppermute(near, 'view', swap)]
where the time goes in v7:
time: 40.7 us; the launch traced here: 40.4 us
  starting transfers between devices  17.7 us (43%)
  waiting for transfers between devices  12.6 us (31%)
  Pallas kernels  5.19 us (13%)
  local copies, waits for them, and re-layouts  2.01 us (5%)
  between operations  1.48 us (4%)
  other arithmetic  1.42 us (3%)
    ppermute x4, starting transfers between devices, shards(): lax.ppermute(total[part], 'view', [(i, i ^ flips[i % 2]) for i in range(v...  5.82 us
    ppermute x4, waiting for transfers between devices, shards(): lax.ppermute(total[part], 'view', [(i, i ^ flips[i % 2]) for i in range(v...  5.78 us
    ppermute x1, starting transfers between devices, shards(): lax.ppermute(lax.dynamic_slice_in_dim(estimate, start, reach, 0), ('view'...  4.93 us
    ppermute x3, starting transfers between devices, shards(): lax.ppermute(packed[k], 'bulk', [(i, i ^ k) for i in range(count)])  4.58 us
    ppermute x1, waiting for transfers between devices, shards(): across = lax.ppermute(quarter, 'view', [(v, v ^ 2) for v in range(views)])  3.2 us
    pallas_call x1, Pallas kernels, shards(): pl.pallas_call(functools.partial(forward_kernel, zb, ny, nx, planes), out...  2.75 us
    ppermute x3, waiting for transfers between devices, shards(): lax.ppermute(packed[k], 'bulk', [(i, i ^ k) for i in range(count)])  1.63 us
    ppermute x1, starting transfers between devices, shards(): across = lax.ppermute(quarter, 'view', [(v, v ^ 2) for v in range(views)])  1.55 us
  transfers between devices with their start and end apart: 14, of which 7 were waited for; matrix products, arithmetic and copies ran while one was open for 2% of the time, Pallas kernels for 10%

profile of v7, /device:TPU:0, one launch (start us, length us, event | category | flops | bytes accessed | tf_op | source)
XLA Modules:
  0.0 40.4 jit_solution(96511522568618076)
XLA Ops:
  0.0 0.9 %constant_dynamic-slice_fusion.2 = f32[7,32,128]{2,1,0:T(8,128)S(1)} fusion(f32[32,32,128]{2,1,0:T(8,128)} %estimate_ref.1, s32[]{:T(128)S(6)} %select_n.102), kind=kLoop, calls=%fused_computation.15 | loop fusion | bytes 229380 | tf_op jit(solution)/shard_map/dynamic_slice | solution.py:295
  0.9 4.9 %collective-permute-start = (f32[7,32,128]{2,1,0:T(8,128)S(1)}, f32[7,32,128]{2,1,0:T(8,128)S(1)}, u32[]{:S(2)}, u32[]{:S(2)}) collective-permute-start(f32[7,32,128]{2,1,0:T(8,128)S(1)} %constant_dynamic-slice_fusion.2), channel_id=1, source_target_pairs={{0,1},{1,0},{2,3},{3,2},{4,4},{5,6},{6,5},{7,7},{8,9},{9,8},{10,11... | collective-permute-start | bytes 344072 | tf_op jit(solution)/shard_map/ppermute | solution.py:294
  5.9 1.0 %copy-done = f32[1,32,32,128]{3,2,1,0:T(8,128)S(1)} copy-done((f32[1,32,32,128]{3,2,1,0:T(8,128)S(1)}, f32[1,32,32,128]{3,2,1,0:T(8,128)}, u32[]{:S(2)}) %copy-start) | copy-done | bytes 524312
  6.9 0.4 %shard_map.64 = (f32[368,128]{1,0:T(8,128)S(1)}, f32[368,128]{1,0:T(8,128)S(1)}, f32[368,128]{1,0:T(8,128)S(1)}, f32[368,128]{1,0:T(8,128)S(1)}) custom-call(f32[1024,128]{1,0:T(8,128)S(1)} %bitcast.8), custom_call_target="tpu_custom_call" | custom-call | flops 536870912 | bytes 8388608 | tf_op jit(solution)/shard_map/pallas_call | solution.py:250
  7.3 2.7 %collective-permute-start.4 = (f32[368,128]{1,0:T(8,128)S(1)}, f32[368,128]{1,0:T(8,128)S(1)}, u32[]{:S(2)}, u32[]{:S(2)}) collective-permute-start(f32[368,128]{1,0:T(8,128)S(1)} %get-tuple-element.34), channel_id=1, source_target_pairs={{0,2},{1,3},{2,0},{3,1},{4,6},{5,7},{6,4},{7,5},{8,10},{9,11},{10,... | collective-permute-start | bytes 565256 | tf_op jit(solution)/shard_map/ppermute | solution.py:281
  10.7 0.5 %collective-permute-start.3 = (f32[368,128]{1,0:T(8,128)S(1)}, f32[368,128]{1,0:T(8,128)S(1)}, u32[]{:S(2)}, u32[]{:S(2)}) collective-permute-start(f32[368,128]{1,0:T(8,128)S(1)} %pad_select_fusion.1), channel_id=1, source_target_pairs={{0,1},{1,0},{2,3},{3,2},{4,5},{5,4},{6,7},{7,6},{8,9},{9,8},{10,11... | collective-permute-start | bytes 565256 | tf_op jit(solution)/shard_map/ppermute | solution.py:281
  11.3 1.4 %collective-permute-start.5 = (f32[368,128]{1,0:T(8,128)S(1)}, f32[368,128]{1,0:T(8,128)S(1)}, u32[]{:S(2)}, u32[]{:S(2)}) collective-permute-start(f32[368,128]{1,0:T(8,128)S(1)} %pad_select_fusion), channel_id=1, source_target_pairs={{0,3},{1,2},{2,1},{3,0},{4,7},{5,6},{6,5},{7,4},{8,11},{9,10},{10,... | collective-permute-start | bytes 565256 | tf_op jit(solution)/shard_map/ppermute | solution.py:281
  12.8 1.5 %collective-permute-start.1 = (f32[7,32,128]{2,1,0:T(8,128)S(1)}, f32[7,32,128]{2,1,0:T(8,128)S(1)}, u32[]{:S(2)}, u32[]{:S(2)}) collective-permute-start(f32[7,32,128]{2,1,0:T(8,128)S(1)} %collective-permute-done), channel_id=1, source_target_pairs={{0,8},{4,12},{8,0},{12,4},{16,24},{20,28},{24,16},{28,20},{1,9},{5... | collective-permute-start | bytes 344072 | tf_op jit(solution)/shard_map/ppermute | solution.py:299
  14.4 3.2 %collective-permute-done.1 = f32[7,32,128]{2,1,0:T(8,128)S(1)} collective-permute-done((f32[7,32,128]{2,1,0:T(8,128)S(1)}, f32[7,32,128]{2,1,0:T(8,128)S(1)}, u32[]{:S(2)}, u32[]{:S(2)}) %collective-permute-start.1) | collective-permute-done | bytes 114720 | tf_op jit(solution)/shard_map/ppermute | solution.py:299
  18.6 0.7 %collective-permute-done.2.other_ref = f32[14,32,128]{2,1,0:T(8,128)S(1)} collective-permute-done((f32[14,32,128]{2,1,0:T(8,128)S(1)}, f32[14,32,128]{2,1,0:T(8,128)S(1)}, u32[]{:S(2)}, u32[]{:S(2)}) %collective-permute-start.2) | collective-permute-done | bytes 229408 | tf_op jit(solution)/shard_map/ppermute | solution.py:303
  19.2 2.7 %shard_map.65 = (f32[48,32,128]{2,1,0:T(8,128)S(1)}, bf16[256,256]{1,0:T(8,128)(2,1)S(1)}, bf16[256,256]{1,0:T(8,128)(2,1)S(1)}, bf16[256,256]{1,0:T(8,128)(2,1)...) custom-call(s32[3]{0:T(128)S(1)} %pad_add_fusion.scalar_ref, ...), custom_call_target="tpu_custom_call" | custom-call | flops 536870912 | bytes 8388608 | tf_op jit(solution)/shard_map/pallas_call | solution.py:307
  22.0 1.6 %collective-permute-done.5.refs_3_ = f32[368,128]{1,0:T(8,128)S(1)} collective-permute-done((f32[368,128]{1,0:T(8,128)S(1)}, f32[368,128]{1,0:T(8,128)S(1)}, u32[]{:S(2)}, u32[]{:S(2)}) %collective-permute-start.5) | collective-permute-done | bytes 188448 | tf_op jit(solution)/shard_map/ppermute | solution.py:281
  23.6 1.3 %shard_map.66 = (f32[8,32,128]{2,1,0:T(8,128)S(1)}, f32[8,32,128]{2,1,0:T(8,128)S(1)}, f32[46,32,128]{2,1,0:T(8,128)S(1)}) custom-call(s32[8,128]{1,0:T(8,128)S(1)} %get-tuple-element.26.flag_ref, f32[32,8,128]{2,1,0:T(8,128)S(1)} %get-tuple-element.27.weight_ref, f32[15,8,128]{2,1,0:T(8,128)S(1)} %get-tuple-element.28.splat_ref, f32[1024,128]{1,0:T(8,128)S(1)} %bitcast.10, ...), custom_call_target="tpu_custom_call" | custom-call | flops 536870912 | bytes 8388608 | tf_op jit(solution)/shard_map/pallas_call | solution.py:328
  25.0 0.7 %shard_map.67 = (f32[8,32,128]{2,1,0:T(8,128)S(1)}, f32[8,32,128]{2,1,0:T(8,128)S(1)}) custom-call(f32[32,8,128]{2,1,0:T(8,128)S(1)} %get-tuple-element.27.weight_ref, f32[15,8,128]{2,1,0:T(8,128)S(1)} %get-tuple-element.28.splat_ref, f32[46,32,128]{2,1,0:T(8,128)S(1)} %get-tuple-element.40.ratio_ref, bf16[256,256]{1,0:T(8,128)(2,1)S(1)} %get-tuple-element.30.rows_high_ref, ...), custom_call_target="tpu_custom_call" | custom-call | flops 536870912 | bytes 8388608 | tf_op jit(solution)/shard_map/pallas_call | solution.py:342
  25.8 0.5 %collective-permute-start.10 = (f32[8,32,128]{2,1,0:T(8,128)S(1)}, f32[8,32,128]{2,1,0:T(8,128)S(1)}, u32[]{:S(2)}, u32[]{:S(2)}) collective-permute-start(f32[8,32,128]{2,1,0:T(8,128)S(1)} %get-tuple-element.42), channel_id=1, source_target_pairs={{0,4},{4,0},{8,12},{12,8},{16,20},{20,16},{24,28},{28,24},{1,5},{5... | collective-permute-start | bytes 393224 | tf_op jit(solution)/shard_map/ppermute | solution.py:350
  26.3 1.6 %collective-permute-start.7 = (f32[8,32,128]{2,1,0:T(8,128)S(1)}, f32[8,32,128]{2,1,0:T(8,128)S(1)}, u32[]{:S(2)}, u32[]{:S(2)}) collective-permute-start(f32[8,32,128]{2,1,0:T(8,128)S(1)} %add.56), channel_id=1, source_target_pairs={{0,8},{4,20},{8,0},{12,28},{16,24},{20,4},{24,16},{28,12},{1,9},{5... | collective-permute-start | bytes 393224 | tf_op jit(solution)/shard_map/ppermute | solution.py:357
  28.0 0.9 %collective-permute-start.11 = (f32[8,32,128]{2,1,0:T(8,128)S(1)}, f32[8,32,128]{2,1,0:T(8,128)S(1)}, u32[]{:S(2)}, u32[]{:S(2)}) collective-permute-start(f32[8,32,128]{2,1,0:T(8,128)S(1)} %add.61), channel_id=1, source_target_pairs={{0,8},{4,20},{8,0},{12,28},{16,24},{20,4},{24,16},{28,12},{1,9},{5... | collective-permute-start | bytes 393224 | tf_op jit(solution)/shard_map/ppermute | solution.py:357
  29.0 2.4 %collective-permute-done.7 = f32[8,32,128]{2,1,0:T(8,128)S(1)} collective-permute-done((f32[8,32,128]{2,1,0:T(8,128)S(1)}, f32[8,32,128]{2,1,0:T(8,128)S(1)}, u32[]{:S(2)}, u32[]{:S(2)}) %collective-permute-start.7) | collective-permute-done | bytes 131104 | tf_op jit(solution)/shard_map/ppermute | solution.py:357
  31.4 1.7 %collective-permute-start.8 = (f32[8,32,128]{2,1,0:T(8,128)S(1)}, f32[8,32,128]{2,1,0:T(8,128)S(1)}, u32[]{:S(2)}, u32[]{:S(2)}) collective-permute-start(f32[8,32,128]{2,1,0:T(8,128)S(1)} %add.57), channel_id=1, source_target_pairs={{0,16},{4,12},{8,24},{12,4},{16,0},{20,28},{24,8},{28,20},{1,17},{... | collective-permute-start | bytes 393224 | tf_op jit(solution)/shard_map/ppermute | solution.py:357
  33.1 1.6 %collective-permute-start.12 = (f32[8,32,128]{2,1,0:T(8,128)S(1)}, f32[8,32,128]{2,1,0:T(8,128)S(1)}, u32[]{:S(2)}, u32[]{:S(2)}) collective-permute-start(f32[8,32,128]{2,1,0:T(8,128)S(1)} %add.62), channel_id=1, source_target_pairs={{0,16},{4,12},{8,24},{12,4},{16,0},{20,28},{24,8},{28,20},{1,17},{... | collective-permute-start | bytes 393224 | tf_op jit(solution)/shard_map/ppermute | solution.py:357
  34.6 1.8 %collective-permute-done.8 = f32[8,32,128]{2,1,0:T(8,128)S(1)} collective-permute-done((f32[8,32,128]{2,1,0:T(8,128)S(1)}, f32[8,32,128]{2,1,0:T(8,128)S(1)}, u32[]{:S(2)}, u32[]{:S(2)}) %collective-permute-start.8) | collective-permute-done | bytes 131104 | tf_op jit(solution)/shard_map/ppermute | solution.py:357
  36.5 1.6 %collective-permute-done.12 = f32[8,32,128]{2,1,0:T(8,128)S(1)} collective-permute-done((f32[8,32,128]{2,1,0:T(8,128)S(1)}, f32[8,32,128]{2,1,0:T(8,128)S(1)}, u32[]{:S(2)}, u32[]{:S(2)}) %collective-permute-start.12) | collective-permute-done | bytes 131104 | tf_op jit(solution)/shard_map/ppermute | solution.py:357
  38.3 1.3 %collective-permute-done.13 = f32[8,32,128]{2,1,0:T(8,128)S(1)} collective-permute-done((f32[8,32,128]{2,1,0:T(8,128)S(1)}, f32[8,32,128]{2,1,0:T(8,128)S(1)}, u32[]{:S(2)}, u32[]{:S(2)}) %collective-permute-start.13) | collective-permute-done | bytes 131104 | tf_op jit(solution)/shard_map/ppermute | solution.py:363
  39.6 0.8 %pad_maximum_fusion = f32[32,32,128]{2,1,0:T(8,128)} fusion(f32[8,32,128]{2,1,0:T(8,128)S(1)} %get-tuple-element.48, f32[8,32,128]{2,1,0:T(8,128)S(1)} %get-tuple-element.47, f32[8,32,128]{2,1,0:T(8,128)S(1)} %get-tuple-element.46, f32[8,32,128]{2,1,0:T(8,128)S(1)} %get-tuple-element.45), kind=kLoop, calls=%fused_computation | loop fusion | flops 393216 | bytes 1048576 | tf_op jit(solution)/shard_map/concatenate | solution.py:365
  (38 shorter events, 1.0 us)
Async XLA Ops:
  0.9 11.9 %collective-permute-start = (f32[7,32,128]{2,1,0:T(8,128)S(1)}, f32[7,32,128]{2,1,0:T(8,128)S(1)}, u32[]{:S(2)}, u32[]{:S(2)}) collective-permute-start(f32[7,32,128]{2,1,0:T(8,128)S(1)} %constant_dynamic-slice_fusion.2), channel_id=1, source_target_pairs={{0,1},{1,0},{2,3},{3,2},{4,4},{5,6},{6,5},{7,7},{8,9},{9,8},{10,11... | collective-permute-start | bytes 344072 | tf_op jit(solution)/shard_map/ppermute | solution.py:294
  5.8 1.0 %copy-start = (f32[1,32,32,128]{3,2,1,0:T(8,128)S(1)}, f32[1,32,32,128]{3,2,1,0:T(8,128)}, u32[]{:S(2)}) copy-start(f32[1,32,32,128]{3,2,1,0:T(8,128)} %param.7) | copy-start | bytes 1572868
  6.9 3.8 %copy-start.1 = (f32[1,32,32,128]{3,2,1,0:T(8,128)S(1)}, f32[1,32,32,128]{3,2,1,0:T(8,128)}, u32[]{:S(2)}) copy-start(f32[1,32,32,128]{3,2,1,0:T(8,128)} %param.7) | copy-start | bytes 1572868
  7.3 16.3 %collective-permute-start.4 = (f32[368,128]{1,0:T(8,128)S(1)}, f32[368,128]{1,0:T(8,128)S(1)}, u32[]{:S(2)}, u32[]{:S(2)}) collective-permute-start(f32[368,128]{1,0:T(8,128)S(1)} %get-tuple-element.34), channel_id=1, source_target_pairs={{0,2},{1,3},{2,0},{3,1},{4,6},{5,7},{6,4},{7,5},{8,10},{9,11},{10,... | collective-permute-start | bytes 565256 | tf_op jit(solution)/shard_map/ppermute | solution.py:281
  10.7 11.3 %collective-permute-start.3 = (f32[368,128]{1,0:T(8,128)S(1)}, f32[368,128]{1,0:T(8,128)S(1)}, u32[]{:S(2)}, u32[]{:S(2)}) collective-permute-start(f32[368,128]{1,0:T(8,128)S(1)} %pad_select_fusion.1), channel_id=1, source_target_pairs={{0,1},{1,0},{2,3},{3,2},{4,5},{5,4},{6,7},{7,6},{8,9},{9,8},{10,11... | collective-permute-start | bytes 565256 | tf_op jit(solution)/shard_map/ppermute | solution.py:281
  11.2 1.5 %copy-start.4 = (f32[1,3,15]{2,0,1:T(1,128)S(1)}, f32[1,3,15]{2,0,1:T(1,128)}, u32[]{:S(2)}) copy-start(f32[1,3,15]{2,0,1:T(1,128)} %param.8) | copy-start | bytes 544
  11.3 8.0 %copy-start.2 = (f32[32,32,128]{2,1,0:T(8,128)S(1)}, f32[32,32,128]{2,1,0:T(8,128)}, u32[]{:S(2)}) copy-start(f32[32,32,128]{2,1,0:T(8,128)} %estimate_ref.1) | copy-start | bytes 1572868
  11.3 12.4 %collective-permute-start.5 = (f32[368,128]{1,0:T(8,128)S(1)}, f32[368,128]{1,0:T(8,128)S(1)}, u32[]{:S(2)}, u32[]{:S(2)}) collective-permute-start(f32[368,128]{1,0:T(8,128)S(1)} %pad_select_fusion), channel_id=1, source_target_pairs={{0,3},{1,2},{2,1},{3,0},{4,7},{5,6},{6,5},{7,4},{8,11},{9,10},{10,... | collective-permute-start | bytes 565256 | tf_op jit(solution)/shard_map/ppermute | solution.py:281
  12.8 4.8 %collective-permute-start.1 = (f32[7,32,128]{2,1,0:T(8,128)S(1)}, f32[7,32,128]{2,1,0:T(8,128)S(1)}, u32[]{:S(2)}, u32[]{:S(2)}) collective-permute-start(f32[7,32,128]{2,1,0:T(8,128)S(1)} %collective-permute-done), channel_id=1, source_target_pairs={{0,8},{4,12},{8,0},{12,4},{16,24},{20,28},{24,16},{28,20},{1,9},{5... | collective-permute-start | bytes 344072 | tf_op jit(solution)/shard_map/ppermute | solution.py:299
  17.7 1.6 %collective-permute-start.2 = (f32[14,32,128]{2,1,0:T(8,128)S(1)}, f32[14,32,128]{2,1,0:T(8,128)S(1)}, u32[]{:S(2)}, u32[]{:S(2)}) collective-permute-start(f32[14,32,128]{2,1,0:T(8,128)S(1)} %pad_maximum_fusion.1.near_ref), channel_id=1, source_target_pairs={{0,4},{4,0},{8,12},{12,8},{16,20},{20,16},{24,28},{28,24},{1,5},{5... | collective-permute-start | bytes 688136 | tf_op jit(solution)/shard_map/ppermute | solution.py:303
  18.6 0.7 %copy-start.3 = (s32[1,32]{1,0:T(1,128)S(1)}, s32[1,32]{1,0:T(1,128)}, u32[]{:S(2)}) copy-start(s32[1,32]{1,0:T(1,128)} %param.11) | copy-start | bytes 388
  24.9 1.4 %collective-permute-start.6 = (f32[8,32,128]{2,1,0:T(8,128)S(1)}, f32[8,32,128]{2,1,0:T(8,128)S(1)}, u32[]{:S(2)}, u32[]{:S(2)}) collective-permute-start(f32[8,32,128]{2,1,0:T(8,128)S(1)} %get-tuple-element.38), channel_id=1, source_target_pairs={{0,4},{4,0},{8,12},{12,8},{16,20},{20,16},{24,28},{28,24},{1,5},{5... | collective-permute-start | bytes 393224 | tf_op jit(solution)/shard_map/ppermute | solution.py:339
  25.8 2.2 %collective-permute-start.10 = (f32[8,32,128]{2,1,0:T(8,128)S(1)}, f32[8,32,128]{2,1,0:T(8,128)S(1)}, u32[]{:S(2)}, u32[]{:S(2)}) collective-permute-start(f32[8,32,128]{2,1,0:T(8,128)S(1)} %get-tuple-element.42), channel_id=1, source_target_pairs={{0,4},{4,0},{8,12},{12,8},{16,20},{20,16},{24,28},{28,24},{1,5},{5... | collective-permute-start | bytes 393224 | tf_op jit(solution)/shard_map/ppermute | solution.py:350
  26.3 5.0 %collective-permute-start.7 = (f32[8,32,128]{2,1,0:T(8,128)S(1)}, f32[8,32,128]{2,1,0:T(8,128)S(1)}, u32[]{:S(2)}, u32[]{:S(2)}) collective-permute-start(f32[8,32,128]{2,1,0:T(8,128)S(1)} %add.56), channel_id=1, source_target_pairs={{0,8},{4,20},{8,0},{12,28},{16,24},{20,4},{24,16},{28,12},{1,9},{5... | collective-permute-start | bytes 393224 | tf_op jit(solution)/shard_map/ppermute | solution.py:357
  28.0 5.1 %collective-permute-start.11 = (f32[8,32,128]{2,1,0:T(8,128)S(1)}, f32[8,32,128]{2,1,0:T(8,128)S(1)}, u32[]{:S(2)}, u32[]{:S(2)}) collective-permute-start(f32[8,32,128]{2,1,0:T(8,128)S(1)} %add.61), channel_id=1, source_target_pairs={{0,8},{4,20},{8,0},{12,28},{16,24},{20,4},{24,16},{28,12},{1,9},{5... | collective-permute-start | bytes 393224 | tf_op jit(solution)/shard_map/ppermute | solution.py:357
  31.4 5.0 %collective-permute-start.8 = (f32[8,32,128]{2,1,0:T(8,128)S(1)}, f32[8,32,128]{2,1,0:T(8,128)S(1)}, u32[]{:S(2)}, u32[]{:S(2)}) collective-permute-start(f32[8,32,128]{2,1,0:T(8,128)S(1)} %add.57), channel_id=1, source_target_pairs={{0,16},{4,12},{8,24},{12,4},{16,0},{20,28},{24,8},{28,20},{1,17},{... | collective-permute-start | bytes 393224 | tf_op jit(solution)/shard_map/ppermute | solution.py:357
  33.1 5.0 %collective-permute-start.12 = (f32[8,32,128]{2,1,0:T(8,128)S(1)}, f32[8,32,128]{2,1,0:T(8,128)S(1)}, u32[]{:S(2)}, u32[]{:S(2)}) collective-permute-start(f32[8,32,128]{2,1,0:T(8,128)S(1)} %add.62), channel_id=1, source_target_pairs={{0,16},{4,12},{8,24},{12,4},{16,0},{20,28},{24,8},{28,20},{1,17},{... | collective-permute-start | bytes 393224 | tf_op jit(solution)/shard_map/ppermute | solution.py:357
  36.5 1.8 %collective-permute-start.9 = (f32[8,32,128]{2,1,0:T(8,128)S(1)}, f32[8,32,128]{2,1,0:T(8,128)S(1)}, u32[]{:S(2)}, u32[]{:S(2)}) collective-permute-start(f32[8,32,128]{2,1,0:T(8,128)S(1)} %exponential_multiply_fusion.1), channel_id=1, source_target_pairs={{0,4},{4,0},{8,12},{12,8},{16,20},{20,16},{24,28},{28,24},{1,5},{5... | collective-permute-start | bytes 393224 | tf_op jit(solution)/shard_map/ppermute | solution.py:363
  38.2 1.4 %collective-permute-start.13 = (f32[8,32,128]{2,1,0:T(8,128)S(1)}, f32[8,32,128]{2,1,0:T(8,128)S(1)}, u32[]{:S(2)}, u32[]{:S(2)}) collective-permute-start(f32[8,32,128]{2,1,0:T(8,128)S(1)} %exponential_multiply_fusion), channel_id=1, source_target_pairs={{0,4},{4,0},{8,12},{12,8},{16,20},{20,16},{24,28},{28,24},{1,5},{5... | collective-permute-start | bytes 393224 | tf_op jit(solution)/shard_map/ppermute | solution.py:363

commit v8 on v6

--- a/solution.py
+++ b/solution.py
@@ -350,7 +350,7 @@
     result = []
     for part in range(parts):
         for step in range(bits):
-            flips = [2 << step, 2 << ((step + bits - 1) % bits)]
+            flips = [2 << ((step + bits - 1) % bits), 2 << step]
             total[part] = total[part] + lax.ppermute(
                 total[part], "view", [(i, i ^ flips[i % 2]) for i in range(views)]
             )

time: 40.7 us -> 40.7 us (level)
  no operation moved by 1% of the time
where the time goes in v8:
time: 40.7 us; the launch traced here: 40.4 us
  starting transfers between devices  17.7 us (43%)
  waiting for transfers between devices  12.6 us (31%)
  Pallas kernels  5.19 us (13%)
  local copies, waits for them, and re-layouts  2.01 us (5%)
  between operations  1.49 us (4%)
  other arithmetic  1.42 us (3%)
    ppermute x4, starting transfers between devices, shards(): lax.ppermute(total[part], 'view', [(i, i ^ flips[i % 2]) for i in range(v...  5.82 us
    ppermute x4, waiting for transfers between devices, shards(): lax.ppermute(total[part], 'view', [(i, i ^ flips[i % 2]) for i in range(v...  5.78 us
    ppermute x1, starting transfers between devices, shards(): lax.ppermute(lax.dynamic_slice_in_dim(estimate, start, reach, 0), ('view'...  4.93 us
    ppermute x3, starting transfers between devices, shards(): lax.ppermute(packed[k], 'bulk', [(i, i ^ k) for i in range(count)])  4.58 us
    ppermute x1, waiting for transfers between devices, shards(): across = lax.ppermute(quarter, 'view', [(v, v ^ 2) for v in range(views)])  3.23 us
    pallas_call x1, Pallas kernels, shards(): pl.pallas_call(functools.partial(forward_kernel, zb, ny, nx, planes), out...  2.74 us
    ppermute x1, starting transfers between devices, shards(): across = lax.ppermute(quarter, 'view', [(v, v ^ 2) for v in range(views)])  1.55 us
    ppermute x2, waiting for transfers between devices, shards(): their = lax.ppermute(own, 'view', swap)  1.3 us
  transfers between devices with their start and end apart: 14, of which 7 were waited for; matrix products, arithmetic and copies ran while one was open for 2% of the time, Pallas kernels for 10%

profile of v8, /device:TPU:0, one launch (start us, length us, event | category | flops | bytes accessed | tf_op | source)
XLA Modules:
  0.0 40.4 jit_solution(18125052728772580549)
XLA Ops:
  0.0 0.9 %constant_dynamic-slice_fusion.2 = f32[7,32,128]{2,1,0:T(8,128)S(1)} fusion(f32[32,32,128]{2,1,0:T(8,128)} %estimate_ref.1, s32[]{:T(128)S(6)} %select_n.102), kind=kLoop, calls=%fused_computation.15 | loop fusion | bytes 229380 | tf_op jit(solution)/shard_map/dynamic_slice | solution.py:294
  0.9 4.9 %collective-permute-start = (f32[7,32,128]{2,1,0:T(8,128)S(1)}, f32[7,32,128]{2,1,0:T(8,128)S(1)}, u32[]{:S(2)}, u32[]{:S(2)}) collective-permute-start(f32[7,32,128]{2,1,0:T(8,128)S(1)} %constant_dynamic-slice_fusion.2), channel_id=1, source_target_pairs={{0,1},{1,0},{2,3},{3,2},{4,4},{5,6},{6,5},{7,7},{8,9},{9,8},{10,11... | collective-permute-start | bytes 344072 | tf_op jit(solution)/shard_map/ppermute | solution.py:293
  5.9 1.0 %copy-done = f32[1,32,32,128]{3,2,1,0:T(8,128)S(1)} copy-done((f32[1,32,32,128]{3,2,1,0:T(8,128)S(1)}, f32[1,32,32,128]{3,2,1,0:T(8,128)}, u32[]{:S(2)}) %copy-start) | copy-done | bytes 524312
  6.9 0.4 %shard_map.64 = (f32[368,128]{1,0:T(8,128)S(1)}, f32[368,128]{1,0:T(8,128)S(1)}, f32[368,128]{1,0:T(8,128)S(1)}, f32[368,128]{1,0:T(8,128)S(1)}) custom-call(f32[1024,128]{1,0:T(8,128)S(1)} %bitcast.8), custom_call_target="tpu_custom_call" | custom-call | tf_op jit(solution)/shard_map/pallas_call | solution.py:250
  7.3 2.7 %collective-permute-start.4 = (f32[368,128]{1,0:T(8,128)S(1)}, f32[368,128]{1,0:T(8,128)S(1)}, u32[]{:S(2)}, u32[]{:S(2)}) collective-permute-start(f32[368,128]{1,0:T(8,128)S(1)} %get-tuple-element.34), channel_id=1, source_target_pairs={{0,2},{1,3},{2,0},{3,1},{4,6},{5,7},{6,4},{7,5},{8,10},{9,11},{10,... | collective-permute-start | bytes 565256 | tf_op jit(solution)/shard_map/ppermute | solution.py:280
  10.7 0.5 %collective-permute-start.3 = (f32[368,128]{1,0:T(8,128)S(1)}, f32[368,128]{1,0:T(8,128)S(1)}, u32[]{:S(2)}, u32[]{:S(2)}) collective-permute-start(f32[368,128]{1,0:T(8,128)S(1)} %pad_select_fusion.1), channel_id=1, source_target_pairs={{0,1},{1,0},{2,3},{3,2},{4,5},{5,4},{6,7},{7,6},{8,9},{9,8},{10,11... | collective-permute-start | bytes 565256 | tf_op jit(solution)/shard_map/ppermute | solution.py:280
  11.3 1.4 %collective-permute-start.5 = (f32[368,128]{1,0:T(8,128)S(1)}, f32[368,128]{1,0:T(8,128)S(1)}, u32[]{:S(2)}, u32[]{:S(2)}) collective-permute-start(f32[368,128]{1,0:T(8,128)S(1)} %pad_select_fusion), channel_id=1, source_target_pairs={{0,3},{1,2},{2,1},{3,0},{4,7},{5,6},{6,5},{7,4},{8,11},{9,10},{10,... | collective-permute-start | bytes 565256 | tf_op jit(solution)/shard_map/ppermute | solution.py:280
  13.5 1.5 %collective-permute-start.1 = (f32[7,32,128]{2,1,0:T(8,128)S(1)}, f32[7,32,128]{2,1,0:T(8,128)S(1)}, u32[]{:S(2)}, u32[]{:S(2)}) collective-permute-start(f32[7,32,128]{2,1,0:T(8,128)S(1)} %collective-permute-done), channel_id=1, source_target_pairs={{0,8},{4,12},{8,0},{12,4},{16,24},{20,28},{24,16},{28,20},{1,9},{5... | collective-permute-start | bytes 344072 | tf_op jit(solution)/shard_map/ppermute | solution.py:298
  15.1 3.2 %collective-permute-done.1 = f32[7,32,128]{2,1,0:T(8,128)S(1)} collective-permute-done((f32[7,32,128]{2,1,0:T(8,128)S(1)}, f32[7,32,128]{2,1,0:T(8,128)S(1)}, u32[]{:S(2)}, u32[]{:S(2)}) %collective-permute-start.1) | collective-permute-done | bytes 114720 | tf_op jit(solution)/shard_map/ppermute | solution.py:298
  18.6 1.3 %collective-permute-done.2.other_ref = f32[14,32,128]{2,1,0:T(8,128)S(1)} collective-permute-done((f32[14,32,128]{2,1,0:T(8,128)S(1)}, f32[14,32,128]{2,1,0:T(8,128)S(1)}, u32[]{:S(2)}, u32[]{:S(2)}) %collective-permute-start.2) | collective-permute-done | bytes 229408 | tf_op jit(solution)/shard_map/ppermute | solution.py:302
  19.9 2.7 %shard_map.65 = (f32[48,32,128]{2,1,0:T(8,128)S(1)}, bf16[256,256]{1,0:T(8,128)(2,1)S(1)}, bf16[256,256]{1,0:T(8,128)(2,1)S(1)}, bf16[256,256]{1,0:T(8,128)(2,1)...) custom-call(s32[3]{0:T(128)S(1)} %pad_add_fusion.scalar_ref, ...), custom_call_target="tpu_custom_call" | custom-call | tf_op jit(solution)/shard_map/pallas_call | solution.py:306
  22.7 1.0 %collective-permute-done.5.refs_3_ = f32[368,128]{1,0:T(8,128)S(1)} collective-permute-done((f32[368,128]{1,0:T(8,128)S(1)}, f32[368,128]{1,0:T(8,128)S(1)}, u32[]{:S(2)}, u32[]{:S(2)}) %collective-permute-start.5) | collective-permute-done | bytes 188448 | tf_op jit(solution)/shard_map/ppermute | solution.py:280
  23.6 1.3 %shard_map.66 = (f32[8,32,128]{2,1,0:T(8,128)S(1)}, f32[8,32,128]{2,1,0:T(8,128)S(1)}, f32[46,32,128]{2,1,0:T(8,128)S(1)}) custom-call(s32[8,128]{1,0:T(8,128)S(1)} %get-tuple-element.26.flag_ref, f32[32,8,128]{2,1,0:T(8,128)S(1)} %get-tuple-element.27.weight_ref, f32[15,8,128]{2,1,0:T(8,128)S(1)} %get-tuple-element.28.splat_ref, f32[1024,128]{1,0:T(8,128)S(1)} %bitcast.10, ...), custom_call_target="tpu_custom_call" | custom-call | tf_op jit(solution)/shard_map/pallas_call | solution.py:326
  25.0 0.7 %shard_map.67 = (f32[8,32,128]{2,1,0:T(8,128)S(1)}, f32[8,32,128]{2,1,0:T(8,128)S(1)}) custom-call(f32[32,8,128]{2,1,0:T(8,128)S(1)} %get-tuple-element.27.weight_ref, f32[15,8,128]{2,1,0:T(8,128)S(1)} %get-tuple-element.28.splat_ref, f32[46,32,128]{2,1,0:T(8,128)S(1)} %get-tuple-element.40.ratio_ref, bf16[256,256]{1,0:T(8,128)(2,1)S(1)} %get-tuple-element.30.rows_high_ref, ...), custom_call_target="tpu_custom_call" | custom-call | flops 536870912 | bytes 2097152 | tf_op jit(solution)/shard_map/pallas_call | solution.py:339
  25.8 0.5 %collective-permute-start.10 = (f32[8,32,128]{2,1,0:T(8,128)S(1)}, f32[8,32,128]{2,1,0:T(8,128)S(1)}, u32[]{:S(2)}, u32[]{:S(2)}) collective-permute-start(f32[8,32,128]{2,1,0:T(8,128)S(1)} %get-tuple-element.42), channel_id=1, source_target_pairs={{0,4},{4,0},{8,12},{12,8},{16,20},{20,16},{24,28},{28,24},{1,5},{5... | collective-permute-start | bytes 393224 | tf_op jit(solution)/shard_map/ppermute | solution.py:347
  26.3 1.7 %collective-permute-start.7 = (f32[8,32,128]{2,1,0:T(8,128)S(1)}, f32[8,32,128]{2,1,0:T(8,128)S(1)}, u32[]{:S(2)}, u32[]{:S(2)}) collective-permute-start(f32[8,32,128]{2,1,0:T(8,128)S(1)} %add.56), channel_id=1, source_target_pairs={{0,16},{4,12},{8,24},{12,4},{16,0},{20,28},{24,8},{28,20},{1,17},{... | collective-permute-start | bytes 393224 | tf_op jit(solution)/shard_map/ppermute | solution.py:354
  28.0 0.9 %collective-permute-start.11 = (f32[8,32,128]{2,1,0:T(8,128)S(1)}, f32[8,32,128]{2,1,0:T(8,128)S(1)}, u32[]{:S(2)}, u32[]{:S(2)}) collective-permute-start(f32[8,32,128]{2,1,0:T(8,128)S(1)} %add.61), channel_id=1, source_target_pairs={{0,16},{4,12},{8,24},{12,4},{16,0},{20,28},{24,8},{28,20},{1,17},{... | collective-permute-start | bytes 393224 | tf_op jit(solution)/shard_map/ppermute | solution.py:354
  29.0 2.4 %collective-permute-done.7 = f32[8,32,128]{2,1,0:T(8,128)S(1)} collective-permute-done((f32[8,32,128]{2,1,0:T(8,128)S(1)}, f32[8,32,128]{2,1,0:T(8,128)S(1)}, u32[]{:S(2)}, u32[]{:S(2)}) %collective-permute-start.7) | collective-permute-done | bytes 131104 | tf_op jit(solution)/shard_map/ppermute | solution.py:354
  31.4 1.6 %collective-permute-start.8 = (f32[8,32,128]{2,1,0:T(8,128)S(1)}, f32[8,32,128]{2,1,0:T(8,128)S(1)}, u32[]{:S(2)}, u32[]{:S(2)}) collective-permute-start(f32[8,32,128]{2,1,0:T(8,128)S(1)} %add.57), channel_id=1, source_target_pairs={{0,8},{4,20},{8,0},{12,28},{16,24},{20,4},{24,16},{28,12},{1,9},{5... | collective-permute-start | bytes 393224 | tf_op jit(solution)/shard_map/ppermute | solution.py:354
  33.1 1.6 %collective-permute-start.12 = (f32[8,32,128]{2,1,0:T(8,128)S(1)}, f32[8,32,128]{2,1,0:T(8,128)S(1)}, u32[]{:S(2)}, u32[]{:S(2)}) collective-permute-start(f32[8,32,128]{2,1,0:T(8,128)S(1)} %add.62), channel_id=1, source_target_pairs={{0,8},{4,20},{8,0},{12,28},{16,24},{20,4},{24,16},{28,12},{1,9},{5... | collective-permute-start | bytes 393224 | tf_op jit(solution)/shard_map/ppermute | solution.py:354
  34.6 1.8 %collective-permute-done.8 = f32[8,32,128]{2,1,0:T(8,128)S(1)} collective-permute-done((f32[8,32,128]{2,1,0:T(8,128)S(1)}, f32[8,32,128]{2,1,0:T(8,128)S(1)}, u32[]{:S(2)}, u32[]{:S(2)}) %collective-permute-start.8) | collective-permute-done | bytes 131104 | tf_op jit(solution)/shard_map/ppermute | solution.py:354
  36.5 1.6 %collective-permute-done.12 = f32[8,32,128]{2,1,0:T(8,128)S(1)} collective-permute-done((f32[8,32,128]{2,1,0:T(8,128)S(1)}, f32[8,32,128]{2,1,0:T(8,128)S(1)}, u32[]{:S(2)}, u32[]{:S(2)}) %collective-permute-start.12) | collective-permute-done | bytes 131104 | tf_op jit(solution)/shard_map/ppermute | solution.py:354
  38.3 1.3 %collective-permute-done.13 = f32[8,32,128]{2,1,0:T(8,128)S(1)} collective-permute-done((f32[8,32,128]{2,1,0:T(8,128)S(1)}, f32[8,32,128]{2,1,0:T(8,128)S(1)}, u32[]{:S(2)}, u32[]{:S(2)}) %collective-permute-start.13) | collective-permute-done | bytes 131104 | tf_op jit(solution)/shard_map/ppermute | solution.py:360
  39.6 0.8 %pad_maximum_fusion = f32[32,32,128]{2,1,0:T(8,128)} fusion(f32[8,32,128]{2,1,0:T(8,128)S(1)} %get-tuple-element.48, f32[8,32,128]{2,1,0:T(8,128)S(1)} %get-tuple-element.47, f32[8,32,128]{2,1,0:T(8,128)S(1)} %get-tuple-element.46, f32[8,32,128]{2,1,0:T(8,128)S(1)} %get-tuple-element.45), kind=kLoop, calls=%fused_computation | loop fusion | flops 393216 | bytes 1048576 | tf_op jit(solution)/shard_map/concatenate | solution.py:362
  (38 shorter events, 1.1 us)
Async XLA Ops:
  0.9 12.5 %collective-permute-start = (f32[7,32,128]{2,1,0:T(8,128)S(1)}, f32[7,32,128]{2,1,0:T(8,128)S(1)}, u32[]{:S(2)}, u32[]{:S(2)}) collective-permute-start(f32[7,32,128]{2,1,0:T(8,128)S(1)} %constant_dynamic-slice_fusion.2), channel_id=1, source_target_pairs={{0,1},{1,0},{2,3},{3,2},{4,4},{5,6},{6,5},{7,7},{8,9},{9,8},{10,11... | collective-permute-start | bytes 344072 | tf_op jit(solution)/shard_map/ppermute | solution.py:293
  5.8 1.0 %copy-start = (f32[1,32,32,128]{3,2,1,0:T(8,128)S(1)}, f32[1,32,32,128]{3,2,1,0:T(8,128)}, u32[]{:S(2)}) copy-start(f32[1,32,32,128]{3,2,1,0:T(8,128)} %param.7) | copy-start | bytes 1572868
  6.9 3.8 %copy-start.1 = (f32[1,32,32,128]{3,2,1,0:T(8,128)S(1)}, f32[1,32,32,128]{3,2,1,0:T(8,128)}, u32[]{:S(2)}) copy-start(f32[1,32,32,128]{3,2,1,0:T(8,128)} %param.7) | copy-start | bytes 1572868
  7.3 16.3 %collective-permute-start.4 = (f32[368,128]{1,0:T(8,128)S(1)}, f32[368,128]{1,0:T(8,128)S(1)}, u32[]{:S(2)}, u32[]{:S(2)}) collective-permute-start(f32[368,128]{1,0:T(8,128)S(1)} %get-tuple-element.34), channel_id=1, source_target_pairs={{0,2},{1,3},{2,0},{3,1},{4,6},{5,7},{6,4},{7,5},{8,10},{9,11},{10,... | collective-permute-start | bytes 565256 | tf_op jit(solution)/shard_map/ppermute | solution.py:280
  10.7 11.9 %collective-permute-start.3 = (f32[368,128]{1,0:T(8,128)S(1)}, f32[368,128]{1,0:T(8,128)S(1)}, u32[]{:S(2)}, u32[]{:S(2)}) collective-permute-start(f32[368,128]{1,0:T(8,128)S(1)} %pad_select_fusion.1), channel_id=1, source_target_pairs={{0,1},{1,0},{2,3},{3,2},{4,5},{5,4},{6,7},{7,6},{8,9},{9,8},{10,11... | collective-permute-start | bytes 565256 | tf_op jit(solution)/shard_map/ppermute | solution.py:280
  11.2 2.1 %copy-start.4 = (f32[1,3,15]{2,0,1:T(1,128)S(1)}, f32[1,3,15]{2,0,1:T(1,128)}, u32[]{:S(2)}) copy-start(f32[1,3,15]{2,0,1:T(1,128)} %param.8) | copy-start | bytes 544
  11.3 8.7 %copy-start.2 = (f32[32,32,128]{2,1,0:T(8,128)S(1)}, f32[32,32,128]{2,1,0:T(8,128)}, u32[]{:S(2)}) copy-start(f32[32,32,128]{2,1,0:T(8,128)} %estimate_ref.1) | copy-start | bytes 1572868
  11.3 12.4 %collective-permute-start.5 = (f32[368,128]{1,0:T(8,128)S(1)}, f32[368,128]{1,0:T(8,128)S(1)}, u32[]{:S(2)}, u32[]{:S(2)}) collective-permute-start(f32[368,128]{1,0:T(8,128)S(1)} %pad_select_fusion), channel_id=1, source_target_pairs={{0,3},{1,2},{2,1},{3,0},{4,7},{5,6},{6,5},{7,4},{8,11},{9,10},{10,... | collective-permute-start | bytes 565256 | tf_op jit(solution)/shard_map/ppermute | solution.py:280
  13.5 4.8 %collective-permute-start.1 = (f32[7,32,128]{2,1,0:T(8,128)S(1)}, f32[7,32,128]{2,1,0:T(8,128)S(1)}, u32[]{:S(2)}, u32[]{:S(2)}) collective-permute-start(f32[7,32,128]{2,1,0:T(8,128)S(1)} %collective-permute-done), channel_id=1, source_target_pairs={{0,8},{4,12},{8,0},{12,4},{16,24},{20,28},{24,16},{28,20},{1,9},{5... | collective-permute-start | bytes 344072 | tf_op jit(solution)/shard_map/ppermute | solution.py:298
  18.3 1.6 %collective-permute-start.2 = (f32[14,32,128]{2,1,0:T(8,128)S(1)}, f32[14,32,128]{2,1,0:T(8,128)S(1)}, u32[]{:S(2)}, u32[]{:S(2)}) collective-permute-start(f32[14,32,128]{2,1,0:T(8,128)S(1)} %pad_maximum_fusion.1.near_ref), channel_id=1, source_target_pairs={{0,4},{4,0},{8,12},{12,8},{16,20},{20,16},{24,28},{28,24},{1,5},{5... | collective-permute-start | bytes 688136 | tf_op jit(solution)/shard_map/ppermute | solution.py:302
  18.6 1.3 %copy-start.3 = (s32[1,32]{1,0:T(1,128)S(1)}, s32[1,32]{1,0:T(1,128)}, u32[]{:S(2)}) copy-start(s32[1,32]{1,0:T(1,128)} %param.11) | copy-start | bytes 388
  24.9 1.4 %collective-permute-start.6 = (f32[8,32,128]{2,1,0:T(8,128)S(1)}, f32[8,32,128]{2,1,0:T(8,128)S(1)}, u32[]{:S(2)}, u32[]{:S(2)}) collective-permute-start(f32[8,32,128]{2,1,0:T(8,128)S(1)} %get-tuple-element.38), channel_id=1, source_target_pairs={{0,4},{4,0},{8,12},{12,8},{16,20},{20,16},{24,28},{28,24},{1,5},{5... | collective-permute-start | bytes 393224 | tf_op jit(solution)/shard_map/ppermute | solution.py:336
  25.8 2.2 %collective-permute-start.10 = (f32[8,32,128]{2,1,0:T(8,128)S(1)}, f32[8,32,128]{2,1,0:T(8,128)S(1)}, u32[]{:S(2)}, u32[]{:S(2)}) collective-permute-start(f32[8,32,128]{2,1,0:T(8,128)S(1)} %get-tuple-element.42), channel_id=1, source_target_pairs={{0,4},{4,0},{8,12},{12,8},{16,20},{20,16},{24,28},{28,24},{1,5},{5... | collective-permute-start | bytes 393224 | tf_op jit(solution)/shard_map/ppermute | solution.py:347
  26.3 5.0 %collective-permute-start.7 = (f32[8,32,128]{2,1,0:T(8,128)S(1)}, f32[8,32,128]{2,1,0:T(8,128)S(1)}, u32[]{:S(2)}, u32[]{:S(2)}) collective-permute-start(f32[8,32,128]{2,1,0:T(8,128)S(1)} %add.56), channel_id=1, source_target_pairs={{0,16},{4,12},{8,24},{12,4},{16,0},{20,28},{24,8},{28,20},{1,17},{... | collective-permute-start | bytes 393224 | tf_op jit(solution)/shard_map/ppermute | solution.py:354
  28.0 5.0 %collective-permute-start.11 = (f32[8,32,128]{2,1,0:T(8,128)S(1)}, f32[8,32,128]{2,1,0:T(8,128)S(1)}, u32[]{:S(2)}, u32[]{:S(2)}) collective-permute-start(f32[8,32,128]{2,1,0:T(8,128)S(1)} %add.61), channel_id=1, source_target_pairs={{0,16},{4,12},{8,24},{12,4},{16,0},{20,28},{24,8},{28,20},{1,17},{... | collective-permute-start | bytes 393224 | tf_op jit(solution)/shard_map/ppermute | solution.py:354
  31.4 5.0 %collective-permute-start.8 = (f32[8,32,128]{2,1,0:T(8,128)S(1)}, f32[8,32,128]{2,1,0:T(8,128)S(1)}, u32[]{:S(2)}, u32[]{:S(2)}) collective-permute-start(f32[8,32,128]{2,1,0:T(8,128)S(1)} %add.57), channel_id=1, source_target_pairs={{0,8},{4,20},{8,0},{12,28},{16,24},{20,4},{24,16},{28,12},{1,9},{5... | collective-permute-start | bytes 393224 | tf_op jit(solution)/shard_map/ppermute | solution.py:354
  33.1 5.0 %collective-permute-start.12 = (f32[8,32,128]{2,1,0:T(8,128)S(1)}, f32[8,32,128]{2,1,0:T(8,128)S(1)}, u32[]{:S(2)}, u32[]{:S(2)}) collective-permute-start(f32[8,32,128]{2,1,0:T(8,128)S(1)} %add.62), channel_id=1, source_target_pairs={{0,8},{4,20},{8,0},{12,28},{16,24},{20,4},{24,16},{28,12},{1,9},{5... | collective-permute-start | bytes 393224 | tf_op jit(solution)/shard_map/ppermute | solution.py:354
  36.5 1.8 %collective-permute-start.9 = (f32[8,32,128]{2,1,0:T(8,128)S(1)}, f32[8,32,128]{2,1,0:T(8,128)S(1)}, u32[]{:S(2)}, u32[]{:S(2)}) collective-permute-start(f32[8,32,128]{2,1,0:T(8,128)S(1)} %exponential_multiply_fusion.1), channel_id=1, source_target_pairs={{0,4},{4,0},{8,12},{12,8},{16,20},{20,16},{24,28},{28,24},{1,5},{5... | collective-permute-start | bytes 393224 | tf_op jit(solution)/shard_map/ppermute | solution.py:360
  38.2 1.4 %collective-permute-start.13 = (f32[8,32,128]{2,1,0:T(8,128)S(1)}, f32[8,32,128]{2,1,0:T(8,128)S(1)}, u32[]{:S(2)}, u32[]{:S(2)}) collective-permute-start(f32[8,32,128]{2,1,0:T(8,128)S(1)} %exponential_multiply_fusion), channel_id=1, source_target_pairs={{0,4},{4,0},{8,12},{12,8},{16,20},{20,16},{24,28},{28,24},{1,5},{5... | collective-permute-start | bytes 393224 | tf_op jit(solution)/shard_map/ppermute | solution.py:360
